TPU v7x, 32 devices: a whole 2x2x4 slice. The times are simulated.
32 devices in a mesh: seq: 8 (over z, x), mp: 4 (over y, core).
Axes of the slice: x: 2, y: 2, z: 4, core: 2. Of those that a mesh axis runs over, the one named last changes fastest.
Arguments:
- byte_input: bfloat16 [4096, 1024], P('seq'), may hold values from -6 to 6
- seq_lengths: int32 [6], replicated, may hold values from 1 to 450, as said below
- cotangent: float32 [4096, 1024], P('seq'), may hold values from -6 to 6
- gain_global: float32 [1024], replicated, may hold values from 0.1 to 1.9
- patch_in: bfloat16 [8192, 1024], P(('mp', 'seq')), may hold values from -0.0625 to 0.0625
- mixer_gate: bfloat16 [1024, 2048], P('seq', 'mp'), may hold values from -0.1875 to 0.1875
- mixer_input: bfloat16 [1024, 2048], P('seq', 'mp'), may hold values from -0.1875 to 0.1875
- mixer_state: bfloat16 [1024, 256], P('seq'), may hold values from -0.1875 to 0.1875
- mixer_step: bfloat16 [1024, 32], P('seq', 'mp'), may hold values from -0.1875 to 0.1875
- conv_input: float32 [4, 2048], P(None, 'mp'), may hold values from -3 to 3
- conv_state: float32 [4, 256], replicated, may hold values from -3 to 3
- step_bias: float32 [32], P('mp'), may hold values from -5 to -1
- decay_log: float32 [32], P('mp'), may hold values from -4.6 to 0.7
- skip_gain: float32 [32], P('mp'), may hold values from 0.5 to 1.5
- gain_mixer: float32 [2048], P('mp'), may hold values from 0.1 to 1.9
- mixer_out: bfloat16 [2048, 1024], P(('mp', 'seq')), may hold values from -0.125 to 0.125
- patch_out: bfloat16 [1024, 8192], P('seq', 'mp'), may hold values from -0.1875 to 0.1875
- gain_attend: float32 [1024], replicated, may hold values from 0.1 to 1.9
- attend_query: bfloat16 [1024, 1024], P('seq', 'mp'), may hold values from -0.1875 to 0.1875
- attend_key: bfloat16 [1024, 1024], P('seq', 'mp'), may hold values from -0.1875 to 0.1875
- attend_value: bfloat16 [1024, 1024], P('seq', 'mp'), may hold values from -0.1875 to 0.1875
- attend_out: bfloat16 [1024, 1024], P(('mp', 'seq')), may hold values from -0.375 to 0.375
- gain_feed: float32 [1024], replicated, may hold values from 0.1 to 1.9
- feed_gate: bfloat16 [1024, 4096], P('seq', 'mp'), may hold values from -0.1875 to 0.1875
- feed_up: bfloat16 [1024, 4096], P('seq', 'mp'), may hold values from -0.1875 to 0.1875
- feed_down: bfloat16 [4096, 1024], P(('mp', 'seq')), may hold values from -0.09375 to 0.09375
Outputs:
- byte_output: bfloat16 [4096, 1024], P('seq')
- grad_input: bfloat16 [4096, 1024], P('seq')
- grad_gain_global: float32 [1024], replicated
- grad_patch_in: float32 [8192, 1024], P(('mp', 'seq'))
- grad_mixer_gate: float32 [1024, 2048], P('seq', 'mp')
- grad_mixer_input: float32 [1024, 2048], P('seq', 'mp')
- grad_mixer_state: float32 [1024, 256], P('seq')
- grad_mixer_step: float32 [1024, 32], P('seq', 'mp')
- grad_conv_input: float32 [4, 2048], P(None, 'mp')
- grad_conv_state: float32 [4, 256], replicated
- grad_step_bias: float32 [32], P('mp')
- grad_decay_log: float32 [32], P('mp')
- grad_skip_gain: float32 [32], P('mp')
- grad_gain_mixer: float32 [2048], P('mp')
- grad_mixer_out: float32 [2048, 1024], P(('mp', 'seq'))
- grad_patch_out: float32 [1024, 8192], P('seq', 'mp')
- grad_gain_attend: float32 [1024], replicated
- grad_attend_query: float32 [1024, 1024], P('seq', 'mp')
- grad_attend_key: float32 [1024, 1024], P('seq', 'mp')
- grad_attend_value: float32 [1024, 1024], P('seq', 'mp')
- grad_attend_out: float32 [1024, 1024], P(('mp', 'seq'))
- grad_gain_feed: float32 [1024], replicated
- grad_feed_gate: float32 [1024, 4096], P('seq', 'mp')
- grad_feed_up: float32 [1024, 4096], P('seq', 'mp')
- grad_feed_down: float32 [4096, 1024], P(('mp', 'seq'))
Inputs may be any that keep to these rules, and one draw needn't show every extreme that they name: `seq_lengths`: lengths in patches of 6 sequences laid end to end over all 512 patches: one is 450 long, the other 5 have 62 together, and one to three of them come before the long one.
All inputs are finite; a program needn't handle non-finite values.
Results may differ from a plain program's by a relative error of at most 0.03.
Values may be sent and summed in bfloat16 or wider, within the bound.
No kernel may reach another device: no remote copies, remote signals or barrier semaphores. Data moves between devices by JAX's collectives and lax.ppermute only.
A program may use at most 192 MiB of HBM per device.

v0:
```python
import jax
import jax.numpy as jnp
from jax import lax
from jax.sharding import PartitionSpec as P

E = 1024
HDIM = 64
DI = 2048
NSTATE = 128
KCONV = 4
PATCH = 8
TOK_DEV = 512
BLOCK = 64


EPS = 1e-05
HIGH = lax.Precision.HIGHEST


def shifted(shard, axis, by):
    length = lax.axis_size(axis)
    pairs = [(i, i + by) for i in range(length) if 0 <= i + by < length]
    return lax.ppermute(shard, axis, pairs)


def prefix(shard, axis, combine, identity):
    length, position = (lax.axis_size(axis), lax.axis_index(axis))
    everything = jax.tree.map(
        lambda part, kind: lax.all_gather(part.astype(kind), axis),
        shard,
        (jnp.bfloat16, jnp.bfloat16),
    )
    start = jax.tree.map(
        lambda part, zero: jnp.broadcast_to(jnp.asarray(zero, part.dtype), part.shape),
        shard,
        identity,
    )

    def prefix_turn(k, before):
        reached = k < position
        new = combine(
            before, jax.tree.map(lambda part, own: part[k].astype(own.dtype), everything, shard)
        )
        return jax.tree.map(lambda a, b: jnp.where(reached, a, b), new, before)

    return lax.fori_loop(0, length, prefix_turn, start)


def carried_in(shard, axis, combine, identity):
    length, position = (lax.axis_size(axis), lax.axis_index(axis))
    everything = jax.tree.map(
        lambda part, kind: lax.all_gather(part.astype(kind), axis),
        shard,
        jax.tree.map(lambda a: jnp.bfloat16 if a.dtype == jnp.float32 else a.dtype, shard),
    )
    start = jax.tree.map(
        lambda part, zero: jnp.broadcast_to(jnp.asarray(zero, part.dtype), part.shape),
        shard,
        identity,
    )

    def carried_turn(k, before):
        at = length - 1 - k
        reached = at > position
        new = combine(
            before, jax.tree.map(lambda part, own: part[at].astype(own.dtype), everything, shard)
        )
        return jax.tree.map(lambda a, b: jnp.where(reached, a, b), new, before)

    return lax.fori_loop(0, length, carried_turn, start)


def product(former, latter):
    return jnp.dot(former, latter, preferred_element_type=jnp.float32)


def product_left(former, latter):
    return lax.dot_general(
        former, latter, (((0,), (0,)), ((), ())), preferred_element_type=jnp.float32
    )


def product_right(former, latter):
    return lax.dot_general(
        former, latter, (((1,), (1,)), ((), ())), preferred_element_type=jnp.float32
    )


def over_heads(partial_sum):
    return lax.psum(partial_sum, "mp")


def gather_slots(pieces):
    return lax.all_gather(pieces.astype(jnp.bfloat16), "mp", axis=1, tiled=True).astype(
        pieces.dtype
    )


def rms_scale(values, scale_gain):
    mean_square = jnp.mean(values * values, axis=-1, keepdims=True)
    return values * lax.rsqrt(mean_square + EPS) * scale_gain


def rms_back(values, scale_gain, upstream):
    pullback = jax.vjp(rms_scale, values, scale_gain)[1]
    return pullback(upstream)


def segment_of(lengths, start_row, row_count):
    bounds = jnp.cumsum(lengths)[:-1]
    places = start_row + jnp.arange(row_count, dtype=jnp.int32)
    return jnp.sum((places[:, None] >= bounds[None, :]).astype(jnp.int32), axis=1)


def conv_silu(extended, kernel, segment_rows):
    row_count = extended.shape[0] - KCONV + 1
    segment_now = segment_rows[KCONV - 1 :]
    summed = jnp.zeros((row_count, extended.shape[1]), jnp.float32)
    for offset in range(KCONV):
        same_seq = (segment_rows[offset : offset + row_count] == segment_now)[:, None]
        summed = (
            summed
            + jnp.where(same_seq, extended[offset : offset + row_count], 0.0) * kernel[offset]
        )
    return jax.nn.silu(summed)


def block_output(
    head_values,
    write_vecs,
    read_vecs,
    step_size,
    log_rate,
    skip_term,
    state_value,
    segment_rows,
    segment_prev,
):
    length = head_values.shape[0]
    running = jnp.cumsum(-step_size * jnp.exp(log_rate), axis=0)
    places = jnp.arange(length)
    allowed = (places[:, None] >= places[None, :]) & (
        segment_rows[:, None] == segment_rows[None, :]
    )
    allowed = allowed[:, :, None]
    spread = jnp.where(allowed, running[:, None, :] - running[None, :, :], 0.0)
    factors = jnp.where(allowed, jnp.exp(spread), 0.0)
    affinity = jnp.dot(read_vecs, write_vecs.T, precision=HIGH, preferred_element_type=jnp.float32)
    mixing = factors * affinity[:, :, None] * step_size[None, :, :]
    inside = jnp.einsum("tsh,shp->thp", mixing, head_values, precision=HIGH)
    carried = jnp.where((segment_rows == segment_prev)[:, None], jnp.exp(running), 0.0)
    reading = (
        jnp.einsum("tn,hpn->thp", read_vecs, state_value, precision=HIGH) * carried[:, :, None]
    )
    result = inside + reading + skip_term[None, :, None] * head_values
    return result.reshape(length, -1)


def block_summary(head_values, write_vecs, step_size, log_rate, segment_rows, segment_prev):
    running = jnp.cumsum(-step_size * jnp.exp(log_rate), axis=0)
    latest = running[-1]
    in_tail = (segment_rows == segment_rows[-1])[:, None]
    weights = jnp.where(in_tail, jnp.exp(latest[None, :] - running), 0.0) * step_size
    scaled = weights[:, :, None] * head_values
    state_local = jnp.einsum("shp,sn->hpn", scaled, write_vecs, precision=HIGH)
    decay_total = jnp.where(segment_rows[-1] == segment_prev, jnp.exp(latest), 0.0)
    return (decay_total, state_local)


def combine_state(earlier, later):
    return (earlier[0] * later[0], later[0][:, None, None] * earlier[1] + later[1])


def patch_attention(queries, keys_all, values_all):
    row_count = queries.shape[0]
    head_count = queries.shape[1] // HDIM
    query_rows = queries.reshape(row_count // PATCH, PATCH, head_count, HDIM)
    key_rows = keys_all.reshape(row_count // PATCH, PATCH, head_count, HDIM)
    value_rows = values_all.reshape(row_count // PATCH, PATCH, head_count, HDIM)
    scores = jnp.einsum("bihd,bjhd->bhij", query_rows, key_rows, precision=HIGH) * HDIM ** (-0.5)
    causal = jnp.arange(PATCH)[:, None] >= jnp.arange(PATCH)[None, :]
    scores = jnp.where(causal, scores, -1e30)
    peak = jnp.max(scores, axis=-1, keepdims=True)
    probs = jnp.exp(scores - peak)
    probs = probs / jnp.sum(probs, axis=-1, keepdims=True)
    context = jnp.einsum("bhij,bjhd->bihd", probs, value_rows, precision=HIGH)
    return context.reshape(row_count, head_count * HDIM)


def add_tail(main_rows, tail_rows):
    keep_count = main_rows.shape[0] - tail_rows.shape[0]
    return jnp.concatenate([main_rows[:keep_count], main_rows[keep_count:] + tail_rows], axis=0)


def shards(
    byte_input,
    seq_lengths,
    cotangent,
    gain_global,
    patch_in,
    mixer_gate,
    mixer_input,
    mixer_state,
    mixer_step,
    conv_input,
    conv_state,
    step_bias,
    decay_log,
    skip_gain,
    gain_mixer,
    mixer_out,
    patch_out,
    gain_attend,
    attend_query,
    attend_key,
    attend_value,
    attend_out,
    gain_feed,
    feed_gate,
    feed_up,
    feed_down,
):
    group_size = lax.axis_size("mp")
    slot_width = PATCH * E // group_size
    slot_start = lax.axis_index("mp") * slot_width
    first_row = lax.axis_index("seq") * BLOCK
    segment_ext = segment_of(seq_lengths, first_row - (KCONV - 1), BLOCK + KCONV - 1)
    segment_rows = segment_ext[KCONV - 1 :]
    segment_prev = segment_of(seq_lengths, first_row - 1, 1)[0]

    def fetch_global():
        return (
            lax.all_gather(patch_in, "seq", axis=0, tiled=True),
            lax.all_gather(mixer_gate, "seq", axis=0, tiled=True),
            lax.all_gather(mixer_input, "seq", axis=0, tiled=True),
            lax.all_gather(mixer_state, "seq", axis=0, tiled=True),
            lax.all_gather(mixer_step, "seq", axis=0, tiled=True),
            lax.all_gather(mixer_out, "seq", axis=0, tiled=True),
            lax.all_gather(patch_out, "seq", axis=0, tiled=True),
        )

    def fetch_local():
        return (
            lax.all_gather(attend_query, "seq", axis=0, tiled=True),
            lax.all_gather(attend_key, "seq", axis=0, tiled=True),
            lax.all_gather(attend_value, "seq", axis=0, tiled=True),
            lax.all_gather(attend_out, "seq", axis=0, tiled=True),
            lax.all_gather(feed_gate, "seq", axis=0, tiled=True),
            lax.all_gather(feed_up, "seq", axis=0, tiled=True),
            lax.all_gather(feed_down, "seq", axis=0, tiled=True),
        )

    def conv_of(extended, kernel):
        return conv_silu(extended, kernel, segment_ext)

    def summary_of(values_in, writes_in, steps_in, rates_in):
        return block_summary(values_in, writes_in, steps_in, rates_in, segment_rows, segment_prev)

    def output_of(values_in, writes_in, reads_in, steps_in, rates_in, skips_in, state_value):
        return block_output(
            values_in,
            writes_in,
            reads_in,
            steps_in,
            rates_in,
            skips_in,
            state_value,
            segment_rows,
            segment_prev,
        )

    full_patch_in, full_gate, full_input, full_state, full_step, full_mixout, full_patchout = (
        fetch_global()
    )
    patches = byte_input.reshape(BLOCK, PATCH * E)
    local_bytes = lax.dynamic_slice_in_dim(patches, slot_start, slot_width, 1)
    hidden = over_heads(product(local_bytes, full_patch_in))
    normed = rms_scale(hidden, gain_global).astype(jnp.bfloat16)
    gate_pre = product(normed, full_gate)
    input_pre = product(normed, full_input)
    state_pre = product(normed, full_state)
    step_pre = product(normed, full_step)
    rim_rows = shifted((input_pre[BLOCK - KCONV + 1 :], state_pre[BLOCK - KCONV + 1 :]), "seq", 1)
    input_ext = jnp.concatenate([rim_rows[0], input_pre], axis=0)
    state_ext = jnp.concatenate([rim_rows[1], state_pre], axis=0)
    input_conv = conv_of(input_ext, conv_input)
    state_conv = conv_of(state_ext, conv_state)
    step_size = jax.nn.softplus(step_pre + step_bias)
    head_count = step_size.shape[1]
    head_values = input_conv.reshape(BLOCK, head_count, HDIM)
    write_vecs = state_conv[:, :NSTATE]
    read_vecs = state_conv[:, NSTATE:]
    decay_total, state_local = summary_of(head_values, write_vecs, step_size, decay_log)
    identity = (jnp.ones_like(decay_total), jnp.zeros_like(state_local))
    state_in = prefix((decay_total, state_local), "seq", combine_state, identity)[1]
    mixer_rows = output_of(
        head_values, write_vecs, read_vecs, step_size, decay_log, skip_gain, state_in
    )
    gate_sigm = jax.nn.sigmoid(gate_pre)
    gate_silu = gate_pre * gate_sigm
    gated = mixer_rows * gate_silu
    mean_square = over_heads(jnp.sum(gated * gated, axis=-1, keepdims=True)) / DI
    root_inverse = lax.rsqrt(mean_square + EPS)
    mixed = (gated * root_inverse * gain_mixer).astype(jnp.bfloat16)
    merged = hidden + over_heads(product(mixed, full_mixout))
    merged_low = merged.astype(jnp.bfloat16)
    slot_values = gather_slots(product(merged_low, full_patchout)).reshape(TOK_DEV, E)
    residual = byte_input.astype(jnp.float32) + slot_values
    full_query, full_key, full_value, full_attout, full_feedgate, full_up, full_down = fetch_local()
    attend_in = rms_scale(residual, gain_attend).astype(jnp.bfloat16)
    queries = product(attend_in, full_query)
    keys_all = product(attend_in, full_key)
    values_all = product(attend_in, full_value)
    context = patch_attention(queries, keys_all, values_all).astype(jnp.bfloat16)
    middle = residual + over_heads(product(context, full_attout))
    feed_in = rms_scale(middle, gain_feed).astype(jnp.bfloat16)
    gate_value = product(feed_in, full_feedgate)
    up_value = product(feed_in, full_up)
    gate_sig = jax.nn.sigmoid(gate_value)
    hidden_units = (gate_value * gate_sig * up_value).astype(jnp.bfloat16)
    byte_output = middle + over_heads(product(hidden_units, full_down))
    full_query, full_key, full_value, full_attout, full_feedgate, full_up, full_down = fetch_local()
    out_low = cotangent.astype(jnp.bfloat16)
    grad_feed_down = product_left(hidden_units, out_low)
    grad_units = product_right(out_low, full_down)
    grad_gate_value = (
        grad_units * up_value * gate_sig * (1.0 + gate_value * (1.0 - gate_sig))
    ).astype(jnp.bfloat16)
    grad_up_value = (grad_units * gate_value * gate_sig).astype(jnp.bfloat16)
    grad_feed_gate = product_left(feed_in, grad_gate_value)
    grad_feed_up = product_left(feed_in, grad_up_value)
    grad_feed_in = over_heads(
        product_right(grad_gate_value, full_feedgate) + product_right(grad_up_value, full_up)
    )
    grad_middle_part, grad_gain_feed = rms_back(middle, gain_feed, grad_feed_in)
    grad_middle = cotangent + grad_middle_part
    middle_low = grad_middle.astype(jnp.bfloat16)
    grad_attend_out = product_left(context, middle_low)
    grad_context = product_right(middle_low, full_attout)
    attention_pull = jax.vjp(patch_attention, queries, keys_all, values_all)[1]
    grad_query_raw, grad_key_raw, grad_value_raw = attention_pull(grad_context)
    grad_query_rows = grad_query_raw.astype(jnp.bfloat16)
    grad_key_rows = grad_key_raw.astype(jnp.bfloat16)
    grad_value_rows = grad_value_raw.astype(jnp.bfloat16)
    grad_attend_query = product_left(attend_in, grad_query_rows)
    grad_attend_key = product_left(attend_in, grad_key_rows)
    grad_attend_value = product_left(attend_in, grad_value_rows)
    grad_attend_in = over_heads(
        product_right(grad_query_rows, full_query)
        + product_right(grad_key_rows, full_key)
        + product_right(grad_value_rows, full_value)
    )
    grad_residual_part, grad_gain_attend = rms_back(residual, gain_attend, grad_attend_in)
    grad_residual = grad_middle + grad_residual_part
    local_sums = (
        lax.psum_scatter(grad_attend_query, "seq", scatter_dimension=0, tiled=True),
        lax.psum_scatter(grad_attend_key, "seq", scatter_dimension=0, tiled=True),
        lax.psum_scatter(grad_attend_value, "seq", scatter_dimension=0, tiled=True),
        lax.psum_scatter(grad_attend_out, "seq", scatter_dimension=0, tiled=True),
        lax.psum_scatter(grad_feed_gate, "seq", scatter_dimension=0, tiled=True),
        lax.psum_scatter(grad_feed_up, "seq", scatter_dimension=0, tiled=True),
        lax.psum_scatter(grad_feed_down, "seq", scatter_dimension=0, tiled=True),
    )
    full_patch_in, full_gate, full_input, full_state, full_step, full_mixout, full_patchout = (
        fetch_global()
    )
    residual_patches = grad_residual.reshape(BLOCK, PATCH * E)
    slot_grad = lax.dynamic_slice_in_dim(residual_patches, slot_start, slot_width, 1).astype(
        jnp.bfloat16
    )
    grad_patch_out = product_left(merged_low, slot_grad)
    grad_merged = over_heads(product_right(slot_grad, full_patchout))
    merged_grad_low = grad_merged.astype(jnp.bfloat16)
    grad_mixer_out = product_left(mixed, merged_grad_low)
    grad_mixed = product_right(merged_grad_low, full_mixout)
    grad_gain_mixer = jnp.sum(grad_mixed * gated * root_inverse, axis=0)
    scaled_grad = grad_mixed * gain_mixer
    inner_dot = over_heads(jnp.sum(scaled_grad * gated, axis=-1, keepdims=True))
    grad_gated = scaled_grad * root_inverse - gated * inner_dot * root_inverse**3 / DI
    grad_mixer_rows = grad_gated * gate_silu
    grad_gate_pre = grad_gated * mixer_rows * gate_sigm * (1.0 + gate_pre * (1.0 - gate_sigm))
    output_pull = jax.vjp(
        output_of, head_values, write_vecs, read_vecs, step_size, decay_log, skip_gain, state_in
    )[1]
    (
        grad_values_a,
        grad_writes_a,
        grad_reads,
        grad_steps_a,
        grad_rates_a,
        grad_skip_gain,
        grad_state_in,
    ) = output_pull(grad_mixer_rows)
    state_end = carried_in((decay_total, grad_state_in), "seq", combine_state, identity)[1]
    summary_pull = jax.vjp(summary_of, head_values, write_vecs, step_size, decay_log)[1]
    grad_values_b, grad_writes_b, grad_steps_b, grad_rates_b = summary_pull(
        (jnp.sum(state_end * state_in, axis=(1, 2)), state_end)
    )
    grad_input_conv = (grad_values_a + grad_values_b).reshape(BLOCK, -1)
    grad_state_conv = over_heads(
        jnp.concatenate([grad_writes_a + grad_writes_b, grad_reads], axis=1)
    )
    grad_step_pre = (grad_steps_a + grad_steps_b) * jax.nn.sigmoid(step_pre + step_bias)
    grad_step_bias = jnp.sum(grad_step_pre, axis=0)
    grad_decay_log = grad_rates_a + grad_rates_b
    grad_input_ext, grad_conv_input = jax.vjp(conv_of, input_ext, conv_input)[1](grad_input_conv)
    grad_state_ext, grad_conv_state = jax.vjp(conv_of, state_ext, conv_state)[1](grad_state_conv)
    rim_back = shifted((grad_input_ext[: KCONV - 1], grad_state_ext[: KCONV - 1]), "seq", -1)
    grad_input_low = add_tail(grad_input_ext[KCONV - 1 :], rim_back[0]).astype(jnp.bfloat16)
    grad_state_low = add_tail(grad_state_ext[KCONV - 1 :], rim_back[1]).astype(jnp.bfloat16)
    grad_gate_low = grad_gate_pre.astype(jnp.bfloat16)
    grad_step_low = grad_step_pre.astype(jnp.bfloat16)
    grad_mixer_gate = product_left(normed, grad_gate_low)
    grad_mixer_input = product_left(normed, grad_input_low)
    grad_mixer_state = product_left(normed, grad_state_low)
    grad_mixer_step = product_left(normed, grad_step_low)
    head_part = over_heads(
        product_right(grad_gate_low, full_gate)
        + product_right(grad_input_low, full_input)
        + product_right(grad_step_low, full_step)
    )
    grad_normed = head_part + product_right(grad_state_low, full_state)
    grad_hidden_part, grad_gain_global = rms_back(hidden, gain_global, grad_normed)
    hidden_grad_low = (grad_merged + grad_hidden_part).astype(jnp.bfloat16)
    grad_patch_in = product_left(local_bytes, hidden_grad_low)
    grad_byte_part = gather_slots(product_right(hidden_grad_low, full_patch_in)).reshape(TOK_DEV, E)
    grad_input = (grad_residual + grad_byte_part).astype(jnp.bfloat16)
    global_sums = (
        lax.psum_scatter(grad_patch_in, "seq", scatter_dimension=0, tiled=True),
        lax.psum_scatter(grad_mixer_gate, "seq", scatter_dimension=0, tiled=True),
        lax.psum_scatter(grad_mixer_input, "seq", scatter_dimension=0, tiled=True),
        lax.psum_scatter(grad_mixer_state, "seq", scatter_dimension=0, tiled=True),
        lax.psum_scatter(grad_mixer_step, "seq", scatter_dimension=0, tiled=True),
        lax.psum_scatter(grad_mixer_out, "seq", scatter_dimension=0, tiled=True),
        lax.psum_scatter(grad_patch_out, "seq", scatter_dimension=0, tiled=True),
    )
    small_sums = lax.psum(
        (
            grad_gain_global,
            grad_conv_input,
            grad_conv_state,
            grad_step_bias,
            grad_decay_log,
            grad_skip_gain,
            grad_gain_mixer,
            grad_gain_attend,
            grad_gain_feed,
        ),
        "seq",
    )
    return (
        byte_output.astype(jnp.bfloat16),
        grad_input,
        small_sums[0],
        global_sums[0],
        global_sums[1],
        global_sums[2],
        global_sums[3],
        global_sums[4],
        small_sums[1],
        small_sums[2],
        small_sums[3],
        small_sums[4],
        small_sums[5],
        small_sums[6],
        global_sums[5],
        global_sums[6],
        small_sums[7],
        local_sums[0],
        local_sums[1],
        local_sums[2],
        local_sums[3],
        small_sums[8],
        local_sums[4],
        local_sums[5],
        local_sums[6],
    )


def solution(mesh):
    in_specs = (
        P("seq", None),
        P(),
        P("seq", None),
        P(),
        P(("mp", "seq"), None),
        P("seq", "mp"),
        P("seq", "mp"),
        P("seq", None),
        P("seq", "mp"),
        P(None, "mp"),
        P(),
        P("mp"),
        P("mp"),
        P("mp"),
        P("mp"),
        P(("mp", "seq"), None),
        P("seq", "mp"),
        P(),
        P("seq", "mp"),
        P("seq", "mp"),
        P("seq", "mp"),
        P(("mp", "seq"), None),
        P(),
        P("seq", "mp"),
        P("seq", "mp"),
        P(("mp", "seq"), None),
    )
    out_specs = (
        P("seq", None),
        P("seq", None),
        P(),
        P(("mp", "seq"), None),
        P("seq", "mp"),
        P("seq", "mp"),
        P("seq", None),
        P("seq", "mp"),
        P(None, "mp"),
        P(),
        P("mp"),
        P("mp"),
        P("mp"),
        P("mp"),
        P(("mp", "seq"), None),
        P("seq", "mp"),
        P(),
        P("seq", "mp"),
        P("seq", "mp"),
        P("seq", "mp"),
        P(("mp", "seq"), None),
        P(),
        P("seq", "mp"),
        P("seq", "mp"),
        P(("mp", "seq"), None),
    )
    return jax.shard_map(shards, mesh=mesh, in_specs=in_specs, out_specs=out_specs, check_vma=False)
```

profile of v0, /device:TPU:0, one launch (start us, length us, event | category | flops | bytes accessed | tf_op | source)
XLA Modules:
  0.0 2337.2 jit_solution(11828510207178903809)
XLA Ops:
  9.7 76.6 %all-gather.16.cloned.1.call-done = bf16[2048,1024]{1,0:T(8,128)(2,1)} async-done(((bf16[256,1024]{1,0:T(8,128)(2,1)}), bf16[2048,1024]{1,0:T(8,128)(2,1)}) %all-gather.16.cloned.1.call-update) | async-done | bytes 4194320 | tf_op jit(solution)/shard_map/all_gather | solution.py:233
  86.3 3.7 fusion.58
  90.8 26.0 %all_gather.82 = bf16[1024,8]{0,1:T(8,128)(2,1)S(1)} all-gather(bf16[128,8]{0,1:T(8,128)(2,1)S(1)} %copy-done.156), channel_id=1, replica_groups=mesh['seq'=8,'mp'=4] {'seq'}, dimensions={0}, use_global_device_ids=true | all-gather | bytes 18432 | tf_op jit(solution)/shard_map/all_gather | solution.py:237
  119.9 31.9 %all_gather.83 = bf16[1024,256]{1,0:T(8,128)(2,1)S(1)} all-gather(bf16[128,256]{1,0:T(8,128)(2,1)S(1)} %copy-done.82), channel_id=1, replica_groups=mesh['seq'=8,'mp'=4] {'seq'}, dimensions={0}, use_global_device_ids=true | all-gather | bytes 589824 | tf_op jit(solution)/shard_map/all_gather | solution.py:236
  156.7 6.8 all-gather.18.cloned.1.call-done
  173.9 20.0 all-gather.2
  194.1 18.7 all-gather.36.cloned.1.call-done
  212.8 8.4 while.30
  222.5 31.4 %all-gather.20.cloned.1.call-done = bf16[1024,512]{1,0:T(8,128)(2,1)} async-done(((bf16[128,512]{1,0:T(8,128)(2,1)}), bf16[1024,512]{1,0:T(8,128)(2,1)}) %all-gather.20.cloned.1.call-update) | async-done | bytes 1048592 | tf_op jit(solution)/shard_map/all_gather | solution.py:234
  256.3 5.7 psum.141
  262.5 32.6 %all-gather.22.cloned.1.call-done = bf16[512,1024]{1,0:T(8,128)(2,1)} async-done(((bf16[64,1024]{1,0:T(8,128)(2,1)}), bf16[512,1024]{1,0:T(8,128)(2,1)}) %all-gather.22.cloned.1.call-update) | async-done | bytes 1048592 | tf_op jit(solution)/shard_map/all_gather | solution.py:238
  298.2 30.7 %all-reduce.29.cloned.1.call-done = f32[64,1024]{1,0:T(8,128)} async-done(((f32[64,1024]{1,0:T(8,128)}), f32[64,1024]{1,0:T(8,128)}) %all-reduce.29.cloned.1.call-update) | async-done | bytes 262160 | tf_op jit(solution)/shard_map/psum | solution.py:90
  329.9 74.5 %all-gather.24.cloned.1.call-done = bf16[1024,2048]{1,0:T(8,128)(2,1)} async-done(((bf16[128,2048]{1,0:T(8,128)(2,1)}), bf16[1024,2048]{1,0:T(8,128)(2,1)}) %all-gather.24.cloned.1.call-update) | async-done | bytes 4194320 | tf_op jit(solution)/shard_map/all_gather | solution.py:239
  404.4 3.7 convolution_convert_fusion.1
  408.8 33.4 %all_gather.92 = bf16[1024,256]{1,0:T(8,128)(2,1)} all-gather(bf16[128,256]{1,0:T(8,128)(2,1)S(1)} %copy-done.83), channel_id=1, replica_groups=mesh['seq'=8,'mp'=4] {'seq'}, dimensions={0}, use_global_device_ids=true | all-gather | bytes 589824 | tf_op jit(solution)/shard_map/all_gather | solution.py:244
  442.2 33.5 %all_gather.93 = bf16[1024,256]{1,0:T(8,128)(2,1)} all-gather(bf16[128,256]{1,0:T(8,128)(2,1)S(1)} %copy-done.84), channel_id=1, replica_groups=mesh['seq'=8,'mp'=4] {'seq'}, dimensions={0}, use_global_device_ids=true | all-gather | bytes 589824 | tf_op jit(solution)/shard_map/all_gather | solution.py:245
  475.8 33.7 %all_gather.91 = bf16[1024,256]{1,0:T(8,128)(2,1)} all-gather(bf16[128,256]{1,0:T(8,128)(2,1)S(1)} %copy-done.85), channel_id=1, replica_groups=mesh['seq'=8,'mp'=4] {'seq'}, dimensions={0}, use_global_device_ids=true | all-gather | bytes 589824 | tf_op jit(solution)/shard_map/all_gather | solution.py:246
  509.4 33.3 %all_gather.94 = bf16[256,1024]{1,0:T(8,128)(2,1)} all-gather(bf16[32,1024]{1,0:T(8,128)(2,1)S(1)} %copy-done.86), channel_id=1, replica_groups=mesh['seq'=8,'mp'=4] {'seq'}, dimensions={0}, use_global_device_ids=true | all-gather | bytes 589824 | tf_op jit(solution)/shard_map/all_gather | solution.py:247
  561.5 3.6 fusion.160
  571.1 2.9 fusion.166
  576.3 47.4 %all-reduce.31.cloned.1.call-done = f32[512,1024]{1,0:T(8,128)} async-done(((f32[512,1024]{1,0:T(8,128)}), f32[512,1024]{1,0:T(8,128)}) %all-reduce.31.cloned.1.call-update) | async-done | bytes 2097168 | tf_op jit(solution)/shard_map/psum | solution.py:90
  628.2 47.3 %all-gather.28.cloned.1.call-done = bf16[1024,1024]{1,0:T(8,128)(2,1)} async-done(((bf16[128,1024]{1,0:T(8,128)(2,1)}), bf16[1024,1024]{1,0:T(8,128)(2,1)}) %all-gather.28.cloned.1.call-update) | async-done | bytes 2097168 | tf_op jit(solution)/shard_map/all_gather | solution.py:248
  675.5 4.5 fusion.167
  680.0 45.5 %all-gather.30.cloned.1.call-done = bf16[1024,1024]{1,0:T(8,128)(2,1)} async-done(((bf16[128,1024]{1,0:T(8,128)(2,1)}), bf16[1024,1024]{1,0:T(8,128)(2,1)}) %all-gather.30.cloned.1.call-update) | async-done | bytes 2097168 | tf_op jit(solution)/shard_map/all_gather | solution.py:249
  725.5 4.5 fusion.168
  730.0 45.7 %all-gather.32.cloned.1.call-done = bf16[1024,1024]{1,0:T(8,128)(2,1)} async-done(((bf16[128,1024]{1,0:T(8,128)(2,1)}), bf16[1024,1024]{1,0:T(8,128)(2,1)}) %all-gather.32.cloned.1.call-update) | async-done | bytes 2097168 | tf_op jit(solution)/shard_map/all_gather | solution.py:250
  775.6 6.6 multiply_convert_fusion
  789.4 47.9 %all-reduce.33.cloned.1.call-done = f32[512,1024]{1,0:T(8,128)} async-done(((f32[512,1024]{1,0:T(8,128)}), f32[512,1024]{1,0:T(8,128)}) %all-reduce.33.cloned.1.call-update) | async-done | bytes 2097168 | tf_op jit(solution)/shard_map/psum | solution.py:90
  837.3 3.5 multiply_reduce_fusion
  848.1 3.7 fusion.8
  858.6 3.2 fusion.6
  869.2 3.0 fusion.172
  879.2 51.6 %all-reduce.35.cloned.1.call-done = f32[512,1024]{1,0:T(8,128)} async-done(((f32[512,1024]{1,0:T(8,128)}), f32[512,1024]{1,0:T(8,128)}) %all-reduce.35.cloned.1.call-update) | async-done | bytes 2097168 | tf_op jit(solution)/shard_map/psum | solution.py:90
  930.7 2.9 multiply_reduce_fusion.1
  938.0 4.5 fusion.90
  942.6 32.2 %all-reduce.37.cloned.1.call-done = f32[64,1024]{1,0:T(8,128)} async-done(((f32[64,1024]{1,0:T(8,128)}), f32[64,1024]{1,0:T(8,128)}) %all-reduce.37.cloned.1.call-update) | async-done | bytes 262160 | tf_op jit(solution)/shard_map/psum | solution.py:90
  977.4 5.9 psum.148
  987.2 4.2 fusion.169
  995.9 31.6 %all-gather.38.cloned.1.call-done = bf16[64,64,128]{2,1,0:T(8,128)(2,1)} async-done(((bf16[8,64,128]{2,1,0:T(8,128)(2,1)}), bf16[64,64,128]{2,1,0:T(8,128)(2,1)}) %all-gather.38.cloned.1.call-update) | async-done | bytes 1048592 | tf_op jit(solution)/shard_map/all_gather | solution.py:52
  1027.5 13.4 while.31
  1058.6 56.6 %all-reduce.39.cloned.1.call-done = (f32[512,1024]{1,0:T(8,128)}, f32[64,1024]{1,0:T(8,128)}, f32[64,256]{1,0:T(8,128)}) async-done(((f32[512,1024]{1,0:T(8,128)}, f32[64,1024]{1,0:T(8,128)}, f32[64,256]{1,0:T(8,128)}), (f32[512,1024]{1,0:T(8,128)}, f32[64,1024]{1,0:T(8,128)}, f32[64,256]{1,0:T(8,128)})) %all-reduce.39.cloned.1.call-update) | async-done | bytes 2424848 | tf_op jit(solution)/shard_map/psum | solution.py:90
  1118.3 4.1 collective-permute-done.3
  1124.0 4.3 convolution_convert_fusion
  1145.7 3.3 fusion.178
  1150.2 3.3 fusion.179
  1155.4 3.4 fusion.34
  1159.7 5.6 fusion.89
  1165.3 5.6 fusion.56
  1172.6 2.9 add_convert_fusion.1
  1175.6 36.3 %all-reduce.17 = (f32[1024]{0:T(1024)}, f32[4,512]{1,0:T(4,128)}, f32[4,256]{1,0:T(4,128)}, f32[8]{0:T(128)}, f32[8]{0:T(128)}, /*index=5*/f32[8]{0:T(128)}, f32[512]{0:T(512)}, f32[1024]{0:T(1024)}, f32[1024]{0:T(1024)}) all-reduce(f32[1024]{0:T(1024)S(1)} %get-tuple-element.293, ...), channel_id=1, replica_groups=mesh['seq'=8,'mp'=4] {'seq'}, use_global_device_ids=true, to_apply=%region_43.44 | all-reduce | flops 6680 | bytes 53440 | tf_op jit(solution)/shard_map/psum | solution.py:437
  1214.5 2.9 add_convert_fusion
  1217.3 62.1 %reduce-scatter.31.cloned.1.call-done = f32[128,256]{1,0:T(8,128)} async-done(((f32[1024,256]{1,0:T(8,128)}), f32[128,256]{1,0:T(8,128)}) %reduce-scatter.31.cloned.1.call-update) | async-done | bytes 131088 | tf_op jit(solution)/shard_map/reduce_scatter | solution.py:357
  1279.4 66.7 %reduce-scatter.35.cloned.1.call-done = f32[32,1024]{1,0:T(8,128)} async-done(((f32[256,1024]{1,0:T(8,128)}), f32[32,1024]{1,0:T(8,128)}) %reduce-scatter.35.cloned.1.call-update) | async-done | bytes 131088 | tf_op jit(solution)/shard_map/reduce_scatter | solution.py:359
  1346.1 66.4 %reduce-scatter.29.cloned.1.call-done = f32[128,256]{1,0:T(8,128)} async-done(((f32[1024,256]{1,0:T(8,128)}), f32[128,256]{1,0:T(8,128)}) %reduce-scatter.29.cloned.1.call-update) | async-done | bytes 131088 | tf_op jit(solution)/shard_map/reduce_scatter | solution.py:356
  1412.5 56.4 %reduce-scatter.23.cloned.1.call-done = f32[128,8]{0,1:T(8,128)} async-done(((f32[1024,8]{0,1:T(8,128)}), f32[128,8]{0,1:T(8,128)}) %reduce-scatter.23.cloned.1.call-update) | async-done | bytes 4112 | tf_op jit(solution)/shard_map/reduce_scatter | solution.py:433
  1468.9 71.5 %reduce-scatter.25.cloned.1.call-done = f32[64,1024]{1,0:T(8,128)} async-done(((f32[512,1024]{1,0:T(8,128)}), f32[64,1024]{1,0:T(8,128)}) %reduce-scatter.25.cloned.1.call-update) | async-done | bytes 262160 | tf_op jit(solution)/shard_map/reduce_scatter | solution.py:434
  1540.4 71.2 %reduce-scatter.17.cloned.1.call-done = f32[128,512]{1,0:T(8,128)} async-done(((f32[1024,512]{1,0:T(8,128)}), f32[128,512]{1,0:T(8,128)}) %reduce-scatter.17.cloned.1.call-update) | async-done | bytes 262160 | tf_op jit(solution)/shard_map/reduce_scatter | solution.py:430
  1611.6 66.7 %reduce-scatter.21.cloned.1.call-done = f32[128,256]{1,0:T(8,128)} async-done(((f32[1024,256]{1,0:T(8,128)}), f32[128,256]{1,0:T(8,128)}) %reduce-scatter.21.cloned.1.call-update) | async-done | bytes 131088 | tf_op jit(solution)/shard_map/reduce_scatter | solution.py:432
  1678.2 71.0 %reduce-scatter.19.cloned.1.call-done = f32[128,512]{1,0:T(8,128)} async-done(((f32[1024,512]{1,0:T(8,128)}), f32[128,512]{1,0:T(8,128)}) %reduce-scatter.19.cloned.1.call-update) | async-done | bytes 262160 | tf_op jit(solution)/shard_map/reduce_scatter | solution.py:431
  1749.3 91.3 %reduce-scatter.37.cloned.1.call-done = f32[128,1024]{1,0:T(8,128)} async-done(((f32[1024,1024]{1,0:T(8,128)}), f32[128,1024]{1,0:T(8,128)}) %reduce-scatter.37.cloned.1.call-update) | async-done | bytes 524304 | tf_op jit(solution)/shard_map/reduce_scatter | solution.py:360
  1840.5 92.2 %reduce-scatter.39.cloned.1.call-done = f32[128,1024]{1,0:T(8,128)} async-done(((f32[1024,1024]{1,0:T(8,128)}), f32[128,1024]{1,0:T(8,128)}) %reduce-scatter.39.cloned.1.call-update) | async-done | bytes 524304 | tf_op jit(solution)/shard_map/reduce_scatter | solution.py:361
  1932.7 91.9 %reduce-scatter.41.cloned.1.call-done = f32[128,1024]{1,0:T(8,128)} async-done(((f32[1024,1024]{1,0:T(8,128)}), f32[128,1024]{1,0:T(8,128)}) %reduce-scatter.41.cloned.1.call-update) | async-done | bytes 524304 | tf_op jit(solution)/shard_map/reduce_scatter | solution.py:362
  2024.6 153.4 %reduce-scatter.27.cloned.1.call-done = f32[128,2048]{1,0:T(8,128)} async-done(((f32[1024,2048]{1,0:T(8,128)}), f32[128,2048]{1,0:T(8,128)}) %reduce-scatter.27.cloned.1.call-update) | async-done | bytes 1048592 | tf_op jit(solution)/shard_map/reduce_scatter | solution.py:435
  2178.0 152.1 %reduce-scatter.15.cloned.1.call-done = f32[256,1024]{1,0:T(8,128)} async-done(((f32[2048,1024]{1,0:T(8,128)}), f32[256,1024]{1,0:T(8,128)}) %reduce-scatter.15.cloned.1.call-update) | async-done | bytes 1048592 | tf_op jit(solution)/shard_map/reduce_scatter | solution.py:429
  (597 shorter events, 179.1 us)
Async XLA Ops:
  7.2 79.1 %all-gather.16.cloned.1.call-start = ((), (), s32[]{:S(2)}) async-start(), calls=%async_computation.14 | async-start | bytes 4718592 | tf_op jit(solution)/shard_map/all_gather | solution.py:233
  7.9 143.8 %all-reduce.27.cloned.1.call-start = ((), (), s32[]{:S(2)}) async-start(), calls=%async_computation.15 | async-start | bytes 524288 | tf_op jit(solution)/shard_map/psum | solution.py:90
  9.5 80.5 %copy-start.38 = (bf16[64,8192]{1,0:T(8,128)(2,1)}, bf16[64,8192]{1,0:T(8,128)(2,1)S(1)}, u32[]{:S(2)}) copy-start(bf16[64,8192]{1,0:T(8,128)(2,1)S(1)} %reshape.393) | copy-start | bytes 3145732
  9.6 81.3 %copy-start.156 = (bf16[128,8]{0,1:T(8,128)(2,1)S(1)}, bf16[128,8]{0,1:T(8,128)(2,1)}, u32[]{:S(2)}) copy-start(bf16[128,8]{0,1:T(8,128)(2,1)} %param.38) | copy-start | bytes 6148
  9.6 107.3 %copy-start.165 = (f32[8]{0:T(128)S(1)}, f32[8]{0:T(128)}, u32[]{:S(2)}) copy-start(f32[8]{0:T(128)} %param.42) | copy-start | bytes 100
  9.6 107.3 %copy-start.170 = (s32[6]{0:T(128)S(1)}, s32[6]{0:T(128)}, u32[]{:S(2)}) copy-start(s32[6]{0:T(128)} %param.31) | copy-start | bytes 76
  9.6 108.8 %copy-start.155 = (f32[4,256]{1,0:T(4,128)S(1)}, f32[4,256]{1,0:T(4,128)}, u32[]{:S(2)}) copy-start(f32[4,256]{1,0:T(4,128)} %param.40) | copy-start | bytes 12292
  9.6 110.2 %copy-start.146 = (f32[4,512]{1,0:T(4,128)S(1)}, f32[4,512]{1,0:T(4,128)}, u32[]{:S(2)}) copy-start(f32[4,512]{1,0:T(4,128)} %param.39) | copy-start | bytes 24580
  9.6 110.2 %copy-start.82 = (bf16[128,256]{1,0:T(8,128)(2,1)S(1)}, bf16[128,256]{1,0:T(8,128)(2,1)}, u32[]{:S(2)}) copy-start(bf16[128,256]{1,0:T(8,128)(2,1)} %param.37) | copy-start | bytes 196612
  9.6 143.9 %copy-start.93 = (f32[1024]{0:T(1024)S(1)}, f32[1024]{0:T(1024)}, u32[]{:S(2)}) copy-start(f32[1024]{0:T(1024)} %param.33) | copy-start | bytes 12292
  9.6 144.9 %copy-start.171 = (f32[8]{0:T(128)S(1)}, f32[8]{0:T(128)}, u32[]{:S(2)}) copy-start(f32[8]{0:T(128)} %param.41) | copy-start | bytes 100
  90.0 73.5 %all-gather.18.cloned.1.call-start = ((), (), s32[]{:S(2)}) async-start(), calls=%async_computation.16 | async-start | bytes 1179648 | tf_op jit(solution)/shard_map/all_gather | solution.py:235
  90.8 122.0 %all-gather.36.cloned.1.call-start = ((), (), s32[]{:S(2)}) async-start(), calls=%async_computation.44 | async-start | bytes 1179648 | tf_op jit(solution)/shard_map/all_gather | solution.py:29
  155.3 12.4 collective-permute-start.1
  165.1 3.8 collective-permute-start
  171.1 82.9 %all-gather.20.cloned.1.call-start = ((), (), s32[]{:S(2)}) async-start(), calls=%async_computation.17 | async-start | bytes 1179648 | tf_op jit(solution)/shard_map/all_gather | solution.py:234
  171.6 123.5 %all-gather.22.cloned.1.call-start = ((), (), s32[]{:S(2)}) async-start(), calls=%async_computation.18 | async-start | bytes 1179648 | tf_op jit(solution)/shard_map/all_gather | solution.py:238
  172.2 156.7 %all-reduce.29.cloned.1.call-start = ((), (), s32[]{:S(2)}) async-start(), calls=%async_computation.19 | async-start | bytes 524288 | tf_op jit(solution)/shard_map/psum | solution.py:90
  221.3 73.9 %copy-start.105 = (f32[512]{0:T(512)S(1)}, f32[512]{0:T(512)}, u32[]{:S(2)}) copy-start(f32[512]{0:T(512)} %param.44) | copy-start | bytes 6148
  222.4 106.5 %copy-start.18 = (f32[64,1024]{1,0:T(8,128)S(1)}, f32[64,1024]{1,0:T(8,128)}, u32[]{:S(2)}) copy-start(f32[64,1024]{1,0:T(8,128)} %all-reduce.27.cloned.1.call-done) | copy-start | bytes 786436
  222.5 107.4 %copy-start.58 = (f32[64,512]{1,0:T(8,128)}, f32[64,512]{1,0:T(8,128)S(1)}, u32[]{:S(2)}) copy-start(f32[64,512]{1,0:T(8,128)S(1)} %copy.216) | copy-start | bytes 393220
  256.2 151.9 %copy-start.32 = (f32[64,512]{1,0:T(8,128)}, f32[64,512]{1,0:T(8,128)S(1)}, u32[]{:S(2)}) copy-start(f32[64,512]{1,0:T(8,128)S(1)} %get-tuple-element.360) | copy-start | bytes 393220
  262.5 145.7 %copy-start.136 = (f32[64]{0:T(128)}, f32[64]{0:T(128)S(1)}, u32[]{:S(2)}) copy-start(f32[64]{0:T(128)S(1)} %get-tuple-element.393) | copy-start | bytes 772
  297.4 107.0 %all-gather.24.cloned.1.call-start = ((), (), s32[]{:S(2)}) async-start(), calls=%async_computation.20 | async-start | bytes 4718592 | tf_op jit(solution)/shard_map/all_gather | solution.py:239
  298.2 244.6 %all-gather.26.cloned.1.call-start = ((), (), s32[]{:S(2)}) async-start(), calls=%async_computation.21 | async-start | bytes 1310720 | tf_op jit(solution)/shard_map/all_gather | solution.py:94
  329.9 78.3 %copy-start.52 = (bf16[64,1024]{1,0:T(8,128)(2,1)}, bf16[64,1024]{1,0:T(8,128)(2,1)S(1)}, u32[]{:S(2)}) copy-start(bf16[64,1024]{1,0:T(8,128)(2,1)S(1)} %add_convert_fusion.2) | copy-start | bytes 393220
  329.9 78.9 %copy-start.83 = (bf16[128,256]{1,0:T(8,128)(2,1)S(1)}, bf16[128,256]{1,0:T(8,128)(2,1)}, u32[]{:S(2)}) copy-start(bf16[128,256]{1,0:T(8,128)(2,1)} %param.48) | copy-start | bytes 196612
  329.9 112.3 %copy-start.84 = (bf16[128,256]{1,0:T(8,128)(2,1)S(1)}, bf16[128,256]{1,0:T(8,128)(2,1)}, u32[]{:S(2)}) copy-start(bf16[128,256]{1,0:T(8,128)(2,1)} %param.49) | copy-start | bytes 196612
  329.9 145.8 %copy-start.85 = (bf16[128,256]{1,0:T(8,128)(2,1)S(1)}, bf16[128,256]{1,0:T(8,128)(2,1)}, u32[]{:S(2)}) copy-start(bf16[128,256]{1,0:T(8,128)(2,1)} %param.50) | copy-start | bytes 196612
  329.9 179.5 %copy-start.86 = (bf16[32,1024]{1,0:T(8,128)(2,1)S(1)}, bf16[32,1024]{1,0:T(8,128)(2,1)}, u32[]{:S(2)}) copy-start(bf16[32,1024]{1,0:T(8,128)(2,1)} %param.51) | copy-start | bytes 196612
  408.2 215.5 %all-reduce.31.cloned.1.call-start = ((), (), s32[]{:S(2)}) async-start(), calls=%async_computation.22 | async-start | bytes 4194304 | tf_op jit(solution)/shard_map/psum | solution.py:90
  475.8 69.6 %copy-start.25 = (bf16[512,1024]{1,0:T(8,128)(2,1)S(1)}, bf16[512,1024]{1,0:T(8,128)(2,1)}, u32[]{:S(2)}) copy-start(bf16[512,1024]{1,0:T(8,128)(2,1)} %param.30) | copy-start | bytes 3145732
  574.0 101.5 %all-gather.28.cloned.1.call-start = ((), (), s32[]{:S(2)}) async-start(), calls=%async_computation.23 | async-start | bytes 2359296 | tf_op jit(solution)/shard_map/all_gather | solution.py:248
  574.7 150.8 %all-gather.30.cloned.1.call-start = ((), (), s32[]{:S(2)}) async-start(), calls=%async_computation.24 | async-start | bytes 2359296 | tf_op jit(solution)/shard_map/all_gather | solution.py:249
  575.3 200.4 %all-gather.32.cloned.1.call-start = ((), (), s32[]{:S(2)}) async-start(), calls=%async_computation.25 | async-start | bytes 2359296 | tf_op jit(solution)/shard_map/all_gather | solution.py:250
  576.0 261.2 %all-reduce.33.cloned.1.call-start = ((), (), s32[]{:S(2)}) async-start(), calls=%async_computation.26 | async-start | bytes 4194304 | tf_op jit(solution)/shard_map/psum | solution.py:90
  787.2 143.5 %all-reduce.35.cloned.1.call-start = ((), (), s32[]{:S(2)}) async-start(), calls=%async_computation.27 | async-start | bytes 4194304 | tf_op jit(solution)/shard_map/psum | solution.py:90
  879.1 95.6 %all-reduce.37.cloned.1.call-start = ((), (), s32[]{:S(2)}) async-start(), calls=%async_computation.28 | async-start | bytes 524288 | tf_op jit(solution)/shard_map/psum | solution.py:90
  942.5 85.0 %all-gather.38.cloned.1.call-start = ((), (), s32[]{:S(2)}) async-start(), calls=%async_computation.45 | async-start | bytes 1179648 | tf_op jit(solution)/shard_map/all_gather | solution.py:52
  987.1 128.1 %all-reduce.39.cloned.1.call-start = ((), (), s32[]{:S(2)}) async-start(), calls=%async_computation.46 | async-start | bytes 4849664 | tf_op jit(solution)/shard_map/psum | solution.py:90
  1051.4 5.5 collective-permute-start.2
  1057.1 59.7 %copy-start.129 = (f32[1,256]{1,0:T(1,128)S(1)}, f32[1,256]{1,0:T(1,128)}, u32[]{:S(2)}) copy-start(f32[1,256]{1,0:T(1,128)} %copy-done.128) | copy-start | bytes 3076
  1058.5 63.9 %copy-start.19 = (f32[64,1024]{1,0:T(8,128)S(1)}, f32[64,1024]{1,0:T(8,128)}, u32[]{:S(2)}) copy-start(f32[64,1024]{1,0:T(8,128)} %all-reduce.27.cloned.1.call-done) | copy-start | bytes 786436
  1058.5 63.9 %copy-start.21 = (bf16[1024,256]{1,0:T(8,128)(2,1)S(1)}, bf16[1024,256]{1,0:T(8,128)(2,1)}, u32[]{:S(2)}) copy-start(bf16[1024,256]{1,0:T(8,128)(2,1)} %copy-done.20) | copy-start | bytes 1572868
  1058.5 63.9 %copy-start.94 = (f32[1024]{0:T(1024)S(1)}, f32[1024]{0:T(1024)}, u32[]{:S(2)}) copy-start(f32[1024]{0:T(1024)} %param.33) | copy-start | bytes 12292
  1058.5 64.0 %copy-start.149 = (f32[64]{0:T(128)S(1)}, f32[64]{0:T(128)}, u32[]{:S(2)}) copy-start(f32[64]{0:T(128)} %copy-done.148) | copy-start | bytes 772
  1058.5 65.3 %copy-start.164 = (f32[64]{0:T(128)S(1)}, f32[64]{0:T(128)}, u32[]{:S(2)}) copy-start(f32[64]{0:T(128)} %copy-done.163) | copy-start | bytes 772
  1058.5 65.3 %copy-start.41 = (f32[64,1024]{1,0:T(8,128)S(1)}, f32[64,1024]{1,0:T(8,128)}, u32[]{:S(2)}) copy-start(f32[64,1024]{1,0:T(8,128)} %all-reduce.37.cloned.1.call-done) | copy-start | bytes 786436
  1058.6 153.3 %all-gather.34.cloned.1.call-start = ((), (), s32[]{:S(2)}) async-start(), calls=%async_computation.29 | async-start | bytes 1310720 | tf_op jit(solution)/shard_map/all_gather | solution.py:94
  1116.9 5.5 collective-permute-start.3
  1128.3 89.0 %reduce-scatter.33.cloned.1.call-start = ((), (), s32[]{:S(2)}) async-start(), calls=%async_computation.39 | async-start | bytes 1179648 | tf_op jit(solution)/shard_map/reduce_scatter | solution.py:358
  1129.9 149.6 %reduce-scatter.31.cloned.1.call-start = ((), (), s32[]{:S(2)}) async-start(), calls=%async_computation.38 | async-start | bytes 1179648 | tf_op jit(solution)/shard_map/reduce_scatter | solution.py:357
  1132.5 213.7 %reduce-scatter.35.cloned.1.call-start = ((), (), s32[]{:S(2)}) async-start(), calls=%async_computation.40 | async-start | bytes 1179648 | tf_op jit(solution)/shard_map/reduce_scatter | solution.py:359
  1134.9 277.6 %reduce-scatter.29.cloned.1.call-start = ((), (), s32[]{:S(2)}) async-start(), calls=%async_computation.37 | async-start | bytes 1179648 | tf_op jit(solution)/shard_map/reduce_scatter | solution.py:356
  1137.5 331.4 %reduce-scatter.23.cloned.1.call-start = ((), (), s32[]{:S(2)}) async-start(), calls=%async_computation.34 | async-start | bytes 36864 | tf_op jit(solution)/shard_map/reduce_scatter | solution.py:433
  1138.3 402.1 %reduce-scatter.25.cloned.1.call-start = ((), (), s32[]{:S(2)}) async-start(), calls=%async_computation.35 | async-start | bytes 2359296 | tf_op jit(solution)/shard_map/reduce_scatter | solution.py:434
  1140.3 471.3 %reduce-scatter.17.cloned.1.call-start = ((), (), s32[]{:S(2)}) async-start(), calls=%async_computation.31 | async-start | bytes 2359296 | tf_op jit(solution)/shard_map/reduce_scatter | solution.py:430
  1142.1 536.1 %reduce-scatter.21.cloned.1.call-start = ((), (), s32[]{:S(2)}) async-start(), calls=%async_computation.33 | async-start | bytes 1179648 | tf_op jit(solution)/shard_map/reduce_scatter | solution.py:432
  1143.6 605.7 %reduce-scatter.19.cloned.1.call-start = ((), (), s32[]{:S(2)}) async-start(), calls=%async_computation.32 | async-start | bytes 2359296 | tf_op jit(solution)/shard_map/reduce_scatter | solution.py:431
  1145.4 695.1 %reduce-scatter.37.cloned.1.call-start = ((), (), s32[]{:S(2)}) async-start(), calls=%async_computation.41 | async-start | bytes 4718592 | tf_op jit(solution)/shard_map/reduce_scatter | solution.py:360
  1149.0 783.7 %reduce-scatter.39.cloned.1.call-start = ((), (), s32[]{:S(2)}) async-start(), calls=%async_computation.42 | async-start | bytes 4718592 | tf_op jit(solution)/shard_map/reduce_scatter | solution.py:361
  1153.6 871.0 %reduce-scatter.41.cloned.1.call-start = ((), (), s32[]{:S(2)}) async-start(), calls=%async_computation.43 | async-start | bytes 4718592 | tf_op jit(solution)/shard_map/reduce_scatter | solution.py:362
  1158.8 1019.2 %reduce-scatter.27.cloned.1.call-start = ((), (), s32[]{:S(2)}) async-start(), calls=%async_computation.36 | async-start | bytes 9437184 | tf_op jit(solution)/shard_map/reduce_scatter | solution.py:435
  1165.3 1164.9 %reduce-scatter.15.cloned.1.call-start = ((), (), s32[]{:S(2)}) async-start(), calls=%async_computation.30 | async-start | bytes 9437184 | tf_op jit(solution)/shard_map/reduce_scatter | solution.py:429
  (145 other events, 2392.2 us)
Sparse Core Ops, SparseCore 0:
  10.2 76.0 all-gather.15
  90.2 30.2 all-reduce.26
  122.8 40.7 all-gather.17
  171.2 41.6 all-gather.35
  215.0 38.8 all-gather.19
  256.2 38.8 all-gather.21
  298.1 30.7 all-reduce.28
  331.0 73.3 all-gather.23
  408.3 14.9 all-gather.25
  574.1 49.6 all-reduce.30
  626.1 49.3 all-gather.27
  677.7 47.7 all-gather.29
  727.8 47.7 all-gather.31
  787.4 49.8 all-reduce.32
  879.2 51.4 all-reduce.34
  942.6 32.0 all-reduce.36
  987.2 40.2 all-gather.37
  1058.7 56.4 all-reduce.38
  1128.5 16.7 all-gather.33
  1149.5 63.3 reduce-scatter.32
  1216.9 62.5 reduce-scatter.30
  1283.8 62.2 reduce-scatter.34
  1350.1 62.3 reduce-scatter.28
  1416.4 52.4 reduce-scatter.22
  1473.4 66.8 reduce-scatter.24
  1544.8 66.7 reduce-scatter.16
  1615.8 62.4 reduce-scatter.20
  1682.3 66.8 reduce-scatter.18
  1753.5 87.0 reduce-scatter.36
  1845.0 87.6 reduce-scatter.38
  1936.9 87.6 reduce-scatter.40
  2029.3 148.7 reduce-scatter.26
  2182.1 148.0 reduce-scatter.14
where the time goes:
time: 2350 us; the launch traced here: 2340 us
  waiting for transfers between devices  1800 us (77%)
  blocking collectives  260 us (11%)
  matrix products  135 us (6%)
  other arithmetic  65.5 us (3%)
  local copies, waits for them, and re-layouts  47.2 us (2%)
    psum x7, waiting for transfers between devices, over_heads(): return lax.psum(partial_sum, 'mp')  266 us
    reduce_scatter x1, waiting for transfers between devices, shards(): lax.psum_scatter(grad_patch_out, 'seq', scatter_dimension=0, tiled=True)  153 us
    reduce_scatter x1, waiting for transfers between devices, shards(): lax.psum_scatter(grad_patch_in, 'seq', scatter_dimension=0, tiled=True)  152 us
    reduce_scatter x1, waiting for transfers between devices, shards(): lax.psum_scatter(grad_feed_up, 'seq', scatter_dimension=0, tiled=True)  92.2 us
    reduce_scatter x1, waiting for transfers between devices, shards(): lax.psum_scatter(grad_feed_down, 'seq', scatter_dimension=0, tiled=True)  91.9 us
    reduce_scatter x1, waiting for transfers between devices, shards(): lax.psum_scatter(grad_feed_gate, 'seq', scatter_dimension=0, tiled=True)  91.3 us
    all_gather x1, waiting for transfers between devices, fetch_global(): lax.all_gather(patch_in, 'seq', axis=0, tiled=True)  76.6 us
    all_gather x1, waiting for transfers between devices, fetch_global(): lax.all_gather(patch_out, 'seq', axis=0, tiled=True)  74.5 us
  transfers between devices with their start and end apart: 37, of which 32 were waited for; matrix products, arithmetic and copies ran while one was open for 4% of the time, Pallas kernels for 0%

commit v1 on v0

--- a/solution.py
+++ b/solution.py
@@ -106,8 +106,20 @@
     return pullback(upstream)
 
 
+def running_bounds(lengths):
+    places = jnp.arange(lengths.shape[0])
+    upto = places[None, :] <= places[:-1, None]
+    return jnp.sum(jnp.where(upto, lengths[None, :], 0), axis=1)
+
+
+def running_sum(values):
+    places = jnp.arange(values.shape[0])
+    lower = (places[:, None] >= places[None, :]).astype(jnp.float32)
+    return jnp.dot(lower, values, precision=HIGH, preferred_element_type=jnp.float32)
+
+
 def segment_of(lengths, start_row, row_count):
-    bounds = jnp.cumsum(lengths)[:-1]
+    bounds = running_bounds(lengths)
     places = start_row + jnp.arange(row_count, dtype=jnp.int32)
     return jnp.sum((places[:, None] >= bounds[None, :]).astype(jnp.int32), axis=1)
 
@@ -137,7 +149,7 @@
     segment_prev,
 ):
     length = head_values.shape[0]
-    running = jnp.cumsum(-step_size * jnp.exp(log_rate), axis=0)
+    running = running_sum(-step_size * jnp.exp(log_rate))
     places = jnp.arange(length)
     allowed = (places[:, None] >= places[None, :]) & (
         segment_rows[:, None] == segment_rows[None, :]
@@ -157,7 +169,7 @@
 
 
 def block_summary(head_values, write_vecs, step_size, log_rate, segment_rows, segment_prev):
-    running = jnp.cumsum(-step_size * jnp.exp(log_rate), axis=0)
+    running = running_sum(-step_size * jnp.exp(log_rate))
     latest = running[-1]
     in_tail = (segment_rows == segment_rows[-1])[:, None]
     weights = jnp.where(in_tail, jnp.exp(latest[None, :] - running), 0.0) * step_size
@@ -192,7 +204,7 @@
     return jnp.concatenate([main_rows[:keep_count], main_rows[keep_count:] + tail_rows], axis=0)
 
 
-def shards(
+def gathered_plan(
     byte_input,
     seq_lengths,
     cotangent,
@@ -477,6 +489,487 @@
     )
 
 
+PAIR_X = [(i, i ^ 1) for i in range(8)]
+PAIR_C = [(i, i ^ 1) for i in range(4)]
+PAIR_Y = [(i, i ^ 2) for i in range(4)]
+
+
+def bf(values):
+    return values.astype(jnp.bfloat16)
+
+
+def swap_x(shard):
+    return lax.ppermute(shard, "seq", PAIR_X)
+
+
+def swap_c(shard):
+    return lax.ppermute(shard, "mp", PAIR_C)
+
+
+def swap_y(shard):
+    return lax.ppermute(shard, "mp", PAIR_Y)
+
+
+def swap_seq(shard, by):
+    return lax.ppermute(shard, "seq", [(i, i ^ by) for i in range(8)])
+
+
+def pick(stacked, index):
+    return lax.dynamic_index_in_dim(stacked, index, 0, keepdims=False)
+
+
+def in_order(mine, other, bit):
+    first = jnp.where(bit == 0, mine, other)
+    second = jnp.where(bit == 0, other, mine)
+    return jnp.concatenate([first, second], axis=0)
+
+
+def select_blocks(blocks, own, count):
+    placed = []
+    for j in range(count):
+        value = blocks[0]
+        for k in range(1, count):
+            value = jnp.where((own ^ k) == j, blocks[k], value)
+        placed.append(value)
+    return placed
+
+
+def scatter_rows(partial, place):
+    z, x, c = place
+    width = partial.shape[1]
+    halves = partial.reshape(2, -1, width)
+    rows = pick(halves, c) + swap_c(bf(pick(halves, 1 - c))).astype(jnp.float32)
+    halves = rows.reshape(2, -1, width)
+    rows = pick(halves, x) + swap_x(bf(pick(halves, 1 - x))).astype(jnp.float32)
+    parts = rows.reshape(4, -1, width)
+    low = bf(parts)
+    rows = pick(parts, z)
+    got = [swap_seq(pick(low, z ^ k), 2 * k) for k in range(1, 4)]
+    for part in got:
+        rows = rows + part.astype(jnp.float32)
+    return rows
+
+
+def gather_rows(rows, place):
+    z, x, c = place
+    parts = [rows] + [swap_seq(rows, 2 * k) for k in range(1, 4)]
+    rows = jnp.concatenate(select_blocks(parts, z, 4), axis=0)
+    rows = in_order(rows, swap_x(rows), x)
+    return in_order(rows, swap_c(rows), c)
+
+
+def both_y(rows):
+    low = bf(rows)
+    return low.astype(jnp.float32) + swap_y(low).astype(jnp.float32)
+
+
+def gather_bytes(rows):
+    far = swap_y(rows)
+    return [rows, swap_c(rows), far, swap_c(far)]
+
+
+def scatter_bytes(partial):
+    width = partial.shape[1]
+    blocks = partial.reshape(4, -1, width)
+    sent = swap_c(bf(jnp.stack([blocks[1], blocks[3]])))
+    near = blocks[0] + sent[0].astype(jnp.float32)
+    far = blocks[2] + sent[1].astype(jnp.float32)
+    return near + swap_y(bf(far)).astype(jnp.float32)
+
+
+def exchange_seq(stacked, s):
+    got = [pick(stacked, s)] + [swap_seq(pick(stacked, s ^ k), k) for k in range(1, 8)]
+    return jnp.stack(select_blocks(got, s, 8))
+
+
+def mixer_core(input_pre, state_pre, step_pre, taps, state_taps, bias, log_rate, skip, segment):
+    length = input_pre.shape[0]
+    seg_ext = jnp.concatenate([jnp.full((KCONV - 1,), -1, jnp.int32), segment])
+
+    def conv(values, kernel):
+        return conv_silu(jnp.pad(values, ((KCONV - 1, 0), (0, 0))), kernel, seg_ext)
+
+    heads = conv(input_pre, taps)
+    state = conv(state_pre, state_taps)
+    writes, reads = (state[:, :NSTATE], state[:, NSTATE:])
+    step_size = jax.nn.softplus(step_pre + bias)
+    running = running_sum(-step_size * jnp.exp(log_rate))
+    places = jnp.arange(length)
+    allowed = (places[:, None] >= places[None, :]) & (segment[:, None] == segment[None, :])
+    affinity = product_right(bf(reads), bf(writes))
+    outs = []
+    for h in range(input_pre.shape[1] // HDIM):
+        values = heads[:, h * HDIM : (h + 1) * HDIM]
+        spread = jnp.where(allowed, running[:, h : h + 1] - running[:, h][None, :], 0.0)
+        factors = jnp.where(allowed, jnp.exp(spread), 0.0)
+        mixing = bf(factors * affinity)
+        outs.append(
+            product(mixing, bf(values * step_size[:, h : h + 1])) + skip[h] * values
+        )
+    return jnp.concatenate(outs, axis=1)
+
+
+def block_attention(queries, keys, values):
+    rows, width = queries.shape
+    heads = width // HDIM
+    q, k, v = (a.reshape(rows // 128, 128, heads, HDIM) for a in (queries, keys, values))
+    scores = jnp.einsum(
+        "bihd,bjhd->bhij", bf(q), bf(k), preferred_element_type=jnp.float32
+    ) * HDIM ** (-0.5)
+    i, j = (jnp.arange(128)[:, None], jnp.arange(128)[None, :])
+    mask = (i >= j) & (i // PATCH == j // PATCH)
+    scores = jnp.where(mask, scores, -1e30)
+    peak = jnp.max(scores, axis=-1, keepdims=True)
+    probs = jnp.exp(scores - peak)
+    probs = probs / jnp.sum(probs, axis=-1, keepdims=True)
+    out = jnp.einsum("bhij,bjhd->bihd", bf(probs), bf(v), preferred_element_type=jnp.float32)
+    return out.reshape(rows, width)
+
+
+def split_plan(
+    byte_input,
+    seq_lengths,
+    cotangent,
+    gain_global,
+    patch_in,
+    mixer_gate,
+    mixer_input,
+    mixer_state,
+    mixer_step,
+    conv_input,
+    conv_state,
+    step_bias,
+    decay_log,
+    skip_gain,
+    gain_mixer,
+    mixer_out,
+    patch_out,
+    gain_attend,
+    attend_query,
+    attend_key,
+    attend_value,
+    attend_out,
+    gain_feed,
+    feed_gate,
+    feed_up,
+    feed_down,
+):
+    s, m = (lax.axis_index("seq"), lax.axis_index("mp"))
+    z, x, y, c = (s // 2, s % 2, m // 2, m % 2)
+    place = (z, x, c)
+    patches = 512
+    f32 = jnp.float32
+
+    step_far = swap_y(mixer_step)
+    gathered_a = lax.all_gather(
+        jnp.concatenate(
+            [
+                mixer_state,
+                mixer_step,
+                step_far,
+                jnp.zeros((128, 112), jnp.bfloat16),
+                attend_query,
+                attend_key,
+                attend_value,
+            ],
+            axis=1,
+        ),
+        "seq",
+        axis=0,
+        tiled=True,
+    )
+    gathered_b = lax.all_gather(
+        jnp.concatenate([feed_gate, feed_up, attend_out.reshape(128, 256)], axis=1),
+        "seq",
+        axis=0,
+        tiled=True,
+    )
+    down = lax.all_gather(feed_down, "seq", axis=0, tiled=True)
+    w_state = gathered_a[:, :256]
+    w_step = jnp.concatenate(
+        [
+            lax.dynamic_slice_in_dim(gathered_a, 256 + jnp.where(y == 0, s, 8 + s), 1, 1),
+            lax.dynamic_slice_in_dim(gathered_a, 256 + jnp.where(y == 0, 8 + s, s), 1, 1),
+        ],
+        axis=1,
+    )
+    w_qkv = gathered_a[:, 384:]
+    w_gate, w_up = (gathered_b[:, :1024], gathered_b[:, 1024:2048])
+    w_out = gathered_b[:, 2048:].reshape(256, 1024)
+
+    own_slots = lax.dynamic_slice_in_dim(byte_input.reshape(64, PATCH, E), 2 * m, 2, 1)
+    sent = own_slots.reshape(64, 8, 256).transpose(1, 0, 2)
+    columns_in = lax.all_to_all(sent, "seq", 0, 0, tiled=True).reshape(patches, 256)
+    hidden = both_y(scatter_rows(product(columns_in, patch_in), place))
+    normed = gather_rows(bf(rms_scale(hidden, gain_global)), place)
+
+    moved = jnp.concatenate(
+        [
+            mixer_gate.reshape(128, 8, HDIM),
+            mixer_input.reshape(128, 8, HDIM),
+            patch_out.reshape(128, 8, 256),
+        ],
+        axis=2,
+    ).transpose(1, 0, 2)
+    moved = exchange_seq(moved, s).reshape(1024, 384)
+    heads_own = moved[:, : 2 * HDIM]
+    w_patch = moved[:, 2 * HDIM :]
+    heads_far = swap_y(heads_own)
+    w_first = jnp.where(y == 0, heads_own, heads_far)
+    w_second = jnp.where(y == 0, heads_far, heads_own)
+    w_heads = jnp.concatenate(
+        [w_first[:, :HDIM], w_second[:, :HDIM], w_first[:, HDIM:], w_second[:, HDIM:]], axis=1
+    )
+    w_mixout = in_order(mixer_out, swap_y(mixer_out), y)
+    table = jnp.concatenate(
+        [
+            lax.dynamic_slice_in_dim(conv_input, s * HDIM, HDIM, 1),
+            lax.dynamic_slice_in_dim(gain_mixer, s * HDIM, HDIM, 0)[None],
+            jnp.broadcast_to(lax.dynamic_slice_in_dim(step_bias, s, 1, 0)[:, None], (1, HDIM)),
+            jnp.broadcast_to(lax.dynamic_slice_in_dim(decay_log, s, 1, 0)[:, None], (1, HDIM)),
+            jnp.broadcast_to(lax.dynamic_slice_in_dim(skip_gain, s, 1, 0)[:, None], (1, HDIM)),
+        ],
+        axis=0,
+    )
+    table = in_order(table[None], swap_y(table)[None], y)
+    taps = jnp.concatenate([table[0, :4], table[1, :4]], axis=1)
+    gain_heads = jnp.concatenate([table[0, 4], table[1, 4]])
+    bias, log_rate, skip = (table[:, 5, 0], table[:, 6, 0], table[:, 7, 0])
+
+    heads_pre = product(normed, w_heads)
+    gate_pre, input_pre = (heads_pre[:, :128], heads_pre[:, 128:])
+    state_pre = product(normed, w_state)
+    step_pre = product(normed, w_step)
+    segment = segment_of(seq_lengths, 0, patches)
+    mixer_rows, core_pull = jax.vjp(
+        lambda *a: mixer_core(*a, segment),
+        input_pre,
+        state_pre,
+        step_pre,
+        taps,
+        conv_state,
+        bias,
+        log_rate,
+        skip,
+    )
+    gate_sigm = jax.nn.sigmoid(gate_pre)
+    gate_silu = gate_pre * gate_sigm
+    gated = mixer_rows * gate_silu
+    scaled = bf(gated * gain_heads)
+    squares = jnp.broadcast_to(jnp.sum(gated * gated, axis=1, keepdims=True), (patches, 128))
+    sums = scatter_rows(jnp.concatenate([product(scaled, w_mixout), squares], axis=1), place)
+    unscaled, root = (sums[:, :1024], lax.rsqrt(sums[:, 1024:1025] / DI + EPS))
+    merged_low = gather_rows(bf(hidden + root * unscaled), place)
+    slots = bf(product(merged_low, w_patch)).reshape(32, 16, 256)
+    slots = lax.all_to_all(slots, ("seq", "mp"), 0, 0, tiled=True)
+    slots = slots.reshape(8, 4, 16, 256).transpose(2, 1, 0, 3).reshape(128, E)
+    residual = lax.dynamic_slice_in_dim(byte_input, m * 128, 128, 0).astype(f32) + slots
+
+    attend_in = jnp.concatenate(gather_bytes(bf(rms_scale(residual, gain_attend))), axis=0)
+    qkv = product(attend_in, w_qkv)
+    context_raw, attention_pull = jax.vjp(
+        block_attention, qkv[:, :256], qkv[:, 256:512], qkv[:, 512:]
+    )
+    context = bf(context_raw)
+    middle = residual + scatter_bytes(product(context, w_out))
+    feed_in = jnp.concatenate(gather_bytes(bf(rms_scale(middle, gain_feed))), axis=0)
+    gate_value = product(feed_in, w_gate)
+    up_value = product(feed_in, w_up)
+    gate_sig = jax.nn.sigmoid(gate_value)
+    hidden_units = bf(gate_value * gate_sig * up_value)
+
+    cot_blocks = cotangent.reshape(4, 128, E)
+    cot_rows = pick(cot_blocks, m)
+    out_low = jnp.concatenate([bf(pick(cot_blocks, m ^ k)) for k in range(4)], axis=0)
+    grad_units = product_right(out_low, down)
+    grad_gate_value = bf(grad_units * up_value * gate_sig * (1.0 + gate_value * (1.0 - gate_sig)))
+    grad_up_value = bf(grad_units * gate_value * gate_sig)
+    grad_feed_in = scatter_bytes(
+        product_right(grad_gate_value, w_gate) + product_right(grad_up_value, w_up)
+    )
+    sum_gate = lax.psum_scatter(
+        bf(product_left(feed_in, grad_gate_value)), "seq", scatter_dimension=0, tiled=True
+    )
+    sum_up = lax.psum_scatter(
+        bf(product_left(feed_in, grad_up_value)), "seq", scatter_dimension=0, tiled=True
+    )
+    grad_middle_part, gain_feed_part = rms_back(middle, gain_feed, grad_feed_in)
+    grad_middle = cot_rows + grad_middle_part
+    middle_low = jnp.concatenate(gather_bytes(bf(grad_middle)), axis=0)
+    grad_context = product_right(middle_low, w_out)
+    grad_qkv = bf(jnp.concatenate(attention_pull(grad_context), axis=1))
+    grad_attend_in = scatter_bytes(product_right(grad_qkv, w_qkv))
+    sum_rest = lax.psum_scatter(
+        jnp.concatenate(
+            [
+                bf(product_left(context, middle_low)).reshape(8, 32, 1024),
+                bf(product_left(hidden_units, out_low)).reshape(8, 128, 1024),
+            ],
+            axis=1,
+        ).reshape(1280, 1024),
+        "seq",
+        scatter_dimension=0,
+        tiled=True,
+    )
+    sum_qkv = lax.psum_scatter(
+        bf(product_left(attend_in, grad_qkv)), "seq", scatter_dimension=0, tiled=True
+    )
+    grad_residual_part, gain_attend_part = rms_back(residual, gain_attend, grad_attend_in)
+    grad_residual = grad_middle + grad_residual_part
+
+    out_rows = bf(middle + scatter_bytes(product(hidden_units, down)))
+    byte_output = jnp.concatenate(select_blocks(gather_bytes(out_rows), m, 4), axis=0)
+
+    slot_rows = bf(grad_residual).reshape(16, 4, 8, 256).transpose(2, 1, 0, 3).reshape(32, 16, 256)
+    slot_grad = lax.all_to_all(slot_rows, ("seq", "mp"), 0, 0, tiled=True).reshape(patches, 256)
+    grad_patch_cols = bf(product_left(merged_low, slot_grad))
+    grad_patch_out = (
+        exchange_seq(grad_patch_cols.reshape(8, 128, 256), s)
+        .transpose(1, 0, 2)
+        .reshape(128, 2048)
+        .astype(f32)
+    )
+    merged_rows = scatter_rows(product_right(slot_grad, w_patch), place)
+    gains = jnp.stack([gain_feed_part, gain_attend_part])
+    merged_rows = both_y(jnp.concatenate([merged_rows, gains, jnp.zeros((6, 1024), f32)], axis=0))
+    grad_merged, gain_rows = (merged_rows[:32], merged_rows[32:])
+    merged_grad_low = bf(grad_merged).astype(f32)
+    kappa = jnp.sum(merged_grad_low * unscaled, axis=1, keepdims=True) * root**3 / DI
+    sent = jnp.concatenate(
+        [
+            jnp.concatenate([merged_grad_low * root, jnp.broadcast_to(kappa, (32, 128))], axis=1),
+            jnp.concatenate([gain_rows, jnp.zeros((8, 128), f32)], axis=1),
+        ],
+        axis=0,
+    )
+    got = gather_rows(bf(sent), place).reshape(16, 40, 1152)
+    merged_grad = got[:, :32, :1024].reshape(patches, 1024)
+    kappa = got[:, :32, 1024:1025].reshape(patches, 1).astype(f32)
+    grad_gain_feed = jnp.sum(got[:, 32, :1024].astype(f32), axis=0)
+    grad_gain_attend = jnp.sum(got[:, 33, :1024].astype(f32), axis=0)
+
+    grad_mixed = product_right(merged_grad, w_mixout)
+    scaled_own = jnp.where(y == 0, scaled[:, :HDIM], scaled[:, HDIM:])
+    grad_mixer_out = product_left(scaled_own, merged_grad)
+    grad_gain_heads = jnp.sum(grad_mixed * gated, axis=0)
+    grad_gated = grad_mixed * gain_heads - gated * kappa
+    grad_gate_low = bf(grad_gated * mixer_rows * gate_sigm * (1.0 + gate_pre * (1.0 - gate_sigm)))
+    (
+        grad_input_pre,
+        grad_state_pre,
+        grad_step_pre,
+        grad_taps,
+        grad_state_taps,
+        grad_bias,
+        grad_log_rate,
+        grad_skip,
+    ) = core_pull(grad_gated * gate_silu)
+    grad_input_low = bf(grad_input_pre)
+    grad_state_low = bf(grad_state_pre)
+    grad_step_low = bf(grad_step_pre)
+    grad_normed = (
+        product_right(jnp.concatenate([grad_gate_low, grad_input_low], axis=1), w_heads)
+        + product_right(grad_state_low, w_state)
+        + product_right(grad_step_low, w_step)
+    )
+    sums = scatter_rows(jnp.concatenate([grad_normed, grad_state_pre], axis=1), place)
+    grad_hidden_part, gain_global_part = rms_back(hidden, gain_global, sums[:, :1024])
+    hidden_rows = grad_merged + grad_hidden_part
+
+    def own(pair):
+        return jnp.where(y == 0, pair[0], pair[1])
+
+    head_row = jnp.concatenate(
+        [
+            jnp.where(y == 0, grad_taps[:, :HDIM], grad_taps[:, HDIM:]).reshape(4 * HDIM),
+            jnp.where(y == 0, grad_gain_heads[:HDIM], grad_gain_heads[HDIM:]),
+            own(grad_bias)[None],
+            own(grad_log_rate)[None],
+            own(grad_skip)[None],
+            jnp.zeros((1024 - 5 * HDIM - 3,), f32),
+        ]
+    )
+    step_own = jnp.where(y == 0, grad_step_pre[:, 0], grad_step_pre[:, 1])
+    small = jnp.stack(
+        [
+            gain_global_part,
+            grad_state_taps.reshape(1024),
+            head_row,
+            jnp.concatenate([step_own, jnp.zeros((512,), f32)]),
+        ]
+    )
+    sent = jnp.concatenate(
+        [
+            jnp.concatenate([hidden_rows, sums[:, 1024:]], axis=1),
+            jnp.pad(small, ((0, 4), (0, 256))),
+        ],
+        axis=0,
+    )
+    got = gather_rows(bf(sent), place).reshape(16, 40, 1280)
+    hidden_grad = got[:, :32, :1024].reshape(patches, 1024)
+    state_grad = got[:, :32, 1024:].reshape(patches, 256)
+    small = got[:, 32:36, :1024].astype(f32)
+    grad_gain_global = jnp.sum(small[:, 0], axis=0)
+    grad_conv_state = jnp.sum(small[:, 1], axis=0).reshape(4, 256)
+    mine = pick(small.reshape(2, 2, 4, 4, 1024), c).transpose(1, 0, 2, 3).reshape(8, 4, 1024)
+    grad_conv_input = mine[:, 2, : 4 * HDIM].reshape(8, 4, HDIM).transpose(1, 0, 2).reshape(4, 512)
+    grad_gain_mixer = mine[:, 2, 4 * HDIM : 5 * HDIM].reshape(512)
+    grad_step_bias = mine[:, 2, 5 * HDIM]
+    grad_decay_log = mine[:, 2, 5 * HDIM + 1]
+    grad_skip_gain = mine[:, 2, 5 * HDIM + 2]
+    normed_cols = lax.dynamic_slice_in_dim(normed, s * 128, 128, 1)
+    grad_mixer_step = product_right(normed_cols.T, bf(mine[:, 3, :512]))
+    grad_mixer_state = product_left(normed_cols, state_grad)
+    grad_patch_in = product_left(columns_in, hidden_grad)
+
+    head_cols = jnp.concatenate(
+        [
+            jnp.where(y == 0, grad_gate_low[:, :HDIM], grad_gate_low[:, HDIM:]),
+            jnp.where(y == 0, grad_input_low[:, :HDIM], grad_input_low[:, HDIM:]),
+        ],
+        axis=1,
+    )
+    grad_head_cols = bf(product_left(normed, head_cols)).reshape(8, 128, 128)
+    grad_head_cols = exchange_seq(grad_head_cols, s).transpose(1, 0, 2).astype(f32)
+    grad_mixer_gate = grad_head_cols[:, :, :HDIM].reshape(128, 512)
+    grad_mixer_input = grad_head_cols[:, :, HDIM:].reshape(128, 512)
+
+    back = bf(product_right(hidden_grad, patch_in)).reshape(32, 16, 256)
+    back = lax.all_to_all(back, ("seq", "mp"), 0, 0, tiled=True)
+    back = back.reshape(8, 4, 16, 256).transpose(2, 1, 0, 3).reshape(128, E)
+    grad_rows = bf(grad_residual + back)
+    grad_input = jnp.concatenate(select_blocks(gather_bytes(grad_rows), m, 4), axis=0)
+
+    sum_qkv, sum_rest = (sum_qkv.astype(f32), sum_rest.astype(f32))
+    return (
+        byte_output,
+        grad_input,
+        grad_gain_global,
+        grad_patch_in,
+        grad_mixer_gate,
+        grad_mixer_input,
+        grad_mixer_state,
+        grad_mixer_step,
+        grad_conv_input,
+        grad_conv_state,
+        grad_step_bias,
+        grad_decay_log,
+        grad_skip_gain,
+        grad_gain_mixer,
+        grad_mixer_out,
+        grad_patch_out,
+        grad_gain_attend,
+        sum_qkv[:, :256],
+        sum_qkv[:, 256:512],
+        sum_qkv[:, 512:],
+        sum_rest[:32],
+        grad_gain_feed,
+        sum_gate.astype(f32),
+        sum_up.astype(f32),
+        sum_rest[32:],
+    )
+
+
 def solution(mesh):
     in_specs = (
         P("seq", None),
@@ -533,4 +1026,5 @@
         P("seq", "mp"),
         P(("mp", "seq"), None),
     )
-    return jax.shard_map(shards, mesh=mesh, in_specs=in_specs, out_specs=out_specs, check_vma=False)
+    plan = split_plan if (mesh.shape["seq"], mesh.shape["mp"]) == (8, 4) else gathered_plan
+    return jax.shard_map(plan, mesh=mesh, in_specs=in_specs, out_specs=out_specs, check_vma=False)

time: 2350 us -> 752 us (0.32)
  waiting for transfers between devices: 1800 us -> 368 us
  blocking collectives: 260 us -> 0 us
  starting transfers between devices: 8.58 us -> 141 us
  matrix products: 135 us -> 73 us
  local copies, waits for them, and re-layouts: 47.2 us -> 71.1 us
    reduce_scatter x14 -> x4, waiting for transfers between devices: 1110 us -> 51.9 us  [the longest x1 51.9 us: split_plan(): lax.psum_scatter(bf(product_left(attend_in, grad_qkv)), 'seq', scatter_di...]
    all_gather x12 -> x3, waiting for transfers between devices: 411 us -> 8.67 us  [the longest x1 8.66 us: split_plan(): down = lax.all_gather(feed_down, 'seq', axis=0, tiled=True)]
    ppermute x4 -> x90, waiting for transfers between devices: 6.73 us -> 283 us  [the longest x45 154 us: swap_seq(): return lax.ppermute(shard, 'seq', [(i, i ^ by) for i in range(8)])]
    psum x7 -> x0, waiting for transfers between devices: 266 us -> none  [over_heads(): return lax.psum(partial_sum, 'mp')]
    all_gather x7 -> x0, blocking collectives: 212 us -> none  [the longest x1 33.7 us: fetch_local(): lax.all_gather(attend_value, 'seq', axis=0, tiled=True)]
    ppermute x4 -> x90, starting transfers between devices: 6.34 us -> 122 us  [the longest x45 93.9 us: swap_seq(): return lax.ppermute(shard, 'seq', [(i, i ^ by) for i in range(8)])]
    psum x3 -> x0, blocking collectives: 47.8 us -> none  [the longest x1 36.3 us: shards(): lax.psum((grad_gain_global, grad_conv_input, grad_conv_state, grad_step_b...]
    dot_general x18 -> x8, matrix products: 28.7 us -> 4.39 us  [the longest x3 1.67 us: block_attention(): jnp.einsum('bihd,bjhd->bhij', bf(q), bf(k), preferred_element_type=jnp.fl...]
  transfers between devices with their start and end apart: 37 -> 101, of which waited for: 32 -> 56; matrix products, arithmetic and copies ran while one was open for 4% -> 23% of each run, Pallas kernels for 0% -> 0%
where the time goes in v1:
time: 752 us; the launch traced here: 738 us
  waiting for transfers between devices  368 us (49%)
  starting transfers between devices  141 us (19%)
  matrix products  73 us (10%)
  local copies, waits for them, and re-layouts  71.1 us (9%)
  other arithmetic  63.1 us (8%)
  between operations  22 us (3%)
    ppermute x45, waiting for transfers between devices, swap_seq(): return lax.ppermute(shard, 'seq', [(i, i ^ by) for i in range(8)])  154 us
    ppermute x45, starting transfers between devices, swap_seq(): return lax.ppermute(shard, 'seq', [(i, i ^ by) for i in range(8)])  93.9 us
    ppermute x8, waiting for transfers between devices, swap_x(): return lax.ppermute(shard, 'seq', PAIR_X)  67.4 us
    reduce_scatter x1, waiting for transfers between devices, split_plan(): lax.psum_scatter(bf(product_left(attend_in, grad_qkv)), 'seq', scatter_di...  51.9 us
    ppermute x15, waiting for transfers between devices, swap_y(): return lax.ppermute(shard, 'mp', PAIR_Y)  50.1 us
    dot_general x17, matrix products, product(): return jnp.dot(former, latter, preferred_element_type=jnp.float32)  26.4 us
    dot_general x15, matrix products, product_right(): lax.dot_general(former, latter, (((1,), (1,)), ((), ())), preferred_eleme...  22.6 us
    unnamed x334, local copies, waits for them, and re-layouts  19.9 us
  transfers between devices with their start and end apart: 101, of which 56 were waited for; matrix products, arithmetic and copies ran while one was open for 23% of the time, Pallas kernels for 0%

profile of v1, /device:TPU:0, one launch (start us, length us, event | category | flops | bytes accessed | tf_op | source)
XLA Modules:
  0.0 738.1 jit_solution(18051607595098809715)
XLA Ops:
  7.3 3.0 collective-permute-start.11
  18.1 5.8 all-to-all-start
  30.7 4.7 collective-permute-start.13
  47.7 5.8 collective-permute-start.18
  55.3 3.3 collective-permute-done.15
  62.9 12.9 %collective-permute-done.1 = bf16[128,1024]{1,0:T(8,128)(2,1)S(1)} collective-permute-done((bf16[128,1024]{1,0:T(8,128)(2,1)S(1)}, bf16[128,1024]{1,0:T(8,128)(2,1)S(1)}, u32[]{:S(2)}, u32[]{:S(2)}) %collective-permute-start.1) | collective-permute-done | bytes 262176 | tf_op jit(solution)/shard_map/ppermute | solution.py:502
  78.7 2.9 collective-permute-start.4
  81.8 9.7 %collective-permute-done.2 = bf16[32,1024]{0,1:T(8,128)(2,1)} collective-permute-done((bf16[32,1024]{0,1:T(8,128)(2,1)S(1)}, bf16[32,1024]{0,1:T(8,128)(2,1)}, u32[]{:S(2)}, u32[]{:S(2)}) %collective-permute-start.2) | collective-permute-done | bytes 65568 | tf_op jit(solution)/shard_map/ppermute | solution.py:514
  91.5 12.7 %collective-permute-done.3 = bf16[32,1024]{0,1:T(8,128)(2,1)} collective-permute-done((bf16[32,1024]{0,1:T(8,128)(2,1)S(1)}, bf16[32,1024]{0,1:T(8,128)(2,1)}, u32[]{:S(2)}, u32[]{:S(2)}) %collective-permute-start.3) | collective-permute-done | bytes 65568 | tf_op jit(solution)/shard_map/ppermute | solution.py:514
  107.2 4.6 collective-permute-done.5
  113.8 4.9 collective-permute-start.7
  118.8 10.0 %collective-permute-done.6 = bf16[32,1024]{0,1:T(8,128)(2,1)S(1)} collective-permute-done((bf16[32,1024]{0,1:T(8,128)(2,1)S(1)}, bf16[32,1024]{0,1:T(8,128)(2,1)S(1)}, u32[]{:S(2)}, u32[]{:S(2)}) %collective-permute-start.6) | collective-permute-done | bytes 65568 | tf_op jit(solution)/shard_map/ppermute | solution.py:514
  128.9 26.6 %collective-permute-done.7 = bf16[32,1024]{0,1:T(8,128)(2,1)S(1)} collective-permute-done((bf16[32,1024]{0,1:T(8,128)(2,1)S(1)}, bf16[32,1024]{0,1:T(8,128)(2,1)S(1)}, u32[]{:S(2)}, u32[]{:S(2)}) %collective-permute-start.7) | collective-permute-done | bytes 65568 | tf_op jit(solution)/shard_map/ppermute | solution.py:514
  160.0 8.9 %collective-permute-done.9 = bf16[128,1024]{0,1:T(8,128)(2,1)S(1)} collective-permute-done((bf16[128,1024]{0,1:T(8,128)(2,1)S(1)}, bf16[128,1024]{0,1:T(8,128)(2,1)S(1)}, u32[]{:S(2)}, u32[]{:S(2)}) %collective-permute-start.9) | collective-permute-done | bytes 262176 | tf_op jit(solution)/shard_map/ppermute | solution.py:502
  190.6 7.3 collective-permute-done.23
  200.0 4.2 collective-permute-start.26
  204.4 9.8 %collective-permute-done.24 = bf16[32,1152]{0,1:T(8,128)(2,1)} collective-permute-done((bf16[32,1152]{0,1:T(8,128)(2,1)S(1)}, bf16[32,1152]{0,1:T(8,128)(2,1)}, u32[]{:S(2)}, u32[]{:S(2)}) %collective-permute-start.24) | collective-permute-done | bytes 73760 | tf_op jit(solution)/shard_map/ppermute | solution.py:514
  214.2 9.7 %collective-permute-done.25 = bf16[32,1152]{0,1:T(8,128)(2,1)} collective-permute-done((bf16[32,1152]{0,1:T(8,128)(2,1)S(1)}, bf16[32,1152]{0,1:T(8,128)(2,1)}, u32[]{:S(2)}, u32[]{:S(2)}) %collective-permute-start.25) | collective-permute-done | bytes 73760 | tf_op jit(solution)/shard_map/ppermute | solution.py:514
  227.7 4.8 collective-permute-start.28
  232.5 3.8 collective-permute-done.27
  236.4 15.3 %collective-permute-done.28 = bf16[32,1024]{0,1:T(8,128)(2,1)S(1)} collective-permute-done((bf16[32,1024]{0,1:T(8,128)(2,1)S(1)}, bf16[32,1024]{0,1:T(8,128)(2,1)S(1)}, u32[]{:S(2)}, u32[]{:S(2)}) %collective-permute-start.28) | collective-permute-done | bytes 65568 | tf_op jit(solution)/shard_map/ppermute | solution.py:514
  253.8 6.6 collective-permute-done.30
  264.0 3.8 all-to-all-start.1
  267.8 10.5 %all-to-all-done.1 = bf16[32,16,256]{2,1,0:T(8,128)(2,1)S(1)} async-done(((bf16[32,16,256]{2,1,0:T(8,128)(2,1)}), bf16[32,16,256]{2,1,0:T(8,128)(2,1)S(1)}, u32[]{:S(2)}, u32[]{:S(2)}) %all-to-all-start.1) | async-done | bytes 262176 | tf_op jit(solution)/shard_map/all_to_all | solution.py:764
  280.7 7.4 %collective-permute-done.33 = bf16[128,1024]{1,0:T(8,128)(2,1)S(1)} collective-permute-done((bf16[128,1024]{1,0:T(8,128)(2,1)S(1)}, bf16[128,1024]{1,0:T(8,128)(2,1)S(1)}, u32[]{:S(2)}, u32[]{:S(2)}) %collective-permute-start.33) | collective-permute-done | bytes 262176 | tf_op jit(solution)/shard_map/ppermute | solution.py:510
  303.4 7.4 %collective-permute-done.36 = bf16[128,1024]{1,0:T(8,128)(2,1)S(1)} collective-permute-done((bf16[128,1024]{1,0:T(8,128)(2,1)S(1)}, bf16[128,1024]{1,0:T(8,128)(2,1)S(1)}, u32[]{:S(2)}, u32[]{:S(2)}) %collective-permute-start.36) | collective-permute-done | bytes 262176 | tf_op jit(solution)/shard_map/ppermute | solution.py:510
  315.3 4.5 collective-permute-done.38
  319.8 8.7 %all-gather.8.cloned.1.call-done = bf16[1024,1024]{1,0:T(8,128)(2,1)} async-done(((bf16[128,1024]{1,0:T(8,128)(2,1)}), bf16[1024,1024]{1,0:T(8,128)(2,1)}) %all-gather.8.cloned.1.call-update) | async-done | bytes 2097168 | tf_op jit(solution)/shard_map/all_gather | solution.py:687
  328.4 3.2 fusion.109
  331.7 3.2 fusion.2
  334.9 5.3 multiply_convert_fusion.1
  341.2 3.8 convolution_convert_fusion
  345.2 3.3 fusion
  348.5 3.0 fusion.373
  359.8 3.8 convolution_convert_fusion.1
  368.8 4.6 collective-permute-done.41
  373.5 2.8 fusion.357
  377.2 7.0 collective-permute-done.48
  404.9 5.7 collective-permute-done.51
  415.9 3.2 all-to-all-start.2
  419.5 2.9 convolution_convert_fusion.2
  426.7 6.5 all-to-all-done.2
  441.3 2.9 collective-permute-start.86
  445.6 6.4 collective-permute-start.88
  453.8 3.5 collective-permute-done.85
  458.7 9.1 %collective-permute-done.53 = bf16[128,1024]{1,0:T(8,128)(2,1)S(1)} collective-permute-done((bf16[128,1024]{1,0:T(8,128)(2,1)S(1)}, bf16[128,1024]{1,0:T(8,128)(2,1)S(1)}, u32[]{:S(2)}, u32[]{:S(2)}) %collective-permute-start.53) | collective-permute-done | bytes 262176 | tf_op jit(solution)/shard_map/ppermute | solution.py:502
  469.7 2.7 collective-permute-start.56
  476.0 2.9 collective-permute-start.57
  479.0 4.3 collective-permute-done.57
  489.1 4.0 collective-permute-done.58
  493.2 4.6 collective-permute-done.59
  499.4 6.9 collective-permute-done.61
  512.9 51.9 %reduce-scatter.5.cloned.1.call-done = bf16[128,768]{1,0:T(8,128)(2,1)} async-done(((bf16[1024,768]{1,0:T(8,128)(2,1)}), bf16[128,768]{1,0:T(8,128)(2,1)}) %reduce-scatter.5.cloned.1.call-update) | async-done | bytes 196624 | tf_op jit(solution)/shard_map/reduce_scatter | solution.py:814
  593.8 3.4 collective-permute-start.79
  615.5 8.8 %collective-permute-done.64 = bf16[128,1280]{1,0:T(8,128)(2,1)S(1)} collective-permute-done((bf16[128,1280]{1,0:T(8,128)(2,1)S(1)}, bf16[128,1280]{1,0:T(8,128)(2,1)S(1)}, u32[]{:S(2)}, u32[]{:S(2)}) %collective-permute-start.64) | collective-permute-done | bytes 327712 | tf_op jit(solution)/shard_map/ppermute | solution.py:502
  626.3 2.7 collective-permute-start.66
  631.8 15.2 %collective-permute-done.65 = bf16[32,1280]{0,1:T(8,128)(2,1)S(1)} collective-permute-done((bf16[32,1280]{0,1:T(8,128)(2,1)}, bf16[32,1280]{0,1:T(8,128)(2,1)S(1)}, u32[]{:S(2)}, u32[]{:S(2)}) %collective-permute-start.65) | collective-permute-done | bytes 81952 | tf_op jit(solution)/shard_map/ppermute | solution.py:514
  647.0 14.2 %collective-permute-done.66 = bf16[32,1280]{0,1:T(8,128)(2,1)S(1)} collective-permute-done((bf16[32,1280]{0,1:T(8,128)(2,1)}, bf16[32,1280]{0,1:T(8,128)(2,1)S(1)}, u32[]{:S(2)}, u32[]{:S(2)}) %collective-permute-start.66) | collective-permute-done | bytes 81952 | tf_op jit(solution)/shard_map/ppermute | solution.py:514
  662.3 3.9 collective-permute-start.68
  666.3 7.2 collective-permute-start.69
  674.3 4.1 collective-permute-done.69
  680.2 7.0 collective-permute-done.71
  697.0 5.0 all-to-all-start.3
  705.6 7.0 all-to-all-done.3
  (824 shorter events, 260.4 us)
Async XLA Ops:
  7.3 166.8 %all-gather.4.cloned.1.call-start = ((), (), s32[]{:S(2)}) async-start(), calls=%async_computation.8 | async-start | bytes 2654208 | tf_op jit(solution)/shard_map/all_gather | solution.py:664
  18.1 29.1 %all-to-all-start = ((bf16[8,64,256]{2,1,0:T(8,128)(2,1)}), bf16[8,64,256]{2,1,0:T(8,128)(2,1)S(1)}, u32[]{:S(2)}, u32[]{:S(2)}) async-start(bf16[8,64,256]{2,1,0:T(8,128)(2,1)} %copy.439), calls=%async_computation | async-start | bytes 524288 | tf_op jit(solution)/shard_map/all_to_all | solution.py:702
  23.9 272.5 %all-gather.6.cloned.1.call-start = ((), (), s32[]{:S(2)}) async-start(), calls=%async_computation.9 | async-start | bytes 5308416 | tf_op jit(solution)/shard_map/all_gather | solution.py:681
  29.3 12.5 %collective-permute-start.12 = (f32[8,64]{1,0:T(8,128)S(1)}, f32[8,64]{1,0:T(8,128)S(1)}, u32[]{:S(2)}, u32[]{:S(2)}) collective-permute-start(f32[8,64]{1,0:T(8,128)S(1)} %concatenate.144), channel_id=1, source_target_pairs={{0,2},{1,3},{2,0},{3,1},{4,6},{5,7},{6,4},{7,5},{8,10},{9,11},{10,... | collective-permute-start | bytes 6152 | tf_op jit(solution)/shard_map/ppermute | solution.py:510
  30.7 16.9 %collective-permute-start.13 = (bf16[128,384]{1,0:T(8,128)(2,1)S(1)}, bf16[128,384]{1,0:T(8,128)(2,1)S(1)}, u32[]{:S(2)}, u32[]{:S(2)}) collective-permute-start(bf16[128,384]{1,0:T(8,128)(2,1)S(1)} %bitcast.925), channel_id=1, source_target_pairs={{0,28},{4,24},{8,20},{12,16},{16,12},{20,8},{24,4},{28,0},{1,29},{... | collective-permute-start | bytes 294920 | tf_op jit(solution)/shard_map/ppermute | solution.py:514
  35.6 17.9 %collective-permute-start.14 = (bf16[128,384]{1,0:T(8,128)(2,1)S(1)}, bf16[128,384]{1,0:T(8,128)(2,1)S(1)}, u32[]{:S(2)}, u32[]{:S(2)}) collective-permute-start(bf16[128,384]{1,0:T(8,128)(2,1)S(1)} %bitcast.924), channel_id=1, source_target_pairs={{0,24},{4,28},{8,16},{12,20},{16,8},{20,12},{24,0},{28,4},{1,25},{... | collective-permute-start | bytes 294920 | tf_op jit(solution)/shard_map/ppermute | solution.py:514
  36.4 22.3 %collective-permute-start.15 = (bf16[128,384]{1,0:T(8,128)(2,1)S(1)}, bf16[128,384]{1,0:T(8,128)(2,1)S(1)}, u32[]{:S(2)}, u32[]{:S(2)}) collective-permute-start(bf16[128,384]{1,0:T(8,128)(2,1)S(1)} %bitcast.923), channel_id=1, source_target_pairs={{0,20},{4,16},{8,28},{12,24},{16,4},{20,0},{24,12},{28,8},{1,21},{... | collective-permute-start | bytes 294920 | tf_op jit(solution)/shard_map/ppermute | solution.py:514
  37.1 21.9 %collective-permute-start.16 = (bf16[128,384]{1,0:T(8,128)(2,1)S(1)}, bf16[128,384]{1,0:T(8,128)(2,1)S(1)}, u32[]{:S(2)}, u32[]{:S(2)}) collective-permute-start(bf16[128,384]{1,0:T(8,128)(2,1)S(1)} %bitcast.922), channel_id=1, source_target_pairs={{0,16},{4,20},{8,24},{12,28},{16,0},{20,4},{24,8},{28,12},{1,17},{... | collective-permute-start | bytes 294920 | tf_op jit(solution)/shard_map/ppermute | solution.py:514
  41.8 17.2 %collective-permute-start.17 = (bf16[128,384]{1,0:T(8,128)(2,1)S(1)}, bf16[128,384]{1,0:T(8,128)(2,1)S(1)}, u32[]{:S(2)}, u32[]{:S(2)}) collective-permute-start(bf16[128,384]{1,0:T(8,128)(2,1)S(1)} %bitcast.928), channel_id=1, source_target_pairs={{0,12},{4,8},{8,4},{12,0},{16,28},{20,24},{24,20},{28,16},{1,13},{... | collective-permute-start | bytes 294920 | tf_op jit(solution)/shard_map/ppermute | solution.py:514
  47.7 12.1 %collective-permute-start.18 = (bf16[128,384]{1,0:T(8,128)(2,1)S(1)}, bf16[128,384]{1,0:T(8,128)(2,1)S(1)}, u32[]{:S(2)}, u32[]{:S(2)}) collective-permute-start(bf16[128,384]{1,0:T(8,128)(2,1)S(1)} %bitcast.927), channel_id=1, source_target_pairs={{0,8},{4,12},{8,0},{12,4},{16,24},{20,28},{24,16},{28,20},{1,9},{5... | collective-permute-start | bytes 294920 | tf_op jit(solution)/shard_map/ppermute | solution.py:514
  58.6 99.7 %collective-permute-start.21 = (bf16[64,1024]{1,0:T(8,128)(2,1)}, bf16[64,1024]{1,0:T(8,128)(2,1)}, u32[]{:S(2)}, u32[]{:S(2)}) collective-permute-start(bf16[64,1024]{1,0:T(8,128)(2,1)} %param.41), channel_id=1, source_target_pairs={{0,2},{1,3},{2,0},{3,1},{4,6},{5,7},{6,4},{7,5},{8,10},{9,11},{10,... | collective-permute-start | bytes 393224 | tf_op jit(solution)/shard_map/ppermute | solution.py:510
  61.2 14.5 %collective-permute-start.1 = (bf16[128,1024]{1,0:T(8,128)(2,1)S(1)}, bf16[128,1024]{1,0:T(8,128)(2,1)S(1)}, u32[]{:S(2)}, u32[]{:S(2)}) collective-permute-start(bf16[128,1024]{1,0:T(8,128)(2,1)S(1)} %fusion.91), channel_id=1, source_target_pairs={{0,4},{4,0},{8,12},{12,8},{16,20},{20,16},{24,28},{28,24},{1,5},{5... | collective-permute-start | bytes 786440 | tf_op jit(solution)/shard_map/ppermute | solution.py:502
  76.0 15.4 %collective-permute-start.2 = (bf16[32,1024]{0,1:T(8,128)(2,1)S(1)}, bf16[32,1024]{0,1:T(8,128)(2,1)}, u32[]{:S(2)}, u32[]{:S(2)}) collective-permute-start(bf16[32,1024]{0,1:T(8,128)(2,1)S(1)} %bitcast.914), channel_id=1, source_target_pairs={{0,8},{4,12},{8,0},{12,4},{16,24},{20,28},{24,16},{28,20},{1,9},{5... | collective-permute-start | bytes 196616 | tf_op jit(solution)/shard_map/ppermute | solution.py:514
  76.3 27.9 %collective-permute-start.3 = (bf16[32,1024]{0,1:T(8,128)(2,1)S(1)}, bf16[32,1024]{0,1:T(8,128)(2,1)}, u32[]{:S(2)}, u32[]{:S(2)}) collective-permute-start(bf16[32,1024]{0,1:T(8,128)(2,1)S(1)} %bitcast.915), channel_id=1, source_target_pairs={{0,16},{4,20},{8,24},{12,28},{16,0},{20,4},{24,8},{28,12},{1,17},{... | collective-permute-start | bytes 196616 | tf_op jit(solution)/shard_map/ppermute | solution.py:514
  78.7 25.5 %collective-permute-start.4 = (bf16[32,1024]{0,1:T(8,128)(2,1)}, bf16[32,1024]{0,1:T(8,128)(2,1)}, u32[]{:S(2)}, u32[]{:S(2)}) collective-permute-start(bf16[32,1024]{0,1:T(8,128)(2,1)} %bitcast.13), channel_id=1, source_target_pairs={{0,24},{4,28},{8,16},{12,20},{16,8},{20,12},{24,0},{28,4},{1,25},{... | collective-permute-start | bytes 196616 | tf_op jit(solution)/shard_map/ppermute | solution.py:514
  112.3 16.6 %collective-permute-start.6 = (bf16[32,1024]{0,1:T(8,128)(2,1)S(1)}, bf16[32,1024]{0,1:T(8,128)(2,1)S(1)}, u32[]{:S(2)}, u32[]{:S(2)}) collective-permute-start(bf16[32,1024]{0,1:T(8,128)(2,1)S(1)} %multiply_convert_fusion.8), channel_id=1, source_target_pairs={{0,24},{4,28},{8,16},{12,20},{16,8},{20,12},{24,0},{28,4},{1,25},{... | collective-permute-start | bytes 196616 | tf_op jit(solution)/shard_map/ppermute | solution.py:514
  113.8 41.7 %collective-permute-start.7 = (bf16[32,1024]{0,1:T(8,128)(2,1)S(1)}, bf16[32,1024]{0,1:T(8,128)(2,1)S(1)}, u32[]{:S(2)}, u32[]{:S(2)}) collective-permute-start(bf16[32,1024]{0,1:T(8,128)(2,1)S(1)} %multiply_convert_fusion.8), channel_id=1, source_target_pairs={{0,16},{4,20},{8,24},{12,28},{16,0},{20,4},{24,8},{28,12},{1,17},{... | collective-permute-start | bytes 196616 | tf_op jit(solution)/shard_map/ppermute | solution.py:514
  118.7 36.8 %collective-permute-start.8 = (bf16[32,1024]{0,1:T(8,128)(2,1)S(1)}, bf16[32,1024]{0,1:T(8,128)(2,1)S(1)}, u32[]{:S(2)}, u32[]{:S(2)}) collective-permute-start(bf16[32,1024]{0,1:T(8,128)(2,1)S(1)} %multiply_convert_fusion.8), channel_id=1, source_target_pairs={{0,8},{4,12},{8,0},{12,4},{16,24},{20,28},{24,16},{28,20},{1,9},{5... | collective-permute-start | bytes 196616 | tf_op jit(solution)/shard_map/ppermute | solution.py:514
  156.0 13.0 %collective-permute-start.9 = (bf16[128,1024]{0,1:T(8,128)(2,1)S(1)}, bf16[128,1024]{0,1:T(8,128)(2,1)S(1)}, u32[]{:S(2)}, u32[]{:S(2)}) collective-permute-start(bf16[128,1024]{0,1:T(8,128)(2,1)S(1)} %pad_maximum_fusion.28), channel_id=1, source_target_pairs={{0,4},{4,0},{8,12},{12,8},{16,20},{20,16},{24,28},{28,24},{1,5},{5... | collective-permute-start | bytes 786440 | tf_op jit(solution)/shard_map/ppermute | solution.py:502
  157.6 11.6 %collective-permute-start.20 = (bf16[1024,128]{1,0:T(8,128)(2,1)S(1)}, bf16[1024,128]{1,0:T(8,128)(2,1)S(1)}, u32[]{:S(2)}, u32[]{:S(2)}) collective-permute-start(bf16[1024,128]{1,0:T(8,128)(2,1)S(1)} %slice.561), channel_id=1, source_target_pairs={{0,2},{1,3},{2,0},{3,1},{4,6},{5,7},{6,4},{7,5},{8,10},{9,11},{10,... | collective-permute-start | bytes 786440 | tf_op jit(solution)/shard_map/ppermute | solution.py:510
  188.6 9.3 %collective-permute-start.23 = (bf16[128,1152]{1,0:T(8,128)(2,1)S(1)}, bf16[128,1152]{1,0:T(8,128)(2,1)S(1)}, u32[]{:S(2)}, u32[]{:S(2)}) collective-permute-start(bf16[128,1152]{1,0:T(8,128)(2,1)S(1)} %fusion.85), channel_id=1, source_target_pairs={{0,4},{4,0},{8,12},{12,8},{16,20},{20,16},{24,28},{28,24},{1,5},{5... | collective-permute-start | bytes 884744 | tf_op jit(solution)/shard_map/ppermute | solution.py:502
  198.6 15.6 %collective-permute-start.24 = (bf16[32,1152]{0,1:T(8,128)(2,1)S(1)}, bf16[32,1152]{0,1:T(8,128)(2,1)}, u32[]{:S(2)}, u32[]{:S(2)}) collective-permute-start(bf16[32,1152]{0,1:T(8,128)(2,1)S(1)} %copy.459), channel_id=1, source_target_pairs={{0,8},{4,12},{8,0},{12,4},{16,24},{20,28},{24,16},{28,20},{1,9},{5... | collective-permute-start | bytes 221192 | tf_op jit(solution)/shard_map/ppermute | solution.py:514
  198.9 25.0 %collective-permute-start.25 = (bf16[32,1152]{0,1:T(8,128)(2,1)S(1)}, bf16[32,1152]{0,1:T(8,128)(2,1)}, u32[]{:S(2)}, u32[]{:S(2)}) collective-permute-start(bf16[32,1152]{0,1:T(8,128)(2,1)S(1)} %copy.461), channel_id=1, source_target_pairs={{0,16},{4,20},{8,24},{12,28},{16,0},{20,4},{24,8},{28,12},{1,17},{... | collective-permute-start | bytes 221192 | tf_op jit(solution)/shard_map/ppermute | solution.py:514
  200.0 23.9 %collective-permute-start.26 = (bf16[32,1152]{0,1:T(8,128)(2,1)}, bf16[32,1152]{0,1:T(8,128)(2,1)}, u32[]{:S(2)}, u32[]{:S(2)}) collective-permute-start(bf16[32,1152]{0,1:T(8,128)(2,1)} %copy.462), channel_id=1, source_target_pairs={{0,24},{4,28},{8,16},{12,20},{16,8},{20,12},{24,0},{28,4},{1,25},{... | collective-permute-start | bytes 221192 | tf_op jit(solution)/shard_map/ppermute | solution.py:514
  225.3 11.1 %collective-permute-start.27 = (bf16[32,1024]{0,1:T(8,128)(2,1)S(1)}, bf16[32,1024]{0,1:T(8,128)(2,1)S(1)}, u32[]{:S(2)}, u32[]{:S(2)}) collective-permute-start(bf16[32,1024]{0,1:T(8,128)(2,1)S(1)} %add_convert_fusion.1), channel_id=1, source_target_pairs={{0,24},{4,28},{8,16},{12,20},{16,8},{20,12},{24,0},{28,4},{1,25},{... | collective-permute-start | bytes 196616 | tf_op jit(solution)/shard_map/ppermute | solution.py:514
  227.7 23.9 %collective-permute-start.28 = (bf16[32,1024]{0,1:T(8,128)(2,1)S(1)}, bf16[32,1024]{0,1:T(8,128)(2,1)S(1)}, u32[]{:S(2)}, u32[]{:S(2)}) collective-permute-start(bf16[32,1024]{0,1:T(8,128)(2,1)S(1)} %add_convert_fusion.1), channel_id=1, source_target_pairs={{0,16},{4,20},{8,24},{12,28},{16,0},{20,4},{24,8},{28,12},{1,17},{... | collective-permute-start | bytes 196616 | tf_op jit(solution)/shard_map/ppermute | solution.py:514
  232.5 19.1 %collective-permute-start.29 = (bf16[32,1024]{0,1:T(8,128)(2,1)S(1)}, bf16[32,1024]{0,1:T(8,128)(2,1)S(1)}, u32[]{:S(2)}, u32[]{:S(2)}) collective-permute-start(bf16[32,1024]{0,1:T(8,128)(2,1)S(1)} %add_convert_fusion.1), channel_id=1, source_target_pairs={{0,8},{4,12},{8,0},{12,4},{16,24},{20,28},{24,16},{28,20},{1,9},{5... | collective-permute-start | bytes 196616 | tf_op jit(solution)/shard_map/ppermute | solution.py:514
  264.0 14.4 %all-to-all-start.1 = ((bf16[32,16,256]{2,1,0:T(8,128)(2,1)}), bf16[32,16,256]{2,1,0:T(8,128)(2,1)S(1)}, u32[]{:S(2)}, u32[]{:S(2)}) async-start(bf16[32,16,256]{2,1,0:T(8,128)(2,1)} %bitcast.70), calls=%async_computation.1 | async-start | bytes 524288 | tf_op jit(solution)/shard_map/all_to_all | solution.py:764
  267.8 60.7 %all-gather.8.cloned.1.call-start = ((), (), s32[]{:S(2)}) async-start(), calls=%async_computation.10 | async-start | bytes 2359296 | tf_op jit(solution)/shard_map/all_gather | solution.py:687
  280.3 229.0 %reduce-scatter.11.cloned.1.call-start = ((), (), s32[]{:S(2)}) async-start(), calls=%async_computation.14 | async-start | bytes 2359296 | tf_op jit(solution)/shard_map/reduce_scatter | solution.py:793
  315.3 16.4 %collective-permute-start.37 = (bf16[128,1024]{1,0:T(8,128)(2,1)}, bf16[128,1024]{1,0:T(8,128)(2,1)}, u32[]{:S(2)}, u32[]{:S(2)}) collective-permute-start(bf16[128,1024]{1,0:T(8,128)(2,1)} %multiply_convert_fusion.5), channel_id=1, source_target_pairs={{0,1},{1,0},{2,3},{3,2},{4,5},{5,4},{6,7},{7,6},{8,9},{9,8},{10,11... | collective-permute-start | bytes 786440 | tf_op jit(solution)/shard_map/ppermute | solution.py:506
  319.8 11.9 %collective-permute-start.39 = (bf16[128,1024]{1,0:T(8,128)(2,1)}, bf16[128,1024]{1,0:T(8,128)(2,1)}, u32[]{:S(2)}, u32[]{:S(2)}) collective-permute-start(bf16[128,1024]{1,0:T(8,128)(2,1)} %collective-permute-done.38), channel_id=1, source_target_pairs={{0,1},{1,0},{2,3},{3,2},{4,5},{5,4},{6,7},{7,6},{8,9},{9,8},{10,11... | collective-permute-start | bytes 786440 | tf_op jit(solution)/shard_map/ppermute | solution.py:506
  345.0 166.1 %reduce-scatter.9.cloned.1.call-start = ((), (), s32[]{:S(2)}) async-start(), calls=%async_computation.13 | async-start | bytes 2359296 | tf_op jit(solution)/shard_map/reduce_scatter | solution.py:790
  358.3 9.1 %collective-permute-start.46 = (bf16[128,1024]{1,0:T(8,128)(2,1)}, bf16[128,1024]{1,0:T(8,128)(2,1)}, u32[]{:S(2)}, u32[]{:S(2)}) collective-permute-start(bf16[128,1024]{1,0:T(8,128)(2,1)} %fusion.54), channel_id=1, source_target_pairs={{0,2},{1,3},{2,0},{3,1},{4,6},{5,7},{6,4},{7,5},{8,10},{9,11},{10,... | collective-permute-start | bytes 786440 | tf_op jit(solution)/shard_map/ppermute | solution.py:510
  363.6 201.1 %reduce-scatter.5.cloned.1.call-start = ((), (), s32[]{:S(2)}) async-start(), calls=%async_computation.11 | async-start | bytes 1769472 | tf_op jit(solution)/shard_map/reduce_scatter | solution.py:814
  401.1 9.5 %collective-permute-start.51 = (bf16[128,1024]{1,0:T(8,128)(2,1)}, bf16[128,1024]{1,0:T(8,128)(2,1)}, u32[]{:S(2)}, u32[]{:S(2)}) collective-permute-start(bf16[128,1024]{1,0:T(8,128)(2,1)} %fusion.52), channel_id=1, source_target_pairs={{0,2},{1,3},{2,0},{3,1},{4,6},{5,7},{6,4},{7,5},{8,10},{9,11},{10,... | collective-permute-start | bytes 786440 | tf_op jit(solution)/shard_map/ppermute | solution.py:510
  404.2 18.5 %collective-permute-start.42 = (bf16[128,1024]{1,0:T(8,128)(2,1)}, bf16[128,1024]{1,0:T(8,128)(2,1)}, u32[]{:S(2)}, u32[]{:S(2)}) collective-permute-start(bf16[128,1024]{1,0:T(8,128)(2,1)} %get-tuple-element.358), channel_id=1, source_target_pairs={{0,2},{1,3},{2,0},{3,1},{4,6},{5,7},{6,4},{7,5},{8,10},{9,11},{10,... | collective-permute-start | bytes 786440 | tf_op jit(solution)/shard_map/ppermute | solution.py:510
  415.9 17.3 %all-to-all-start.2 = ((bf16[32,16,256]{2,1,0:T(8,128)(2,1)}), bf16[32,16,256]{2,1,0:T(8,128)(2,1)S(1)}, u32[]{:S(2)}, u32[]{:S(2)}) async-start(bf16[32,16,256]{2,1,0:T(8,128)(2,1)} %bitcast.103), calls=%async_computation.2 | async-start | bytes 524288 | tf_op jit(solution)/shard_map/all_to_all | solution.py:824
  419.0 271.6 %reduce-scatter.7.cloned.1.call-start = ((), (), s32[]{:S(2)}) async-start(), calls=%async_computation.12 | async-start | bytes 2949120 | tf_op jit(solution)/shard_map/reduce_scatter | solution.py:802
  422.4 11.4 %collective-permute-start.44 = (bf16[128,1024]{1,0:T(8,128)(2,1)S(1)}, bf16[128,1024]{1,0:T(8,128)(2,1)S(1)}, u32[]{:S(2)}, u32[]{:S(2)}) collective-permute-start(bf16[128,1024]{1,0:T(8,128)(2,1)S(1)} %copy-done.47), channel_id=1, source_target_pairs={{0,1},{1,0},{2,3},{3,2},{4,5},{5,4},{6,7},{7,6},{8,9},{9,8},{10,11... | collective-permute-start | bytes 786440 | tf_op jit(solution)/shard_map/ppermute | solution.py:506
  422.7 11.1 %collective-permute-start.43 = (bf16[128,1024]{1,0:T(8,128)(2,1)}, bf16[128,1024]{1,0:T(8,128)(2,1)S(1)}, u32[]{:S(2)}, u32[]{:S(2)}) collective-permute-start(bf16[128,1024]{1,0:T(8,128)(2,1)} %collective-permute-done.42), channel_id=1, source_target_pairs={{0,1},{1,0},{2,3},{3,2},{4,5},{5,4},{6,7},{7,6},{8,9},{9,8},{10,11... | collective-permute-start | bytes 786440 | tf_op jit(solution)/shard_map/ppermute | solution.py:506
  433.7 10.5 %collective-permute-start.52 = (bf16[256,1024]{1,0:T(8,128)(2,1)S(1)}, bf16[256,1024]{1,0:T(8,128)(2,1)S(1)}, u32[]{:S(2)}, u32[]{:S(2)}) collective-permute-start(bf16[256,1024]{1,0:T(8,128)(2,1)S(1)} %fusion.51), channel_id=1, source_target_pairs={{0,1},{1,0},{2,3},{3,2},{4,5},{5,4},{6,7},{7,6},{8,9},{9,8},{10,11... | collective-permute-start | bytes 1572872 | tf_op jit(solution)/shard_map/ppermute | solution.py:506
  436.5 9.1 %collective-permute-start.83 = (bf16[128,256]{1,0:T(8,128)(2,1)S(1)}, bf16[128,256]{1,0:T(8,128)(2,1)S(1)}, u32[]{:S(2)}, u32[]{:S(2)}) collective-permute-start(bf16[128,256]{1,0:T(8,128)(2,1)S(1)} %get-tuple-element.352), channel_id=1, source_target_pairs={{0,28},{4,24},{8,20},{12,16},{16,12},{20,8},{24,4},{28,0},{1,29},{... | collective-permute-start | bytes 196616 | tf_op jit(solution)/shard_map/ppermute | solution.py:514
  438.8 13.2 %collective-permute-start.84 = (bf16[128,256]{1,0:T(8,128)(2,1)S(1)}, bf16[128,256]{1,0:T(8,128)(2,1)S(1)}, u32[]{:S(2)}, u32[]{:S(2)}) collective-permute-start(bf16[128,256]{1,0:T(8,128)(2,1)S(1)} %get-tuple-element.351), channel_id=1, source_target_pairs={{0,24},{4,28},{8,16},{12,20},{16,8},{20,12},{24,0},{28,4},{1,25},{... | collective-permute-start | bytes 196616 | tf_op jit(solution)/shard_map/ppermute | solution.py:514
  441.3 16.0 %collective-permute-start.85 = (bf16[128,256]{1,0:T(8,128)(2,1)S(1)}, bf16[128,256]{1,0:T(8,128)(2,1)S(1)}, u32[]{:S(2)}, u32[]{:S(2)}) collective-permute-start(bf16[128,256]{1,0:T(8,128)(2,1)S(1)} %get-tuple-element.350), channel_id=1, source_target_pairs={{0,20},{4,16},{8,28},{12,24},{16,4},{20,0},{24,12},{28,8},{1,21},{... | collective-permute-start | bytes 196616 | tf_op jit(solution)/shard_map/ppermute | solution.py:514
  441.3 16.8 %collective-permute-start.86 = (bf16[128,256]{1,0:T(8,128)(2,1)S(1)}, bf16[128,256]{1,0:T(8,128)(2,1)S(1)}, u32[]{:S(2)}, u32[]{:S(2)}) collective-permute-start(bf16[128,256]{1,0:T(8,128)(2,1)S(1)} %get-tuple-element.349), channel_id=1, source_target_pairs={{0,16},{4,20},{8,24},{12,28},{16,0},{20,4},{24,8},{28,12},{1,17},{... | collective-permute-start | bytes 196616 | tf_op jit(solution)/shard_map/ppermute | solution.py:514
  444.3 13.9 %collective-permute-start.87 = (bf16[128,256]{1,0:T(8,128)(2,1)S(1)}, bf16[128,256]{1,0:T(8,128)(2,1)S(1)}, u32[]{:S(2)}, u32[]{:S(2)}) collective-permute-start(bf16[128,256]{1,0:T(8,128)(2,1)S(1)} %get-tuple-element.348), channel_id=1, source_target_pairs={{0,12},{4,8},{8,4},{12,0},{16,28},{20,24},{24,20},{28,16},{1,13},{... | collective-permute-start | bytes 196616 | tf_op jit(solution)/shard_map/ppermute | solution.py:514
  445.6 12.8 %collective-permute-start.88 = (bf16[128,256]{1,0:T(8,128)(2,1)S(1)}, bf16[128,256]{1,0:T(8,128)(2,1)S(1)}, u32[]{:S(2)}, u32[]{:S(2)}) collective-permute-start(bf16[128,256]{1,0:T(8,128)(2,1)S(1)} %get-tuple-element.347), channel_id=1, source_target_pairs={{0,8},{4,12},{8,0},{12,4},{16,24},{20,28},{24,16},{28,20},{1,9},{5... | collective-permute-start | bytes 196616 | tf_op jit(solution)/shard_map/ppermute | solution.py:514
  457.3 10.4 %collective-permute-start.53 = (bf16[128,1024]{1,0:T(8,128)(2,1)S(1)}, bf16[128,1024]{1,0:T(8,128)(2,1)S(1)}, u32[]{:S(2)}, u32[]{:S(2)}) collective-permute-start(bf16[128,1024]{1,0:T(8,128)(2,1)S(1)} %fusion.95), channel_id=1, source_target_pairs={{0,4},{4,0},{8,12},{12,8},{16,20},{20,16},{24,28},{28,24},{1,5},{5... | collective-permute-start | bytes 786440 | tf_op jit(solution)/shard_map/ppermute | solution.py:502
  486.6 11.2 %collective-permute-start.59 = (bf16[40,1152]{1,0:T(8,128)(2,1)S(1)}, bf16[40,1152]{1,0:T(8,128)(2,1)S(1)}, u32[]{:S(2)}, u32[]{:S(2)}) collective-permute-start(bf16[40,1152]{1,0:T(8,128)(2,1)S(1)} %fusion.176), channel_id=1, source_target_pairs={{0,16},{4,20},{8,24},{12,28},{16,0},{20,4},{24,8},{28,12},{1,17},{... | collective-permute-start | bytes 276488 | tf_op jit(solution)/shard_map/ppermute | solution.py:514
  486.6 11.2 %collective-permute-start.60 = (bf16[40,1152]{1,0:T(8,128)(2,1)S(1)}, bf16[40,1152]{1,0:T(8,128)(2,1)S(1)}, u32[]{:S(2)}, u32[]{:S(2)}) collective-permute-start(bf16[40,1152]{1,0:T(8,128)(2,1)S(1)} %fusion.176), channel_id=1, source_target_pairs={{0,8},{4,12},{8,0},{12,4},{16,24},{20,28},{24,16},{28,20},{1,9},{5... | collective-permute-start | bytes 276488 | tf_op jit(solution)/shard_map/ppermute | solution.py:514
  507.4 59.1 %collective-permute-start.62 = (bf16[320,1152]{1,0:T(8,128)(2,1)}, bf16[320,1152]{1,0:T(8,128)(2,1)}, u32[]{:S(2)}, u32[]{:S(2)}) collective-permute-start(bf16[320,1152]{1,0:T(8,128)(2,1)} %pad_maximum_fusion.15), channel_id=1, source_target_pairs={{0,1},{1,0},{2,3},{3,2},{4,5},{5,4},{6,7},{7,6},{8,9},{9,8},{10,11... | collective-permute-start | bytes 2211848 | tf_op jit(solution)/shard_map/ppermute | solution.py:506
  585.1 27.0 %collective-permute-start.63 = (bf16[256,1280]{1,0:T(8,128)(2,1)}, bf16[256,1280]{1,0:T(8,128)(2,1)}, u32[]{:S(2)}, u32[]{:S(2)}) collective-permute-start(bf16[256,1280]{1,0:T(8,128)(2,1)} %fusion.38), channel_id=1, source_target_pairs={{0,1},{1,0},{2,3},{3,2},{4,5},{5,4},{6,7},{7,6},{8,9},{9,8},{10,11... | collective-permute-start | bytes 1966088 | tf_op jit(solution)/shard_map/ppermute | solution.py:506
  592.6 9.7 %collective-permute-start.78 = (bf16[128,128]{1,0:T(8,128)(2,1)S(1)}, bf16[128,128]{1,0:T(8,128)(2,1)S(1)}, u32[]{:S(2)}, u32[]{:S(2)}) collective-permute-start(bf16[128,128]{1,0:T(8,128)(2,1)S(1)} %get-tuple-element.386), channel_id=1, source_target_pairs={{0,20},{4,16},{8,28},{12,24},{16,4},{20,0},{24,12},{28,8},{1,21},{... | collective-permute-start | bytes 98312 | tf_op jit(solution)/shard_map/ppermute | solution.py:514
  593.8 17.5 %collective-permute-start.79 = (bf16[128,128]{1,0:T(8,128)(2,1)}, bf16[128,128]{1,0:T(8,128)(2,1)S(1)}, u32[]{:S(2)}, u32[]{:S(2)}) collective-permute-start(bf16[128,128]{1,0:T(8,128)(2,1)} %get-tuple-element.385), channel_id=1, source_target_pairs={{0,16},{4,20},{8,24},{12,28},{16,0},{20,4},{24,8},{28,12},{1,17},{... | collective-permute-start | bytes 98312 | tf_op jit(solution)/shard_map/ppermute | solution.py:514
  597.2 14.1 %collective-permute-start.80 = (bf16[128,128]{1,0:T(8,128)(2,1)}, bf16[128,128]{1,0:T(8,128)(2,1)}, u32[]{:S(2)}, u32[]{:S(2)}) collective-permute-start(bf16[128,128]{1,0:T(8,128)(2,1)} %get-tuple-element.384), channel_id=1, source_target_pairs={{0,12},{4,8},{8,4},{12,0},{16,28},{20,24},{24,20},{28,16},{1,13},{... | collective-permute-start | bytes 98312 | tf_op jit(solution)/shard_map/ppermute | solution.py:514
  598.3 13.0 %collective-permute-start.81 = (bf16[128,128]{1,0:T(8,128)(2,1)}, bf16[128,128]{1,0:T(8,128)(2,1)}, u32[]{:S(2)}, u32[]{:S(2)}) collective-permute-start(bf16[128,128]{1,0:T(8,128)(2,1)} %get-tuple-element.383), channel_id=1, source_target_pairs={{0,8},{4,12},{8,0},{12,4},{16,24},{20,28},{24,16},{28,20},{1,9},{5... | collective-permute-start | bytes 98312 | tf_op jit(solution)/shard_map/ppermute | solution.py:514
  613.4 10.9 %collective-permute-start.64 = (bf16[128,1280]{1,0:T(8,128)(2,1)S(1)}, bf16[128,1280]{1,0:T(8,128)(2,1)S(1)}, u32[]{:S(2)}, u32[]{:S(2)}) collective-permute-start(bf16[128,1280]{1,0:T(8,128)(2,1)S(1)} %fusion.84), channel_id=1, source_target_pairs={{0,4},{4,0},{8,12},{12,8},{16,20},{20,16},{24,28},{28,24},{1,5},{5... | collective-permute-start | bytes 983048 | tf_op jit(solution)/shard_map/ppermute | solution.py:502
  625.4 21.6 %collective-permute-start.65 = (bf16[32,1280]{0,1:T(8,128)(2,1)}, bf16[32,1280]{0,1:T(8,128)(2,1)S(1)}, u32[]{:S(2)}, u32[]{:S(2)}) collective-permute-start(bf16[32,1280]{0,1:T(8,128)(2,1)} %bitcast.134), channel_id=1, source_target_pairs={{0,8},{4,12},{8,0},{12,4},{16,24},{20,28},{24,16},{28,20},{1,9},{5... | collective-permute-start | bytes 245768 | tf_op jit(solution)/shard_map/ppermute | solution.py:514
  626.3 34.9 %collective-permute-start.66 = (bf16[32,1280]{0,1:T(8,128)(2,1)}, bf16[32,1280]{0,1:T(8,128)(2,1)S(1)}, u32[]{:S(2)}, u32[]{:S(2)}) collective-permute-start(bf16[32,1280]{0,1:T(8,128)(2,1)} %bitcast.135), channel_id=1, source_target_pairs={{0,16},{4,20},{8,24},{12,28},{16,0},{20,4},{24,8},{28,12},{1,17},{... | collective-permute-start | bytes 245768 | tf_op jit(solution)/shard_map/ppermute | solution.py:514
  629.9 31.3 %collective-permute-start.67 = (bf16[32,1280]{0,1:T(8,128)(2,1)}, bf16[32,1280]{0,1:T(8,128)(2,1)S(1)}, u32[]{:S(2)}, u32[]{:S(2)}) collective-permute-start(bf16[32,1280]{0,1:T(8,128)(2,1)} %bitcast.136), channel_id=1, source_target_pairs={{0,24},{4,28},{8,16},{12,20},{16,8},{20,12},{24,0},{28,4},{1,25},{... | collective-permute-start | bytes 245768 | tf_op jit(solution)/shard_map/ppermute | solution.py:514
  662.3 11.9 %collective-permute-start.68 = (bf16[40,1280]{1,0:T(8,128)(2,1)S(1)}, bf16[40,1280]{1,0:T(8,128)(2,1)S(1)}, u32[]{:S(2)}, u32[]{:S(2)}) collective-permute-start(bf16[40,1280]{1,0:T(8,128)(2,1)S(1)} %pad_maximum_fusion.38), channel_id=1, source_target_pairs={{0,24},{4,28},{8,16},{12,20},{16,8},{20,12},{24,0},{28,4},{1,25},{... | collective-permute-start | bytes 307208 | tf_op jit(solution)/shard_map/ppermute | solution.py:514
  666.3 12.1 %collective-permute-start.69 = (bf16[40,1280]{1,0:T(8,128)(2,1)S(1)}, bf16[40,1280]{1,0:T(8,128)(2,1)S(1)}, u32[]{:S(2)}, u32[]{:S(2)}) collective-permute-start(bf16[40,1280]{1,0:T(8,128)(2,1)S(1)} %pad_maximum_fusion.38), channel_id=1, source_target_pairs={{0,16},{4,20},{8,24},{12,28},{16,0},{20,4},{24,8},{28,12},{1,17},{... | collective-permute-start | bytes 307208 | tf_op jit(solution)/shard_map/ppermute | solution.py:514
  697.0 15.6 %all-to-all-start.3 = ((bf16[32,16,256]{2,1,0:T(8,128)(2,1)}), bf16[32,16,256]{2,1,0:T(8,128)(2,1)}, u32[]{:S(2)}, u32[]{:S(2)}) async-start(bf16[32,16,256]{2,1,0:T(8,128)(2,1)} %bitcast.916), calls=%async_computation.3 | async-start | bytes 524288 | tf_op jit(solution)/shard_map/all_to_all | solution.py:938
  (194 other events, 1892.4 us)
Sparse Core Ops, SparseCore 0:
  15.9 87.1 all-gather.3
  105.8 101.2 all-gather.5
  280.4 47.9 all-gather.7
  345.1 66.1 reduce-scatter.10
  414.7 83.4 reduce-scatter.8
  501.4 63.3 reduce-scatter.4
  568.7 96.7 reduce-scatter.6

commit v2 on v0

--- a/solution.py
+++ b/solution.py
@@ -1,6 +1,10 @@
+from functools import partial
+
 import jax
 import jax.numpy as jnp
 from jax import lax
+from jax.experimental import pallas as pl
+from jax.experimental.pallas import tpu as pltpu
 from jax.sharding import PartitionSpec as P
 
 E = 1024
@@ -106,8 +110,20 @@
     return pullback(upstream)
 
 
+def running_bounds(lengths):
+    places = jnp.arange(lengths.shape[0])
+    upto = places[None, :] <= places[:-1, None]
+    return jnp.sum(jnp.where(upto, lengths[None, :], 0), axis=1)
+
+
+def running_sum(values):
+    places = jnp.arange(values.shape[0])
+    lower_part = (places[:, None] >= places[None, :]).astype(jnp.float32)
+    return jnp.dot(lower_part, values, precision=HIGH, preferred_element_type=jnp.float32)
+
+
 def segment_of(lengths, start_row, row_count):
-    bounds = jnp.cumsum(lengths)[:-1]
+    bounds = running_bounds(lengths)
     places = start_row + jnp.arange(row_count, dtype=jnp.int32)
     return jnp.sum((places[:, None] >= bounds[None, :]).astype(jnp.int32), axis=1)
 
@@ -137,7 +153,7 @@
     segment_prev,
 ):
     length = head_values.shape[0]
-    running = jnp.cumsum(-step_size * jnp.exp(log_rate), axis=0)
+    running = running_sum(-step_size * jnp.exp(log_rate))
     places = jnp.arange(length)
     allowed = (places[:, None] >= places[None, :]) & (
         segment_rows[:, None] == segment_rows[None, :]
@@ -157,7 +173,7 @@
 
 
 def block_summary(head_values, write_vecs, step_size, log_rate, segment_rows, segment_prev):
-    running = jnp.cumsum(-step_size * jnp.exp(log_rate), axis=0)
+    running = running_sum(-step_size * jnp.exp(log_rate))
     latest = running[-1]
     in_tail = (segment_rows == segment_rows[-1])[:, None]
     weights = jnp.where(in_tail, jnp.exp(latest[None, :] - running), 0.0) * step_size
@@ -192,7 +208,7 @@
     return jnp.concatenate([main_rows[:keep_count], main_rows[keep_count:] + tail_rows], axis=0)
 
 
-def shards(
+def gathered_plan(
     byte_input,
     seq_lengths,
     cotangent,
@@ -477,6 +493,1069 @@
     )
 
 
+ROWS = 512
+HALF = 256
+VMEM_BYTES = 56 * 1024 * 1024
+
+
+def bf(values):
+    return values.astype(jnp.bfloat16)
+
+
+def up(values):
+    return values.astype(jnp.float32)
+
+
+def whole(shape):
+    return pl.BlockSpec(shape, lambda *_: (0,) * len(shape))
+
+
+def scalars():
+    return pl.BlockSpec(memory_space=pltpu.SMEM)
+
+
+def kernel_params(count=1):
+    return pltpu.CompilerParams(
+        vmem_limit_bytes=VMEM_BYTES, dimension_semantics=("arbitrary",) * count
+    )
+
+
+def cost(flops, size):
+    return pl.CostEstimate(flops=flops, bytes_accessed=size, transcendentals=0)
+
+
+def block_index(place, k):
+    c, y = (place[0], place[1])
+    c = 1 - c if k >= 2 else c
+    y = 1 - y if k % 2 else y
+    return c * 2 + y
+
+
+def put_pieces(place, pieces, out_ref, rows=128):
+    for k, piece in enumerate(pieces):
+        at = pl.multiple_of(block_index(place, k) * rows, rows)
+        out_ref[pl.ds(at, rows), :] = piece[:rows, :]
+
+
+def lane_of(values, lane):
+    lanes = lax.broadcasted_iota(jnp.int32, values.shape, 1)
+    return jnp.sum(jnp.where(lanes == lane, values, 0.0), axis=1, keepdims=True)
+
+
+def segments(lengths, shift, shape, axis):
+    rows = lax.broadcasted_iota(jnp.int32, shape, axis) - shift
+    total = jnp.zeros(shape, jnp.int32)
+    bound = 0
+    for k in range(lengths.shape[0] - 1):
+        bound = bound + lengths[k]
+        total = total + (rows >= bound).astype(jnp.int32)
+    return total
+
+
+def tap_masks(lengths):
+    here = segments(lengths, 0, (ROWS, 1), 0)
+    rows = lax.broadcasted_iota(jnp.int32, (ROWS, 1), 0)
+    return [
+        up((rows >= j) & (segments(lengths, j, (ROWS, 1), 0) == here))
+        for j in range(1, KCONV)
+    ]
+
+
+def conv_rows(values, taps, masks):
+    total = values * taps[KCONV - 1 : KCONV, :]
+    for j in range(1, KCONV):
+        earlier = pltpu.roll(values, j, 0) * masks[j - 1]
+        total = total + earlier * taps[KCONV - 1 - j : KCONV - j, :]
+    return total
+
+
+def conv_back(values, taps, masks, grads):
+    rows_grad = grads * taps[KCONV - 1 : KCONV, :]
+    taps_grad = [None] * KCONV
+    taps_grad[KCONV - 1] = jnp.sum(grads * values, axis=0, keepdims=True)
+    for j in range(1, KCONV):
+        masked = grads * masks[j - 1]
+        rows_grad = rows_grad + pltpu.roll(masked, ROWS - j, 0) * taps[
+            KCONV - 1 - j : KCONV - j, :
+        ]
+        taps_grad[KCONV - 1 - j] = jnp.sum(
+            masked * pltpu.roll(values, j, 0), axis=0, keepdims=True
+        )
+    return rows_grad, taps_grad
+
+
+def silu_parts(values):
+    gate = 1.0 / (1.0 + jnp.exp(-values))
+    return values * gate, gate * (1.0 + values * (1.0 - gate))
+
+
+def softplus(values):
+    return jnp.maximum(values, 0.0) + jnp.log1p(jnp.exp(-jnp.abs(values)))
+
+
+def lower(shape, flip=False):
+    rows = lax.broadcasted_iota(jnp.int32, shape, 0)
+    columns = lax.broadcasted_iota(jnp.int32, shape, 1)
+    return up(rows <= columns) if flip else up(rows >= columns)
+
+
+def allowed_pairs(lengths):
+    rows = lax.broadcasted_iota(jnp.int32, (ROWS, ROWS), 0)
+    columns = lax.broadcasted_iota(jnp.int32, (ROWS, ROWS), 1)
+    same = segments(lengths, 0, (ROWS, 1), 0) == segments(lengths, 0, (1, ROWS), 1)
+    return (rows >= columns) & same
+
+
+def decay_block(run, run_row, r):
+    spread = run[r * HALF : (r + 1) * HALF, :] - run_row[:, : (r + 1) * HALF]
+    return jnp.exp(jnp.minimum(spread, 0.0))
+
+
+def head_columns(j, i, table):
+    return lane_of(table, 2 * j + i)
+
+
+def by_head(first, second):
+    lanes = lax.broadcasted_iota(jnp.int32, (1, 2 * HDIM), 1)
+    return jnp.where(lanes < HDIM, first, second)
+
+
+def shared_setup(
+    j, lengths, pre_ref, state_taps, params, affinity, step_ref, run_ref, run_t, wr_ref, mask_ref
+):
+    @pl.when(j == 0)
+    def _():
+        step = softplus(pre_ref[:, 1280:] + params[0:1, :])
+        step_ref[...] = step
+        running = jnp.dot(
+            lower((ROWS, ROWS)), -step * jnp.exp(params[1:2, :]), precision=HIGH,
+            preferred_element_type=jnp.float32,
+        )
+        run_ref[...] = running
+        run_t[...] = running.T
+        masks = [jnp.broadcast_to(mask, (ROWS, 128)) for mask in tap_masks(lengths)]
+        for k in range(KCONV - 1):
+            mask_ref[k] = masks[k]
+        masks = [jnp.concatenate([mask, mask], axis=1) for mask in masks]
+        state = silu_parts(conv_rows(pre_ref[:, 1024:1280], state_taps[...], masks))[0]
+        wr_ref[...] = bf(state)
+        pairs = product_right(bf(state[:, NSTATE:]), bf(state[:, :NSTATE]))
+        affinity[...] = jnp.where(allowed_pairs(lengths), pairs, 0.0)
+
+
+def start_weights(place, pieces, weights, arrived):
+    copies = []
+    for v, piece in enumerate(pieces):
+        at = pl.multiple_of(place[2 + v] * 128 + (64 if v == 8 else 0), 64)
+        target = weights.at[pl.ds(at, piece.shape[0]), :]
+        copies.append(pltpu.make_async_copy(piece, target, arrived.at[v]))
+    for copy in copies:
+        copy.start()
+    return copies
+
+
+def put_mix_out(weights, mix_out):
+    for s in range(8):
+        rows = slice(s * HDIM, (s + 1) * HDIM)
+        mix_out[rows, :512] = weights[s * 128 : s * 128 + 64, 1408:]
+        mix_out[rows, 512:] = weights[s * 128 + 64 : (s + 1) * 128, 1408:]
+
+
+def mixer_forward_kernel(
+    place, lengths, p0, p1, p2, p3, table, state_taps, params, w0, w1, w2, w3, w4, w5, w6, w7, w8,
+    send, keep, normed, pre, inside, scaled,
+    affinity, step_ref, run_ref, run_t, wr_ref, mask_ref, squares, mix_out,
+    weights, arrived,
+):
+    j = pl.program_id(0)
+
+    @pl.when(j == 0)
+    def _():
+        copies = start_weights(place, (w0, w1, w2, w3, w4, w5, w6, w7, w8), weights, arrived)
+        put_pieces(place, (p0, p1, p2, p3), normed)
+        for copy in copies:
+            copy.wait()
+        pre[...] = product(normed[...], weights[:, :1408])
+        put_mix_out(weights, mix_out)
+        squares[...] = jnp.zeros_like(squares)
+
+    shared_setup(j, lengths, pre, state_taps, params, affinity, step_ref, run_ref, run_t, wr_ref, mask_ref)
+    columns = pl.ds(pl.multiple_of(j * 128, 128), 128)
+    masks = [mask_ref[k] for k in range(KCONV - 1)]
+    values = silu_parts(
+        conv_rows(pre[:, pl.ds(pl.multiple_of(512 + j * 128, 128), 128)], table[:, columns], masks)
+    )[0]
+    step = by_head(*[head_columns(j, i, step_ref[...]) for i in range(2)])
+    steps = bf(values * step)
+    for i in range(2):
+        run = head_columns(j, i, run_ref[...])
+        run_row = run_t[pl.ds(2 * j + i, 1), :]
+        for r in range(2):
+            seen = (r + 1) * HALF
+            mixing = bf(
+                affinity[r * HALF : seen, :seen] * decay_block(run, run_row, r)
+            )
+            inner = product(mixing, steps[:seen, i * HDIM : (i + 1) * HDIM])
+            if i == 0:
+                inside[r * HALF : seen, columns] = jnp.concatenate([inner, inner], axis=1)
+            else:
+                kept = inside[r * HALF : seen, columns]
+                inside[r * HALF : seen, columns] = by_head(
+                    kept, jnp.concatenate([inner, inner], axis=1)
+                )
+    skip = by_head(*[head_columns(j, i, params[2:3, :]) for i in range(2)])
+    rows = inside[:, columns] + skip * values
+    gated = rows * silu_parts(pre[:, columns])[0]
+    scaled[:, columns] = bf(gated * table[4:5, columns])
+    squares[...] += jnp.broadcast_to(jnp.sum(gated * gated, axis=1, keepdims=True), (ROWS, 128))
+
+    @pl.when(j == 3)
+    def _():
+        for out, half in ((send, 1 - place[0]), (keep, place[0])):
+            at = pl.ds(pl.multiple_of(half * HALF, HALF), HALF)
+            out[:, :1024] = bf(product(scaled[at, :], mix_out[...]))
+            out[:, 1024:] = bf(squares[at, :])
+
+
+def mixer_forward(place, lengths, pieces, weights, table, state_taps, params):
+    f32, low = (jnp.float32, jnp.bfloat16)
+    shapes = [
+        ((HALF, 1152), low),
+        ((HALF, 1152), low),
+        ((ROWS, 1024), low),
+        ((ROWS, 1408), f32),
+        ((ROWS, 512), f32),
+        ((ROWS, 512), low),
+    ]
+    return pl.pallas_call(
+        mixer_forward_kernel,
+        grid=(4,),
+        in_specs=[scalars(), scalars()]
+        + [whole(a.shape) for a in (*pieces, table, state_taps, params)]
+        + [pl.BlockSpec(memory_space=pl.ANY)] * 9,
+        out_specs=[whole(s) for s, _ in shapes],
+        out_shape=[jax.ShapeDtypeStruct(s, t) for s, t in shapes],
+        scratch_shapes=[
+            pltpu.VMEM((ROWS, ROWS), f32),
+            pltpu.VMEM((ROWS, 128), f32),
+            pltpu.VMEM((ROWS, 128), f32),
+            pltpu.VMEM((128, ROWS), f32),
+            pltpu.VMEM((ROWS, 256), low),
+            pltpu.VMEM((KCONV - 1, ROWS, 128), f32),
+            pltpu.VMEM((ROWS, 128), f32),
+            pltpu.VMEM((512, 1024), low),
+            pltpu.VMEM((1024, 1920), low),
+            pltpu.SemaphoreType.DMA((9,)),
+        ],
+        compiler_params=kernel_params(),
+        cost_estimate=cost(14_000_000_000, 10_000_000),
+        name="mixer_forward",
+    )(place, lengths, *pieces, table, state_taps, params, *weights)
+
+
+def mixer_backward_kernel(
+    place, lengths, g0, g1, g2, g3, table, state_taps, params, pre, inside,
+    w0, w1, w2, w3, w4, w5, w6, w7, w8,
+    send, keep, grads, merged, table_grad, state_taps_grad, params_grad,
+    grad_mixed, kappa, affinity, step_ref, run_ref, run_t, wr_ref, mask_ref, pair_grad, run_grad, step_grad,
+    mix_out, weights, arrived,
+):
+    j = pl.program_id(0)
+    pieces = (w0, w1, w2, w3, w4, w5, w6, w7, w8)
+
+    @pl.when(j == 0)
+    def _():
+        for copy in start_weights(place, pieces, weights, arrived):
+            copy.wait()
+
+    shared_setup(j, lengths, pre, state_taps, params, affinity, step_ref, run_ref, run_t, wr_ref, mask_ref)
+
+    @pl.when(j == 0)
+    def _():
+        for k, piece in enumerate((g0, g1, g2, g3)):
+            at = pl.ds(pl.multiple_of(block_index(place, k) * 128, 128), 128)
+            merged[at, :] = piece[:128, :1024]
+            kappa[at, :] = up(piece[:128, 1024:])
+        put_mix_out(weights, mix_out)
+        grad_mixed[...] = product_right(merged[...], mix_out[...])
+        pair_grad[...] = jnp.zeros_like(pair_grad)
+        run_grad[...] = jnp.zeros_like(run_grad)
+        step_grad[...] = jnp.zeros_like(step_grad)
+        params_grad[...] = jnp.zeros_like(params_grad)
+        table_grad[...] = jnp.zeros_like(table_grad)
+        state_taps_grad[...] = jnp.zeros_like(state_taps_grad)
+
+    columns = pl.ds(pl.multiple_of(j * 128, 128), 128)
+    columns_in = pl.ds(pl.multiple_of(512 + j * 128, 128), 128)
+    masks = [mask_ref[k] for k in range(KCONV - 1)]
+    taps = table[:, columns]
+    before = pre[:, columns_in]
+    values, values_slope = silu_parts(conv_rows(before, taps, masks))
+    step = by_head(*[head_columns(j, i, step_ref[...]) for i in range(2)])
+    skip = by_head(*[head_columns(j, i, params[2:3, :]) for i in range(2)])
+    steps = bf(values * step)
+    gate, gate_slope = silu_parts(pre[:, columns])
+    within = inside[:, columns]
+    rows = within + skip * values
+    gated = rows * gate
+    mixed_grad = grad_mixed[:, columns]
+    gain_grad = jnp.sum(mixed_grad * gated, axis=0, keepdims=True)
+    gated_grad = mixed_grad * table[4:5, columns] - gated * kappa[...]
+    grads[:, columns] = bf(gated_grad * rows * gate_slope)
+    rows_grad = gated_grad * gate
+    rows_low = bf(rows_grad)
+    rows_turned = rows_low.T
+    steps_grads = []
+    for i in range(2):
+        run = head_columns(j, i, run_ref[...])
+        run_row = run_t[pl.ds(2 * j + i, 1), :]
+        lanes = slice(i * HDIM, (i + 1) * HDIM)
+        turned = jnp.zeros((HDIM, ROWS), jnp.float32)
+        for r in range(2):
+            seen = (r + 1) * HALF
+            block = slice(r * HALF, seen)
+            decay = decay_block(run, run_row, r)
+            mixing = bf(affinity[block, :seen] * decay)
+            mixing_grad = product_right(rows_low[block, lanes], steps[:seen, lanes])
+            pair_grad[block, :seen] += mixing_grad * decay
+            part = product(rows_turned[lanes, block], mixing)
+            if seen < ROWS:
+                part = jnp.concatenate(
+                    [part, jnp.zeros((HDIM, ROWS - seen), jnp.float32)], axis=1
+                )
+            turned = turned + part
+        steps_grads.append(turned)
+    steps_grad = jnp.concatenate(steps_grads, axis=0).T
+    lanes_in = lax.broadcasted_iota(jnp.int32, (128, 128), 0)
+    lanes_out = lax.broadcasted_iota(jnp.int32, (128, 128), 1)
+    to_head = up(lanes_out == 2 * j + lanes_in // HDIM)
+
+    def head_sums(columns_of):
+        return jnp.dot(columns_of, to_head, precision=HIGH, preferred_element_type=jnp.float32)
+
+    run_grad[...] += head_sums(up(rows_low) * within - up(steps) * steps_grad)
+    step_grad[...] += head_sums(steps_grad * values)
+    params_grad[2:3, :] += jnp.sum(head_sums(rows_grad * values), axis=0, keepdims=True)
+    conv_grad = (steps_grad * step + skip * rows_grad) * values_slope
+    before_grad, taps_grad = conv_back(before, taps, masks, conv_grad)
+    grads[:, columns_in] = bf(before_grad)
+    for k in range(KCONV):
+        table_grad[k : k + 1, columns] = taps_grad[k]
+    table_grad[4:5, columns] = gain_grad
+
+    @pl.when(j == 3)
+    def _():
+        decay_grad = jnp.dot(
+            lower((ROWS, ROWS), True), run_grad[...], precision=HIGH,
+            preferred_element_type=jnp.float32,
+        )
+        rate = jnp.exp(params[1:2, :])
+        step_total = step_grad[...] - decay_grad * rate
+        slope = 1.0 / (1.0 + jnp.exp(-(pre[:, 1280:] + params[0:1, :])))
+        lanes = lax.broadcasted_iota(jnp.int32, (1, 128), 1)
+        step_total = jnp.where(lanes < 8, step_total * slope, 0.0)
+        grads[:, 1280:] = bf(step_total)
+        params_grad[0:1, :] = jnp.sum(step_total, axis=0, keepdims=True)
+        params_grad[1:2, :] = jnp.sum(
+            -decay_grad * step_ref[...] * rate, axis=0, keepdims=True
+        )
+        pairs = jnp.where(allowed_pairs(lengths), pair_grad[...], 0.0)
+        read_grad = product(bf(pairs), wr_ref[:, :NSTATE])
+        write_grad = product(bf(pairs.T), wr_ref[:, NSTATE:])
+        wide = [jnp.concatenate([mask, mask], axis=1) for mask in masks]
+        state_before = pre[:, 1024:1280]
+        state_slope = silu_parts(conv_rows(state_before, state_taps[...], wide))[1]
+        state_grad, state_taps_parts = conv_back(
+            state_before,
+            state_taps[...],
+            wide,
+            jnp.concatenate([write_grad, read_grad], axis=1) * state_slope,
+        )
+        grads[:, 1024:1280] = bf(state_grad)
+        for k in range(KCONV):
+            state_taps_grad[k : k + 1, :] = state_taps_parts[k]
+        for out, half in ((send, 1 - place[0]), (keep, place[0])):
+            at = pl.ds(pl.multiple_of(half * HALF, HALF), HALF)
+            out[:, :1024] = bf(product_right(grads[at, :], weights[:, :1408]))
+            out[:, 1024:] = grads[at, 1024:1280]
+
+
+def mixer_backward(place, lengths, pieces, weights, table, state_taps, params, pre, inside):
+    f32, low = (jnp.float32, jnp.bfloat16)
+    shapes = [
+        ((HALF, 1280), low),
+        ((HALF, 1280), low),
+        ((ROWS, 1408), low),
+        ((ROWS, 1024), low),
+        ((8, 512), f32),
+        ((8, 256), f32),
+        ((8, 128), f32),
+    ]
+    operands = (*pieces, table, state_taps, params, pre, inside)
+    return pl.pallas_call(
+        mixer_backward_kernel,
+        grid=(4,),
+        in_specs=[scalars(), scalars()]
+        + [whole(a.shape) for a in operands]
+        + [pl.BlockSpec(memory_space=pl.ANY)] * 9,
+        out_specs=[whole(s) for s, _ in shapes],
+        out_shape=[jax.ShapeDtypeStruct(s, t) for s, t in shapes],
+        scratch_shapes=[
+            pltpu.VMEM((ROWS, 512), f32),
+            pltpu.VMEM((ROWS, 128), f32),
+            pltpu.VMEM((ROWS, ROWS), f32),
+            pltpu.VMEM((ROWS, 128), f32),
+            pltpu.VMEM((ROWS, 128), f32),
+            pltpu.VMEM((128, ROWS), f32),
+            pltpu.VMEM((ROWS, 256), low),
+            pltpu.VMEM((KCONV - 1, ROWS, 128), f32),
+            pltpu.VMEM((ROWS, ROWS), f32),
+            pltpu.VMEM((ROWS, 128), f32),
+            pltpu.VMEM((ROWS, 128), f32),
+            pltpu.VMEM((512, 1024), low),
+            pltpu.VMEM((1024, 1920), low),
+            pltpu.SemaphoreType.DMA((9,)),
+        ],
+        compiler_params=kernel_params(),
+        cost_estimate=cost(22_000_000_000, 14_000_000),
+        name="mixer_backward",
+    )(place, lengths, *operands, *weights)
+
+
+def patch_mask():
+    rows = lax.broadcasted_iota(jnp.int32, (128, 128), 0)
+    columns = lax.broadcasted_iota(jnp.int32, (128, 128), 1)
+    return (rows >= columns) & (rows // PATCH == columns // PATCH)
+
+
+def patch_probs(queries, keys, mask):
+    scores = product_right(queries, keys) * HDIM ** (-0.5)
+    scores = jnp.where(mask, scores, -1e30)
+    weights = jnp.exp(scores - jnp.max(scores, axis=1, keepdims=True))
+    return weights / jnp.sum(weights, axis=1, keepdims=True)
+
+
+def split_blocks(values, keep, send):
+    for k, out in ((0, keep), (1, send), (2, keep), (3, send)):
+        out[k // 2] = bf(values[k * 128 : (k + 1) * 128, :])
+
+
+def put_w_out(weights, w_out):
+    for s in range(8):
+        for q in range(4):
+            at = s * 128 + q * 32
+            w_out[s * 32 : (s + 1) * 32, q * 256 : (q + 1) * 256] = weights[at : at + 32, 768:]
+
+
+def attend_forward_kernel(
+    place, x0, x1, x2, x3, w0, w1, w2, w3, w4, w5, w6, w7, w8,
+    keep, send, rows, qkv, context, w_out, weights, arrived,
+):
+    for copy in start_weights(place, (w0, w1, w2, w3, w4, w5, w6, w7, w8), weights, arrived):
+        copy.wait()
+    put_w_out(weights, w_out)
+    for k, piece in enumerate((x0, x1, x2, x3)):
+        rows[k * 128 : (k + 1) * 128, :] = piece[...]
+    qkv[...] = bf(product(rows[...], weights[:, :768]))
+    mask = patch_mask()
+    for b in range(4):
+        at = slice(b * 128, (b + 1) * 128)
+        outs = []
+        for h in range(4):
+            q, k, v = (qkv[at, n * 256 + h * HDIM : n * 256 + (h + 1) * HDIM] for n in range(3))
+            outs.append(product(bf(patch_probs(q, k, mask)), v))
+        context[at, :] = bf(jnp.concatenate(outs, axis=1))
+    split_blocks(product(context[...], w_out[...]), keep, send)
+
+
+def attend_forward(place, pieces, weights):
+    low = jnp.bfloat16
+    shapes = [(2, 128, 1024), (2, 128, 1024), (ROWS, 1024), (ROWS, 768), (ROWS, 256)]
+    return pl.pallas_call(
+        attend_forward_kernel,
+        grid=(1,),
+        in_specs=[scalars()]
+        + [whole(a.shape) for a in pieces]
+        + [pl.BlockSpec(memory_space=pl.ANY)] * 9,
+        out_specs=[whole(s) for s in shapes],
+        out_shape=[jax.ShapeDtypeStruct(s, low) for s in shapes],
+        compiler_params=pltpu.CompilerParams(vmem_limit_bytes=VMEM_BYTES),
+        scratch_shapes=[
+            pltpu.VMEM((256, 1024), low),
+            pltpu.VMEM((1024, 1024), low),
+            pltpu.SemaphoreType.DMA((9,)),
+        ],
+        cost_estimate=cost(8_000_000_000, 7_000_000),
+        name="attend_forward",
+    )(place, *pieces, *weights)
+
+
+def attend_backward_kernel(
+    place, g0, g1, g2, g3, qkv, w0, w1, w2, w3, w4, w5, w6, w7, w8,
+    keep, send, rows, qkv_grad, w_out, weights, arrived,
+):
+    for copy in start_weights(place, (w0, w1, w2, w3, w4, w5, w6, w7, w8), weights, arrived):
+        copy.wait()
+    put_w_out(weights, w_out)
+    for k, piece in enumerate((g0, g1, g2, g3)):
+        rows[k * 128 : (k + 1) * 128, :] = piece[...]
+    context_grad = product_right(rows[...], w_out[...])
+    mask = patch_mask()
+    for b in range(4):
+        at = slice(b * 128, (b + 1) * 128)
+        outs = [[], [], []]
+        for h in range(4):
+            q, k, v = (qkv[at, n * 256 + h * HDIM : n * 256 + (h + 1) * HDIM] for n in range(3))
+            probs = patch_probs(q, k, mask)
+            grad = bf(context_grad[at, h * HDIM : (h + 1) * HDIM])
+            probs_grad = product_right(grad, v)
+            mean = jnp.sum(probs * probs_grad, axis=1, keepdims=True)
+            scores_grad = probs * (probs_grad - mean) * HDIM ** (-0.5)
+            outs[0].append(product(bf(scores_grad), k))
+            outs[1].append(product(bf(scores_grad.T), q))
+            outs[2].append(product(bf(probs.T), grad))
+        qkv_grad[at, :] = bf(jnp.concatenate(outs[0] + outs[1] + outs[2], axis=1))
+    split_blocks(product_right(qkv_grad[...], weights[:, :768]), keep, send)
+
+
+def attend_backward(place, pieces, qkv, weights):
+    low = jnp.bfloat16
+    shapes = [(2, 128, 1024), (2, 128, 1024), (ROWS, 1024), (ROWS, 768)]
+    return pl.pallas_call(
+        attend_backward_kernel,
+        grid=(1,),
+        in_specs=[scalars()]
+        + [whole(a.shape) for a in (*pieces, qkv)]
+        + [pl.BlockSpec(memory_space=pl.ANY)] * 9,
+        out_specs=[whole(s) for s in shapes],
+        out_shape=[jax.ShapeDtypeStruct(s, low) for s in shapes],
+        compiler_params=pltpu.CompilerParams(vmem_limit_bytes=VMEM_BYTES),
+        scratch_shapes=[
+            pltpu.VMEM((256, 1024), low),
+            pltpu.VMEM((1024, 1024), low),
+            pltpu.SemaphoreType.DMA((9,)),
+        ],
+        cost_estimate=cost(11_000_000_000, 7_000_000),
+        name="attend_backward",
+    )(place, *pieces, qkv, *weights)
+
+
+def feed_kernel(
+    place, x0, x1, x2, x3, out_grad, w0, w1, w2, w3, w4, w5, w6, w7, w8,
+    keep, send, out_keep, out_send, rows, hidden, gate_grad, up_grad,
+    weights, total, total_out, arrived,
+):
+    j = pl.program_id(0)
+
+    @pl.when(j == 0)
+    def _():
+        pieces = (w0, w1, w2, w3, w4, w5, w6, w7, w8)
+        copies = start_weights(place, pieces, weights, arrived)
+        for k, piece in enumerate((x0, x1, x2, x3)):
+            rows[k * 128 : (k + 1) * 128, :] = piece[...]
+        total[...] = jnp.zeros_like(total)
+        total_out[...] = jnp.zeros_like(total_out)
+        for copy in copies:
+            copy.wait()
+
+    chunk = pl.multiple_of(j * 256, 256)
+    w_gate = weights[:, pl.ds(chunk, 256)]
+    w_up = weights[:, pl.ds(pl.multiple_of(1024 + chunk, 256), 256)]
+    w_down = weights[pl.ds(chunk, 256), 2048:]
+    gate, slope = silu_parts(product(rows[...], w_gate))
+    lift = product(rows[...], w_up)
+    units = bf(gate * lift)
+    hidden[...] = units
+    units_grad = product_right(out_grad[...], w_down)
+    gate_low = bf(units_grad * lift * slope)
+    up_low = bf(units_grad * gate)
+    gate_grad[...] = gate_low
+    up_grad[...] = up_low
+    total[...] += product_right(gate_low, w_gate) + product_right(up_low, w_up)
+    total_out[...] += product(units, w_down)
+
+    @pl.when(j == pl.num_programs(0) - 1)
+    def _():
+        split_blocks(total, keep, send)
+        split_blocks(total_out, out_keep, out_send)
+
+
+def feed(place, pieces, out_grad, weights):
+    low = jnp.bfloat16
+    pair = (2, 128, 1024)
+    column = pl.BlockSpec((ROWS, 256), lambda j: (0, j))
+    return pl.pallas_call(
+        feed_kernel,
+        grid=(4,),
+        in_specs=[scalars()]
+        + [whole(a.shape) for a in (*pieces, out_grad)]
+        + [pl.BlockSpec(memory_space=pl.ANY)] * 9,
+        out_specs=[whole(pair)] * 4 + [whole((ROWS, 1024)), column, column, column],
+        out_shape=[jax.ShapeDtypeStruct(pair, low)] * 4
+        + [jax.ShapeDtypeStruct((ROWS, 1024), low)] * 4,
+        scratch_shapes=[
+            pltpu.VMEM((1024, 3072), low),
+            pltpu.VMEM((ROWS, 1024), jnp.float32),
+            pltpu.VMEM((ROWS, 1024), jnp.float32),
+            pltpu.SemaphoreType.DMA((9,)),
+        ],
+        compiler_params=kernel_params(),
+        cost_estimate=cost(14_000_000_000, 12_000_000),
+        name="feed",
+    )(place, *pieces, out_grad, *weights)
+
+
+def put_by_target(place, values, out):
+    for s in range(8):
+        out[place[11 + s], :, : values.shape[1]] = values[s * 128 : (s + 1) * 128, :]
+
+
+def feed_grads_kernel(place, rows, gate_grad, up_grad, hidden, out_grad, grads, turned):
+    j = pl.program_id(0)
+
+    @pl.when(j == 0)
+    def _():
+        turned[...] = rows[...].T
+
+    @pl.when(j == 4)
+    def _():
+        turned[...] = hidden[...].T
+
+    columns = pl.ds(pl.multiple_of((j % 2) * 512, 512), 512)
+    for first, right in ((0, gate_grad), (2, up_grad), (4, out_grad)):
+
+        @pl.when((j >= first) & (j < first + 2))
+        def _():
+            put_by_target(place, bf(product(turned[...], right[:, columns])), grads)
+
+
+def feed_grads(place, rows, gate_grad, up_grad, hidden, out_grad):
+    low = jnp.bfloat16
+    return pl.pallas_call(
+        feed_grads_kernel,
+        grid=(6,),
+        in_specs=[scalars()] + [whole((ROWS, 1024))] * 5,
+        out_specs=pl.BlockSpec((8, 128, 512), lambda j: (0, 0, j)),
+        out_shape=jax.ShapeDtypeStruct((8, 128, 3072), low),
+        scratch_shapes=[pltpu.VMEM((1024, ROWS), low)],
+        compiler_params=kernel_params(),
+        cost_estimate=cost(7_000_000_000, 11_000_000),
+        name="feed_grads",
+    )(place, rows, gate_grad, up_grad, hidden, out_grad)
+
+
+def attend_grads_kernel(place, rows, qkv_grad, context, middle_grad, grads):
+    put_by_target(place, bf(product(rows[...].T, qkv_grad[...])), grads)
+    out_grad = bf(product(context[...].T, middle_grad[...]))
+    for s in range(8):
+        for q in range(4):
+            grads[place[11 + s], q * 32 : (q + 1) * 32, 768:] = out_grad[
+                s * 32 : (s + 1) * 32, q * 256 : (q + 1) * 256
+            ]
+
+
+def attend_grads(place, rows, qkv_grad, context, middle_grad):
+    operands = (rows, qkv_grad, context, middle_grad)
+    return pl.pallas_call(
+        attend_grads_kernel,
+        grid=(1,),
+        in_specs=[scalars()] + [whole(a.shape) for a in operands],
+        out_specs=whole((8, 128, 1024)),
+        out_shape=jax.ShapeDtypeStruct((8, 128, 1024), jnp.bfloat16),
+        compiler_params=kernel_params(),
+        cost_estimate=cost(4_000_000_000, 6_000_000),
+        name="attend_grads",
+    )(place, *operands)
+
+
+def placed_kernel(turned, place, p0, p1, p2, p3, weights, rows, result):
+    put_pieces(place, (p0, p1, p2, p3), rows)
+    left = rows[:, :1024]
+    result[...] = bf(product_right(left, weights[...]) if turned else product(left, weights[...]))
+
+
+def placed_product(place, pieces, weights, turned):
+    width = pieces[0].shape[1]
+    low = jnp.bfloat16
+    return pl.pallas_call(
+        partial(placed_kernel, turned),
+        in_specs=[scalars()] + [whole(a.shape) for a in (*pieces, weights)],
+        out_specs=[whole((ROWS, width)), whole((ROWS, 256))],
+        grid=(1,),
+        out_shape=[
+            jax.ShapeDtypeStruct((ROWS, width), low),
+            jax.ShapeDtypeStruct((ROWS, 256), low),
+        ],
+        compiler_params=kernel_params(),
+        cost_estimate=cost(300_000_000, 3_000_000),
+        name="placed_product",
+    )(place, *pieces, weights)
+
+
+PAIR_C = [(i, i ^ 1) for i in range(4)]
+PAIR_Y = [(i, i ^ 2) for i in range(4)]
+
+
+def swap_c(shard):
+    return lax.ppermute(shard, "mp", PAIR_C)
+
+
+def swap_y(shard):
+    return lax.ppermute(shard, "mp", PAIR_Y)
+
+
+def swap_seq(shard, by):
+    return lax.ppermute(shard, "seq", [(i, i ^ by) for i in range(8)])
+
+
+RING = (0, 2, 4, 6, 7, 5, 3, 1)
+UP = [(RING[i], RING[(i + 1) % 8]) for i in range(8)]
+DOWN = [(b, a) for a, b in UP]
+REACH = (0, -1, 1, -2, 2, -3, 3, 4, 4)
+
+
+def swap_up(shard):
+    return lax.ppermute(shard, "seq", UP)
+
+
+def swap_down(shard):
+    return lax.ppermute(shard, "seq", DOWN)
+
+
+def chosen(index, values):
+    places = jnp.arange(len(values), dtype=jnp.int32)
+    return jnp.sum(jnp.where(index[..., None] == places, jnp.array(values, jnp.int32), 0), axis=-1)
+
+
+def places_of(c, y, s):
+    at = [RING.index(k) for k in range(8)]
+    own = chosen(s, at)
+    owners = chosen((own + jnp.array(REACH, jnp.int32) + 8) % 8, RING)
+    ahead = (jnp.array(at, jnp.int32) - own + 8) % 8
+    return jnp.concatenate([jnp.stack([c, y]), owners, ahead]).astype(jnp.int32)
+
+
+class RingGather:
+    def __init__(self, shard):
+        self.pieces = [shard]
+        self.flying = [shard, shard]
+
+    def step(self):
+        ahead, behind = self.flying
+        if len(self.pieces) == 7:
+            ahead, behind = (ahead[:64], behind[64:])
+        self.flying = [swap_up(ahead), swap_down(behind)]
+
+    def landed(self, value):
+        value, self.flying = lax.optimization_barrier((value, self.flying))
+        self.pieces = self.pieces + self.flying
+        return value
+
+
+class RingSum:
+    def __init__(self, blocks):
+        self.blocks = blocks
+        self.flying = None
+        self.count = 0
+
+    def step(self):
+        if self.count == 0:
+            far = self.blocks[4]
+            sent = [far[:64], far[64:]]
+        elif self.count == 1:
+            ahead, behind = (self.blocks[3], self.blocks[5])
+            sent = [
+                jnp.concatenate([bf(up(ahead[:64]) + up(self.flying[0])), ahead[64:]]),
+                jnp.concatenate([behind[:64], bf(up(behind[64:]) + up(self.flying[1]))]),
+            ]
+        else:
+            sent = [
+                bf(up(self.blocks[k]) + up(part))
+                for k, part in zip((4 - self.count, 4 + self.count), self.flying, strict=True)
+            ]
+        self.flying = [swap_up(sent[0]), swap_down(sent[1])]
+        self.count += 1
+
+    def landed(self, value):
+        value, self.flying = lax.optimization_barrier((value, self.flying))
+        return value
+
+    def result(self):
+        return up(self.blocks[0]) + up(self.flying[0]) + up(self.flying[1])
+
+
+def pick(stacked, index):
+    return lax.dynamic_index_in_dim(stacked, index, 0, keepdims=False)
+
+
+def over_seq(rows):
+    return lax.all_to_all(rows, "seq", 0, 0, tiled=True)
+
+
+def over_all(blocks):
+    return lax.all_to_all(blocks, ("seq", "mp"), 0, 0, tiled=True)
+
+
+def from_all_seq(rows):
+    return over_seq(jnp.broadcast_to(rows[None], (8, *rows.shape)))
+
+
+def sum_rows(send, keep, y):
+    total = up(keep) + up(swap_c(send))
+    parts = total.reshape(2, 128, -1)
+    return pick(parts, y) + up(swap_y(bf(pick(parts, 1 - y))))
+
+
+def gather_rows(rows):
+    far = swap_y(rows)
+    return [rows, far, swap_c(rows), swap_c(far)]
+
+
+def alike(parts):
+    return (parts[0] + parts[2]) + (parts[1] + parts[3])
+
+
+def sum_group(partial, c, y):
+    halves = bf(partial).reshape(2, HALF, -1)
+    return bf(sum_rows(pick(halves, 1 - c), pick(halves, c), y))
+
+
+def sum_seq(rows):
+    return jnp.sum(up(over_seq(rows.reshape(8, 16, -1))), axis=0)
+
+
+def gather_bytes(rows):
+    far = swap_y(rows)
+    return [rows, swap_c(rows), far, swap_c(far)]
+
+
+def sum_bytes(keep, send):
+    got = up(keep) + up(swap_c(send))
+    return got[0] + up(swap_y(bf(got[1])))
+
+
+def placed(parts, m):
+    blocks = jnp.stack(parts)
+    return jnp.concatenate([pick(blocks, m ^ k) for k in range(4)], axis=0)
+
+
+def to_bytes(columns):
+    got = over_all(columns.reshape(32, 16, 256))
+    return got.reshape(8, 4, 16, 256).transpose(2, 1, 0, 3).reshape(128, E)
+
+
+def to_columns(rows):
+    sent = rows.reshape(16, 4, 8, 256).transpose(2, 1, 0, 3).reshape(32, 16, 256)
+    return over_all(sent).reshape(ROWS, 256)
+
+
+def split_plan(
+    byte_input,
+    seq_lengths,
+    cotangent,
+    gain_global,
+    patch_in,
+    mixer_gate,
+    mixer_input,
+    mixer_state,
+    mixer_step,
+    conv_input,
+    conv_state,
+    step_bias,
+    decay_log,
+    skip_gain,
+    gain_mixer,
+    mixer_out,
+    patch_out,
+    gain_attend,
+    attend_query,
+    attend_key,
+    attend_value,
+    attend_out,
+    gain_feed,
+    feed_gate,
+    feed_up,
+    feed_down,
+):
+    s, m = (lax.axis_index("seq"), lax.axis_index("mp"))
+    y, c = (m // 2, m % 2)
+    place = places_of(c, y, s)
+    f32 = jnp.float32
+
+    out_halves = mixer_out.reshape(64, 2, 512).transpose(1, 0, 2).reshape(128, 512)
+    w_mixer = RingGather(jnp.concatenate(
+        [
+            mixer_gate,
+            mixer_input,
+            mixer_state,
+            mixer_step,
+            jnp.zeros((128, 120), jnp.bfloat16),
+            out_halves,
+        ],
+        axis=1,
+    ))
+    w_mixer.step()
+    out_quarters = attend_out.reshape(32, 4, 256).transpose(1, 0, 2).reshape(128, 256)
+    w_attend = RingGather(
+        jnp.concatenate([attend_query, attend_key, attend_value, out_quarters], axis=1)
+    )
+    w_feed = RingGather(jnp.concatenate([feed_gate, feed_up, feed_down], axis=1))
+    table = jnp.concatenate([conv_input, gain_mixer[None], jnp.zeros((3, 512), f32)], axis=0)
+    state_taps = jnp.concatenate([conv_state, jnp.zeros((4, 256), f32)], axis=0)
+    params = jnp.pad(jnp.stack([step_bias, decay_log, skip_gain]), ((0, 5), (0, 120)))
+
+    own_slots = lax.dynamic_slice_in_dim(byte_input.reshape(64, PATCH, E), 2 * m, 2, 1)
+    columns_in = over_seq(own_slots.reshape(64, 8, 256).transpose(1, 0, 2)).reshape(ROWS, 256)
+    columns_in = w_mixer.landed(columns_in)
+    w_mixer.step()
+    rows = sum_group(product(columns_in, patch_in), c, y)
+    hidden = w_mixer.landed(bf(sum_seq(rows)))
+    w_mixer.step()
+    hidden = w_mixer.landed(from_all_seq(hidden).reshape(128, 1024))
+    w_mixer.step()
+    hidden = up(hidden)
+    normed_parts = w_mixer.landed(gather_rows(bf(rms_scale(hidden, gain_global))))
+
+    w_attend.step()
+    w_feed.step()
+    send, keep, normed, pre, inside, scaled = mixer_forward(
+        place, seq_lengths, normed_parts, w_mixer.pieces, table, state_taps, params
+    )
+    w_patch = over_seq(patch_out.reshape(128, 8, 256).transpose(1, 0, 2))
+    send, w_patch = w_attend.landed((send, w_patch))
+    w_attend.step()
+    w_patch = w_patch.reshape(1024, 256)
+    sums = w_attend.landed(w_feed.landed(sum_rows(send, keep, y)))
+    w_attend.step()
+    w_feed.step()
+    unscaled, root = (sums[:, :1024], lax.rsqrt(sums[:, 1024:1025] / DI + EPS))
+    merged_parts = w_attend.landed(gather_rows(bf(hidden + root * unscaled)))
+    w_attend.step()
+    merged_low, slots = placed_product(place, merged_parts, w_patch, False)
+    slots = w_attend.landed(w_feed.landed(to_bytes(slots)))
+    w_feed.step()
+    residual = up(lax.dynamic_slice_in_dim(byte_input, m * 128, 128, 0)) + slots
+
+    attend_parts = gather_bytes(bf(rms_scale(residual, gain_attend)))
+    keep, send, attend_in, qkv, context = attend_forward(place, attend_parts, w_attend.pieces)
+    send = w_feed.landed(send)
+    w_feed.step()
+    middle = residual + sum_bytes(keep, send)
+    feed_parts = w_feed.landed(gather_bytes(bf(rms_scale(middle, gain_feed))))
+    cot_blocks = cotangent.reshape(4, 128, E)
+    cot_rows = pick(cot_blocks, m)
+    out_low = jnp.concatenate([bf(pick(cot_blocks, m ^ k)) for k in range(4)], axis=0)
+    keep, send, out_keep, out_send, feed_in, hidden_units, grad_gate, grad_up = feed(
+        place, feed_parts, out_low, w_feed.pieces
+    )
+    feed_sums = feed_grads(place, feed_in, grad_gate, grad_up, hidden_units, out_low)
+    grad_middle_part, gain_feed_part = rms_back(middle, gain_feed, sum_bytes(keep, send))
+    grad_middle = cot_rows + grad_middle_part
+    middle_parts, feed_sums = lax.optimization_barrier((gather_bytes(bf(grad_middle)), feed_sums))
+    feed_sums = RingSum(feed_sums)
+    feed_sums.step()
+    keep, send, middle_low, grad_qkv = attend_backward(place, middle_parts, qkv, w_attend.pieces)
+    send = feed_sums.landed(send)
+    feed_sums.step()
+    attend_sums = attend_grads(place, attend_in, grad_qkv, context, middle_low)
+    grad_attend_in, attend_sums = lax.optimization_barrier((sum_bytes(keep, send), attend_sums))
+    attend_sums = RingSum(attend_sums)
+    grad_attend_in = feed_sums.landed(grad_attend_in)
+    feed_sums.step()
+    grad_residual_part, gain_attend_part = rms_back(residual, gain_attend, grad_attend_in)
+    grad_residual = grad_middle + grad_residual_part
+
+    slot_grad, out_send = lax.optimization_barrier(
+        (to_columns(bf(grad_residual)), swap_c(out_send))
+    )
+    slot_grad = feed_sums.landed(slot_grad)
+    feed_sums.step()
+    grad_patch_out = bf(product_left(merged_low, slot_grad)).reshape(8, 128, 256)
+    rows = sum_group(product_right(slot_grad, w_patch), c, y)
+    out_parts = up(out_keep) + up(out_send)
+    rows, out_far = lax.optimization_barrier((rows, bf(out_parts[1])))
+    merged_rows, out_far = lax.optimization_barrier((sum_seq(rows), swap_y(out_far)))
+    out_rows = bf(middle + out_parts[0] + up(out_far))
+    merged_rows = feed_sums.landed(merged_rows)
+    attend_sums.step()
+    gains = jnp.stack([gain_feed_part, gain_attend_part])
+    got = from_all_seq(
+        bf(jnp.concatenate([merged_rows, gains, jnp.zeros((6, 1024), f32)], axis=0))
+    )
+    got, out_far, out_near = lax.optimization_barrier((got, swap_y(out_rows), swap_c(out_rows)))
+    got = attend_sums.landed(got)
+    attend_sums.step()
+    grad_merged = up(got[:, :16].reshape(128, 1024))
+    gains = jnp.sum(up(got[:, 16:18]), axis=0)
+    kappa = jnp.sum(grad_merged * unscaled, axis=1, keepdims=True) * root**3 / DI
+    rows = jnp.concatenate([grad_merged * root, jnp.broadcast_to(kappa, (128, 128))], axis=1)
+    merged_parts = gather_rows(
+        bf(jnp.concatenate([rows, jnp.pad(gains, ((0, 6), (0, 128)))], axis=0))
+    )
+    merged_parts = attend_sums.landed(merged_parts)
+    attend_sums.step()
+    out_both = swap_c(out_far)
+    grad_patch_out = over_seq(grad_patch_out)
+    gains = alike([up(part[128:130, :1024]) for part in merged_parts])
+    send, keep, grads, merged_grad, table_grad, state_taps_grad, params_grad = mixer_backward(
+        place,
+        seq_lengths,
+        merged_parts,
+        w_mixer.pieces,
+        table,
+        state_taps,
+        params,
+        pre,
+        inside,
+    )
+    send, grad_patch_out, out_both = attend_sums.landed((send, grad_patch_out, out_both))
+    attend_sums.step()
+    byte_output = placed([out_rows, out_near, out_far, out_both], m)
+    sums = attend_sums.landed(sum_rows(send, keep, y))
+    feed_sums, attend_sums = (feed_sums.result(), attend_sums.result())
+    grad_hidden_part, gain_global_part = rms_back(hidden, gain_global, sums[:, :1024])
+    rows = jnp.concatenate([grad_merged + grad_hidden_part, sums[:, 1024:]], axis=1)
+    small = jnp.stack([gain_global_part, state_taps_grad[:4].reshape(1024)])
+    hidden_parts = gather_rows(
+        bf(jnp.concatenate([rows, jnp.pad(small, ((0, 6), (0, 256)))], axis=0))
+    )
+    small = alike([up(part[128:130, :1024]) for part in hidden_parts])
+    hidden_rows, back = placed_product(place, hidden_parts, patch_in, True)
+    grad_input = placed(gather_bytes(bf(grad_residual + to_bytes(back))), m)
+
+    hidden_grad = hidden_rows[:, :1024]
+    normed_columns = lax.dynamic_slice_in_dim(normed, s * 128, 128, 1)
+    first_grad = product_left(normed_columns, grads)
+    own_scaled = lax.dynamic_slice_in_dim(scaled, s * HDIM, HDIM, 1)
+    return (
+        byte_output,
+        grad_input,
+        small[0],
+        product_left(columns_in, hidden_grad),
+        first_grad[:, :512],
+        first_grad[:, 512:1024],
+        product_left(normed_columns, hidden_rows[:, 1024:]),
+        first_grad[:, 1280:1288],
+        table_grad[:4],
+        small[1].reshape(4, 256),
+        params_grad[0, :8],
+        params_grad[1, :8],
+        params_grad[2, :8],
+        table_grad[4],
+        product_left(own_scaled, merged_grad),
+        grad_patch_out.transpose(1, 0, 2).reshape(128, 2048).astype(f32),
+        gains[1],
+        attend_sums[:, :256],
+        attend_sums[:, 256:512],
+        attend_sums[:, 512:768],
+        attend_sums[:, 768:].reshape(4, 32, 256).transpose(1, 0, 2).reshape(32, 1024),
+        gains[0],
+        feed_sums[:, :1024],
+        feed_sums[:, 1024:2048],
+        feed_sums[:, 2048:],
+    )
+
+
 def solution(mesh):
     in_specs = (
         P("seq", None),
@@ -533,4 +1612,5 @@
         P("seq", "mp"),
         P(("mp", "seq"), None),
     )
-    return jax.shard_map(shards, mesh=mesh, in_specs=in_specs, out_specs=out_specs, check_vma=False)
+    plan = split_plan if (mesh.shape["seq"], mesh.shape["mp"]) == (8, 4) else gathered_plan
+    return jax.shard_map(plan, mesh=mesh, in_specs=in_specs, out_specs=out_specs, check_vma=False)

time: 2350 us -> 533 us (0.23)
  waiting for transfers between devices: 1800 us -> 211 us
  blocking collectives: 260 us -> 0 us
  matrix products: 135 us -> 11.9 us
  starting transfers between devices: 8.58 us -> 125 us
  Pallas kernels: 0 us -> 101 us
  other arithmetic: 65.5 us -> 38.7 us
    reduce_scatter x14 -> x0, waiting for transfers between devices: 1110 us -> none  [the longest x1 153 us: shards(): lax.psum_scatter(grad_patch_out, 'seq', scatter_dimension=0, tiled=True)]
    all_gather x12 -> x0, waiting for transfers between devices: 411 us -> none  [the longest x1 76.6 us: fetch_global(): lax.all_gather(patch_in, 'seq', axis=0, tiled=True)]
    psum x7 -> x0, waiting for transfers between devices: 266 us -> none  [over_heads(): return lax.psum(partial_sum, 'mp')]
    all_gather x7 -> x0, blocking collectives: 212 us -> none  [the longest x1 33.7 us: fetch_local(): lax.all_gather(attend_value, 'seq', axis=0, tiled=True)]
    ppermute x4 -> x83, waiting for transfers between devices: 6.73 us -> 121 us  [the longest x17 65.8 us: swap_y(): return lax.ppermute(shard, 'mp', PAIR_Y)]
    pallas_call x0 -> x9, Pallas kernels: none -> 101 us  [the longest x1 24.6 us: mixer_backward(): pl.pallas_call(mixer_backward_kernel, grid=(4,), in_specs=[scalars(), sca...]
    all_to_all x0 -> x10, waiting for transfers between devices: none -> 90.5 us  [the longest x7 48.5 us: over_seq(): return lax.all_to_all(rows, 'seq', 0, 0, tiled=True)]
    ppermute x4 -> x83, starting transfers between devices: 6.34 us -> 83.9 us  [the longest x20 32.8 us: swap_down(): return lax.ppermute(shard, 'seq', DOWN)]
  transfers between devices with their start and end apart: 37 -> 93, of which waited for: 32 -> 40; matrix products, arithmetic and copies ran while one was open for 4% -> 12% of each run, Pallas kernels for 0% -> 15%
where the time goes in v2:
time: 533 us; the launch traced here: 529 us
  waiting for transfers between devices  211 us (40%)
  starting transfers between devices  125 us (23%)
  Pallas kernels  101 us (19%)
  local copies, waits for them, and re-layouts  38.9 us (7%)
  other arithmetic  38.7 us (7%)
  matrix products  11.9 us (2%)
    ppermute x17, waiting for transfers between devices, swap_y(): return lax.ppermute(shard, 'mp', PAIR_Y)  65.8 us
    all_to_all x7, waiting for transfers between devices, over_seq(): return lax.all_to_all(rows, 'seq', 0, 0, tiled=True)  48.5 us
    all_to_all x3, waiting for transfers between devices, over_all(): return lax.all_to_all(blocks, ('seq', 'mp'), 0, 0, tiled=True)  42 us
    ppermute x20, waiting for transfers between devices, swap_up(): return lax.ppermute(shard, 'seq', UP)  34 us
    ppermute x20, starting transfers between devices, swap_down(): return lax.ppermute(shard, 'seq', DOWN)  32.8 us
    all_to_all x7, starting transfers between devices, over_seq(): return lax.all_to_all(rows, 'seq', 0, 0, tiled=True)  29.8 us
    ppermute x20, starting transfers between devices, swap_up(): return lax.ppermute(shard, 'seq', UP)  26.3 us
    pallas_call x1, Pallas kernels, mixer_backward(): pl.pallas_call(mixer_backward_kernel, grid=(4,), in_specs=[scalars(), sca...  24.6 us
  transfers between devices with their start and end apart: 93, of which 40 were waited for; matrix products, arithmetic and copies ran while one was open for 12% of the time, Pallas kernels for 15%

profile of v2, /device:TPU:0, one launch (start us, length us, event | category | flops | bytes accessed | tf_op | source)
XLA Modules:
  0.0 528.8 jit_solution(11506411932983041822)
XLA Ops:
  3.5 3.1 collective-permute-start
  9.0 6.3 %all-to-all-start = ((bf16[8,64,256]{2,1,0:T(8,128)(2,1)}), bf16[8,64,256]{2,1,0:T(8,128)(2,1)S(1)}, u32[]{:S(2)}, u32[]{:S(2)}) async-start(bf16[8,64,256]{2,1,0:T(8,128)(2,1)} %copy.111), calls=%async_computation | async-start | bytes 524288 | tf_op jit(solution)/shard_map/all_to_all | solution.py:1292
  15.2 10.7 %all-to-all-done = bf16[8,64,256]{2,1,0:T(8,128)(2,1)S(1)} async-done(((bf16[8,64,256]{2,1,0:T(8,128)(2,1)}), bf16[8,64,256]{2,1,0:T(8,128)(2,1)S(1)}, u32[]{:S(2)}, u32[]{:S(2)}) %all-to-all-start) | async-done | bytes 262176 | tf_op jit(solution)/shard_map/all_to_all | solution.py:1292
  33.1 4.8 collective-permute-done.3
  38.7 3.7 all-to-all-start.1
  42.4 8.6 %all-to-all-done.1 = bf16[8,16,1024]{2,1,0:T(8,128)(2,1)S(1)} async-done(((bf16[8,16,1024]{2,1,0:T(8,128)(2,1)}), bf16[8,16,1024]{2,1,0:T(8,128)(2,1)S(1)}, u32[]{:S(2)}, u32[]{:S(2)}) %all-to-all-start.1) | async-done | bytes 262176 | tf_op jit(solution)/shard_map/all_to_all | solution.py:1292
  54.6 3.6 all-to-all-start.2
  58.3 2.1 collective-permute-start.13
  62.6 7.4 %all-to-all-done.2 = bf16[8,16,1024]{2,1,0:T(8,128)(2,1)S(1)} async-done(((bf16[8,16,1024]{2,1,0:T(8,128)(2,1)}), bf16[8,16,1024]{2,1,0:T(8,128)(2,1)S(1)}, u32[]{:S(2)}, u32[]{:S(2)}) %all-to-all-start.2) | async-done | bytes 262176 | tf_op jit(solution)/shard_map/all_to_all | solution.py:1292
  70.0 4.7 all-to-all-start.3
  75.0 2.1 collective-permute-start.8
  78.5 2.1 collective-permute-start.11
  83.5 4.6 collective-permute-done.11.w7
  88.1 2.5 collective-permute-start.14
  92.1 16.6 %mixer_forward.1 = (bf16[256,1152]{1,0:T(8,128)(2,1)}, bf16[256,1152]{1,0:T(8,128)(2,1)}, bf16[512,1024]{1,0:T(8,128)(2,1)}, f32[512,1408]{1,0:T(8,128)}, f32[512,512]{1,0:T(8,128)}, /*index=5*/bf16[512,512]{1,0:T(8,128)(2,1)}) custom-call(s32[19]{0:T(128)} %pad_add_fusion.place, s32[6]{0:T(128)} %lengths.3, bf16[128,1024]{1,0:T(8,128)(2,1)} %copy-done.27, ...), custom_call_target="tpu_custom_call" | custom-call | flops 14000000000 | bytes 10000000 | tf_op jit(solution)/shard_map/mixer_forward/pallas_call | solution.py:730
  115.2 5.3 %collective-permute-done.16 = bf16[128,1152]{1,0:T(8,128)(2,1)S(1)} collective-permute-done((bf16[128,1152]{1,0:T(8,128)(2,1)S(1)}, bf16[128,1152]{1,0:T(8,128)(2,1)S(1)}, u32[]{:S(2)}, u32[]{:S(2)}) %collective-permute-start.16) | collective-permute-done | bytes 294944 | tf_op jit(solution)/shard_map/ppermute | solution.py:1204
  120.6 8.9 %collective-permute-done.17.w1 = bf16[128,3072]{1,0:T(8,128)(2,1)} collective-permute-done((bf16[128,3072]{1,0:T(8,128)(2,1)S(1)}, bf16[128,3072]{1,0:T(8,128)(2,1)}, u32[]{:S(2)}, u32[]{:S(2)}) %collective-permute-start.17) | collective-permute-done | bytes 786464 | tf_op jit(solution)/shard_map/ppermute | solution.py:1218
  129.6 5.0 collective-permute-done.19.w3
  135.0 2.0 collective-permute-start.21
  139.0 4.3 collective-permute-done.21.p1
  144.8 12.7 %collective-permute-start.27 = (bf16[128,3072]{1,0:T(8,128)(2,1)}, bf16[128,3072]{1,0:T(8,128)(2,1)}, u32[]{:S(2)}, u32[]{:S(2)}) collective-permute-start(bf16[128,3072]{1,0:T(8,128)(2,1)} %collective-permute-done.18.w2), channel_id=1, source_target_pairs={{8,0},{16,8},{24,16},{28,24},{20,28},{12,20},{4,12},{0,4},{9,1},{1... | collective-permute-start | bytes 2359304 | tf_op jit(solution)/shard_map/ppermute | solution.py:1222
  158.3 2.6 placed_product.2
  161.0 4.0 all-to-all-start.4
  167.1 16.9 %all-to-all-done.4 = bf16[32,16,256]{2,1,0:T(8,128)(2,1)S(1)} async-done(((bf16[32,16,256]{2,1,0:T(8,128)(2,1)}), bf16[32,16,256]{2,1,0:T(8,128)(2,1)S(1)}, u32[]{:S(2)}, u32[]{:S(2)}) %all-to-all-start.4) | async-done | bytes 262176 | tf_op jit(solution)/shard_map/all_to_all | solution.py:1296
  186.5 6.4 %collective-permute-done.31.x2 = bf16[128,1024]{1,0:T(8,128)(2,1)S(1)} collective-permute-done((bf16[128,1024]{1,0:T(8,128)(2,1)S(1)}, bf16[128,1024]{1,0:T(8,128)(2,1)S(1)}, u32[]{:S(2)}, u32[]{:S(2)}) %collective-permute-start.31) | collective-permute-done | bytes 262176 | tf_op jit(solution)/shard_map/ppermute | solution.py:1204
  196.4 10.3 %attend_forward.1 = (bf16[2,128,1024]{2,1,0:T(8,128)(2,1)}, bf16[2,128,1024]{2,1,0:T(8,128)(2,1)}, bf16[512,1024]{1,0:T(8,128)(2,1)}, bf16[512,768]{1,0:T(8,128)(2,1)}, bf16[512,256]{1,0:T(8,128)(2,1)}) custom-call(s32[19]{0:T(128)} %pad_add_fusion.place, bf16[128,1024]{1,0:T(8,128)(2,1)} %copy-done.33, bf16[128,1024]{1,0:T(8,128)(2,1)} %copy-done.85, ...), custom_call_target="tpu_custom_call" | custom-call | flops 8000000000 | bytes 7000000 | tf_op jit(solution)/shard_map/attend_forward/pallas_call | solution.py:974
  206.7 6.4 %collective-permute-done.33.w5 = bf16[128,3072]{1,0:T(8,128)(2,1)S(1)} collective-permute-done((bf16[128,3072]{1,0:T(8,128)(2,1)}, bf16[128,3072]{1,0:T(8,128)(2,1)S(1)}, u32[]{:S(2)}, u32[]{:S(2)}) %collective-permute-start.33) | collective-permute-done | bytes 786464 | tf_op jit(solution)/shard_map/ppermute | solution.py:1218
  214.7 2.1 collective-permute-done.35
  219.9 6.6 %collective-permute-done.36 = bf16[128,1024]{1,0:T(8,128)(2,1)S(1)} collective-permute-done((bf16[128,1024]{1,0:T(8,128)(2,1)S(1)}, bf16[128,1024]{1,0:T(8,128)(2,1)S(1)}, u32[]{:S(2)}, u32[]{:S(2)}) %collective-permute-start.36) | collective-permute-done | bytes 262176 | tf_op jit(solution)/shard_map/ppermute | solution.py:1204
  232.8 2.5 collective-permute-done.38.x2
  238.1 2.3 collective-permute-done.40.w7
  242.7 16.3 %feed.1 = (bf16[2,128,1024]{2,1,0:T(8,128)(2,1)}, bf16[2,128,1024]{2,1,0:T(8,128)(2,1)}, bf16[2,128,1024]{2,1,0:T(8,128)(2,1)}, bf16[2,128,1024]{2,1,0:T(8,128)(...) custom-call(s32[19]{0:T(128)} %pad_add_fusion.place, ...), custom_call_target="tpu_custom_call" | custom-call | flops 14000000000 | bytes 12000000 | tf_op jit(solution)/shard_map/feed/pallas_call | solution.py:1087
  259.1 2.1 collective-permute-done.42
  263.5 7.3 %collective-permute-done.43 = bf16[128,1024]{1,0:T(8,128)(2,1)S(1)} collective-permute-done((bf16[128,1024]{1,0:T(8,128)(2,1)S(1)}, bf16[128,1024]{1,0:T(8,128)(2,1)S(1)}, u32[]{:S(2)}, u32[]{:S(2)}) %collective-permute-start.43) | collective-permute-done | bytes 262176 | tf_op jit(solution)/shard_map/ppermute | solution.py:1204
  273.9 6.0 %collective-permute-done.45.g2 = bf16[128,1024]{1,0:T(8,128)(2,1)S(1)} collective-permute-done((bf16[128,1024]{1,0:T(8,128)(2,1)S(1)}, bf16[128,1024]{1,0:T(8,128)(2,1)S(1)}, u32[]{:S(2)}, u32[]{:S(2)}) %collective-permute-start.45) | collective-permute-done | bytes 262176 | tf_op jit(solution)/shard_map/ppermute | solution.py:1204
  279.9 9.5 %feed_grads.1 = bf16[8,128,3072]{2,1,0:T(8,128)(2,1)} custom-call(s32[19]{0:T(128)} %pad_add_fusion.place, bf16[512,1024]{1,0:T(8,128)(2,1)} %get-tuple-element.204.rows, bf16[512,1024]{1,0:T(8,128)(2,1)} %get-tuple-element.205.gate_grad, bf16[512,1024]{1,0:T(8,128)(2,1)} %get-tuple-element.206.up_grad, bf16[512,1024]{1,0:T(8,128)(2,1)} %get-tuple-element.207.hidden, ...), custom_call_target="tpu_custom_call" | custom-call | flops 7000000000 | bytes 11000000 | tf_op jit(solution)/shard_map/feed_grads/pallas_call | solution.py:1134
  293.1 13.4 %attend_backward.1 = (bf16[2,128,1024]{2,1,0:T(8,128)(2,1)}, bf16[2,128,1024]{2,1,0:T(8,128)(2,1)}, bf16[512,1024]{1,0:T(8,128)(2,1)}, bf16[512,768]{1,0:T(8,128)(2,1)}) custom-call(s32[19]{0:T(128)} %pad_add_fusion.place, bf16[128,1024]{1,0:T(8,128)(2,1)} %copy-done.42, bf16[128,1024]{1,0:T(8,128)(2,1)} %copy-done.80, bf16[128,1024]{1,0:T(8,128)(2,1)} %copy-done.78, ...), custom_call_target="tpu_custom_call" | custom-call | flops 11000000512 | bytes 7000000 | tf_op jit(solution)/shard_map/attend_backward/pallas_call | solution.py:1024
  312.0 4.7 attend_grads.1
  316.7 2.4 collective-permute-done.50
  319.2 8.9 %collective-permute-done.52 = bf16[128,3072]{1,0:T(8,128)(2,1)S(1)} collective-permute-done((bf16[128,3072]{1,0:T(8,128)(2,1)S(1)}, bf16[128,3072]{1,0:T(8,128)(2,1)S(1)}, u32[]{:S(2)}, u32[]{:S(2)}) %collective-permute-start.52) | collective-permute-done | bytes 786464 | tf_op jit(solution)/shard_map/ppermute | solution.py:1222
  330.0 3.1 fusion.3
  337.4 2.8 all-to-all-start.5
  340.2 17.8 %all-to-all-done.5 = bf16[32,16,256]{2,1,0:T(8,128)(2,1)S(1)} async-done(((bf16[32,16,256]{2,1,0:T(8,128)(2,1)}), bf16[32,16,256]{2,1,0:T(8,128)(2,1)S(1)}, u32[]{:S(2)}, u32[]{:S(2)}) %all-to-all-start.5) | async-done | bytes 262176 | tf_op jit(solution)/shard_map/all_to_all | solution.py:1296
  364.0 3.6 fusion.1
  372.3 3.9 all-to-all-start.6
  378.2 2.0 collective-permute-start.63
  381.4 2.5 convolution_convert_fusion.2
  383.9 11.1 %all-to-all-done.6 = bf16[8,16,1024]{2,1,0:T(8,128)(2,1)S(1)} async-done(((bf16[8,16,1024]{2,1,0:T(8,128)(2,1)}), bf16[8,16,1024]{2,1,0:T(8,128)(2,1)S(1)}, u32[]{:S(2)}, u32[]{:S(2)}) %all-to-all-start.6) | async-done | bytes 262176 | tf_op jit(solution)/shard_map/all_to_all | solution.py:1292
  397.1 4.1 all-to-all-start.7
  403.1 10.7 %all-to-all-done.7 = bf16[8,24,1024]{2,1,0:T(8,128)(2,1)} async-done(((bf16[8,24,1024]{2,1,0:T(8,128)(2,1)}), bf16[8,24,1024]{2,1,0:T(8,128)(2,1)}, u32[]{:S(2)}, u32[]{:S(2)}) %all-to-all-start.7) | async-done | bytes 393248 | tf_op jit(solution)/shard_map/all_to_all | solution.py:1292
  413.8 3.6 all-to-all-start.8
  422.4 2.1 collective-permute-start.69
  424.5 4.8 collective-permute-done.65.g1
  432.5 2.0 collective-permute-done.69
  434.5 3.5 collective-permute-done.68
  441.7 24.6 %mixer_backward.1 = (bf16[256,1280]{1,0:T(8,128)(2,1)}, bf16[256,1280]{1,0:T(8,128)(2,1)}, bf16[512,1408]{1,0:T(8,128)(2,1)}, bf16[512,1024]{1,0:T(8,128)(2,1)},...) custom-call(s32[19]{0:T(128)} %pad_add_fusion.place, s32[6]{0:T(128)} %lengths.3, ...), custom_call_target="tpu_custom_call" | custom-call | flops 22000001024 | bytes 14000000 | tf_op jit(solution)/shard_map/mixer_backward/pallas_call | solution.py:895
  476.0 5.0 collective-permute-done.74
  488.6 2.0 fusion.54
  490.6 2.9 collective-permute-done.77.p1
  497.4 2.7 placed_product.3
  500.1 4.2 all-to-all-start.9
  507.5 7.3 %all-to-all-done.9 = bf16[32,16,256]{2,1,0:T(8,128)(2,1)S(1)} async-done(((bf16[32,16,256]{2,1,0:T(8,128)(2,1)}), bf16[32,16,256]{2,1,0:T(8,128)(2,1)S(1)}, u32[]{:S(2)}, u32[]{:S(2)}) %all-to-all-start.9) | async-done | bytes 262176 | tf_op jit(solution)/shard_map/all_to_all | solution.py:1296
  519.0 4.5 collective-permute-done.81
  523.5 2.7 fusion.5
  (461 shorter events, 140.7 us)
Async XLA Ops:
  3.5 22.4 %collective-permute-start = (bf16[128,1920]{1,0:T(8,128)(2,1)S(1)}, bf16[128,1920]{1,0:T(8,128)(2,1)S(1)}, u32[]{:S(2)}, u32[]{:S(2)}) collective-permute-start(bf16[128,1920]{1,0:T(8,128)(2,1)S(1)} %concatenate.68.w0), channel_id=1, source_target_pairs={{0,8},{8,16},{16,24},{24,28},{28,20},{20,12},{12,4},{4,0},{1,9},{9... | collective-permute-start | bytes 1474568 | tf_op jit(solution)/shard_map/ppermute | solution.py:1218
  6.6 19.3 %collective-permute-start.1 = (bf16[128,1920]{1,0:T(8,128)(2,1)S(1)}, bf16[128,1920]{1,0:T(8,128)(2,1)S(1)}, u32[]{:S(2)}, u32[]{:S(2)}) collective-permute-start(bf16[128,1920]{1,0:T(8,128)(2,1)S(1)} %concatenate.68.w0), channel_id=1, source_target_pairs={{8,0},{16,8},{24,16},{28,24},{20,28},{12,20},{4,12},{0,4},{9,1},{1... | collective-permute-start | bytes 1474568 | tf_op jit(solution)/shard_map/ppermute | solution.py:1222
  9.0 16.9 %all-to-all-start = ((bf16[8,64,256]{2,1,0:T(8,128)(2,1)}), bf16[8,64,256]{2,1,0:T(8,128)(2,1)S(1)}, u32[]{:S(2)}, u32[]{:S(2)}) async-start(bf16[8,64,256]{2,1,0:T(8,128)(2,1)} %copy.111), calls=%async_computation | async-start | bytes 524288 | tf_op jit(solution)/shard_map/all_to_all | solution.py:1292
  31.1 19.9 %collective-permute-start.4 = (bf16[128,1920]{1,0:T(8,128)(2,1)S(1)}, bf16[128,1920]{1,0:T(8,128)(2,1)S(1)}, u32[]{:S(2)}, u32[]{:S(2)}) collective-permute-start(bf16[128,1920]{1,0:T(8,128)(2,1)S(1)} %copy-done.70), channel_id=1, source_target_pairs={{0,8},{8,16},{16,24},{24,28},{28,20},{20,12},{12,4},{4,0},{1,9},{9... | collective-permute-start | bytes 1474568 | tf_op jit(solution)/shard_map/ppermute | solution.py:1218
  31.3 20.6 %collective-permute-start.5 = (bf16[128,1920]{1,0:T(8,128)(2,1)}, bf16[128,1920]{1,0:T(8,128)(2,1)}, u32[]{:S(2)}, u32[]{:S(2)}) collective-permute-start(bf16[128,1920]{1,0:T(8,128)(2,1)} %copy-done.71), channel_id=1, source_target_pairs={{8,0},{16,8},{24,16},{28,24},{20,28},{12,20},{4,12},{0,4},{9,1},{1... | collective-permute-start | bytes 1474568 | tf_op jit(solution)/shard_map/ppermute | solution.py:1222
  38.7 12.3 %all-to-all-start.1 = ((bf16[8,16,1024]{2,1,0:T(8,128)(2,1)}), bf16[8,16,1024]{2,1,0:T(8,128)(2,1)S(1)}, u32[]{:S(2)}, u32[]{:S(2)}) async-start(bf16[8,16,1024]{2,1,0:T(8,128)(2,1)} %bitcast.13), calls=%async_computation.1 | async-start | bytes 524288 | tf_op jit(solution)/shard_map/all_to_all | solution.py:1292
  51.8 22.9 %collective-permute-start.6 = (bf16[128,1920]{1,0:T(8,128)(2,1)}, bf16[128,1920]{1,0:T(8,128)(2,1)S(1)}, u32[]{:S(2)}, u32[]{:S(2)}) collective-permute-start(bf16[128,1920]{1,0:T(8,128)(2,1)} %copy-done.72), channel_id=1, source_target_pairs={{0,8},{8,16},{16,24},{24,28},{28,20},{20,12},{12,4},{4,0},{1,9},{9... | collective-permute-start | bytes 1474568 | tf_op jit(solution)/shard_map/ppermute | solution.py:1218
  52.9 21.8 %collective-permute-start.7 = (bf16[128,1920]{1,0:T(8,128)(2,1)}, bf16[128,1920]{1,0:T(8,128)(2,1)S(1)}, u32[]{:S(2)}, u32[]{:S(2)}) collective-permute-start(bf16[128,1920]{1,0:T(8,128)(2,1)} %collective-permute-done.5.w4), channel_id=1, source_target_pairs={{8,0},{16,8},{24,16},{28,24},{20,28},{12,20},{4,12},{0,4},{9,1},{1... | collective-permute-start | bytes 1474568 | tf_op jit(solution)/shard_map/ppermute | solution.py:1222
  54.6 15.4 %all-to-all-start.2 = ((bf16[8,16,1024]{2,1,0:T(8,128)(2,1)}), bf16[8,16,1024]{2,1,0:T(8,128)(2,1)S(1)}, u32[]{:S(2)}, u32[]{:S(2)}) async-start(bf16[8,16,1024]{2,1,0:T(8,128)(2,1)} %broadcast_in_dim.40), calls=%async_computation.2 | async-start | bytes 524288 | tf_op jit(solution)/shard_map/all_to_all | solution.py:1292
  58.3 50.4 %collective-permute-start.13 = (bf16[128,1024]{1,0:T(8,128)(2,1)S(1)}, bf16[128,1024]{1,0:T(8,128)(2,1)S(1)}, u32[]{:S(2)}, u32[]{:S(2)}) collective-permute-start(bf16[128,1024]{1,0:T(8,128)(2,1)S(1)} %pad_maximum_fusion.7.w0), channel_id=1, source_target_pairs={{0,8},{8,16},{16,24},{24,28},{28,20},{20,12},{12,4},{4,0},{1,9},{9... | collective-permute-start | bytes 786440 | tf_op jit(solution)/shard_map/ppermute | solution.py:1218
  70.0 38.7 %all-to-all-start.3 = ((bf16[8,128,256]{2,1,0:T(8,128)(2,1)}), bf16[8,128,256]{2,1,0:T(8,128)(2,1)S(1)}, u32[]{:S(2)}, u32[]{:S(2)}) async-start(bf16[8,128,256]{2,1,0:T(8,128)(2,1)} %bitcast.254), calls=%async_computation.3 | async-start | bytes 1048576 | tf_op jit(solution)/shard_map/all_to_all | solution.py:1292
  78.4 12.2 %collective-permute-start.9 = (bf16[128,1024]{1,0:T(8,128)(2,1)S(1)}, bf16[128,1024]{1,0:T(8,128)(2,1)S(1)}, u32[]{:S(2)}, u32[]{:S(2)}) collective-permute-start(bf16[128,1024]{1,0:T(8,128)(2,1)S(1)} %fusion.13.p0), channel_id=1, source_target_pairs={{0,1},{1,0},{2,3},{3,2},{4,5},{5,4},{6,7},{7,6},{8,9},{9,8},{10,11... | collective-permute-start | bytes 786440 | tf_op jit(solution)/shard_map/ppermute | solution.py:1200
  78.5 9.6 %collective-permute-start.11 = (bf16[64,1920]{1,0:T(8,128)(2,1)S(1)}, bf16[64,1920]{1,0:T(8,128)(2,1)S(1)}, u32[]{:S(2)}, u32[]{:S(2)}) collective-permute-start(bf16[64,1920]{1,0:T(8,128)(2,1)S(1)} %slice.267), channel_id=1, source_target_pairs={{0,8},{8,16},{16,24},{24,28},{28,20},{20,12},{12,4},{4,0},{1,9},{9... | collective-permute-start | bytes 737288 | tf_op jit(solution)/shard_map/ppermute | solution.py:1218
  80.6 10.0 %collective-permute-start.12 = (bf16[64,1920]{1,0:T(8,128)(2,1)S(1)}, bf16[64,1920]{1,0:T(8,128)(2,1)S(1)}, u32[]{:S(2)}, u32[]{:S(2)}) collective-permute-start(bf16[64,1920]{1,0:T(8,128)(2,1)S(1)} %slice.268), channel_id=1, source_target_pairs={{8,0},{16,8},{24,16},{28,24},{20,28},{12,20},{4,12},{0,4},{9,1},{1... | collective-permute-start | bytes 737288 | tf_op jit(solution)/shard_map/ppermute | solution.py:1222
  81.5 9.1 %collective-permute-start.10 = (bf16[128,1024]{1,0:T(8,128)(2,1)S(1)}, bf16[128,1024]{1,0:T(8,128)(2,1)S(1)}, u32[]{:S(2)}, u32[]{:S(2)}) collective-permute-start(bf16[128,1024]{1,0:T(8,128)(2,1)S(1)} %collective-permute-done.8.p1), channel_id=1, source_target_pairs={{0,1},{1,0},{2,3},{3,2},{4,5},{5,4},{6,7},{7,6},{8,9},{9,8},{10,11... | collective-permute-start | bytes 786440 | tf_op jit(solution)/shard_map/ppermute | solution.py:1200
  88.1 20.6 %collective-permute-start.14 = (bf16[128,1024]{1,0:T(8,128)(2,1)S(1)}, bf16[128,1024]{1,0:T(8,128)(2,1)}, u32[]{:S(2)}, u32[]{:S(2)}) collective-permute-start(bf16[128,1024]{1,0:T(8,128)(2,1)S(1)} %pad_maximum_fusion.7.w0), channel_id=1, source_target_pairs={{8,0},{16,8},{24,16},{28,24},{20,28},{12,20},{4,12},{0,4},{9,1},{1... | collective-permute-start | bytes 786440 | tf_op jit(solution)/shard_map/ppermute | solution.py:1222
  108.9 20.6 %collective-permute-start.17 = (bf16[128,3072]{1,0:T(8,128)(2,1)S(1)}, bf16[128,3072]{1,0:T(8,128)(2,1)}, u32[]{:S(2)}, u32[]{:S(2)}) collective-permute-start(bf16[128,3072]{1,0:T(8,128)(2,1)S(1)} %constant_dynamic-update-slice_fusion.w0), channel_id=1, source_target_pairs={{0,8},{8,16},{16,24},{24,28},{28,20},{20,12},{12,4},{4,0},{1,9},{9... | collective-permute-start | bytes 2359304 | tf_op jit(solution)/shard_map/ppermute | solution.py:1218
  109.2 20.5 %collective-permute-start.18 = (bf16[128,3072]{1,0:T(8,128)(2,1)S(1)}, bf16[128,3072]{1,0:T(8,128)(2,1)}, u32[]{:S(2)}, u32[]{:S(2)}) collective-permute-start(bf16[128,3072]{1,0:T(8,128)(2,1)S(1)} %constant_dynamic-update-slice_fusion.w0), channel_id=1, source_target_pairs={{8,0},{16,8},{24,16},{28,24},{20,28},{12,20},{4,12},{0,4},{9,1},{1... | collective-permute-start | bytes 2359304 | tf_op jit(solution)/shard_map/ppermute | solution.py:1222
  111.2 9.3 %collective-permute-start.16 = (bf16[128,1152]{1,0:T(8,128)(2,1)S(1)}, bf16[128,1152]{1,0:T(8,128)(2,1)S(1)}, u32[]{:S(2)}, u32[]{:S(2)}) collective-permute-start(bf16[128,1152]{1,0:T(8,128)(2,1)S(1)} %fusion.40), channel_id=1, source_target_pairs={{0,2},{1,3},{2,0},{3,1},{4,6},{5,7},{6,4},{7,5},{8,10},{9,11},{10,... | collective-permute-start | bytes 884744 | tf_op jit(solution)/shard_map/ppermute | solution.py:1204
  113.1 21.6 %collective-permute-start.19 = (bf16[128,1024]{1,0:T(8,128)(2,1)S(1)}, bf16[128,1024]{1,0:T(8,128)(2,1)S(1)}, u32[]{:S(2)}, u32[]{:S(2)}) collective-permute-start(bf16[128,1024]{1,0:T(8,128)(2,1)S(1)} %collective-permute-done.13.w1), channel_id=1, source_target_pairs={{0,8},{8,16},{16,24},{24,28},{28,20},{20,12},{12,4},{4,0},{1,9},{9... | collective-permute-start | bytes 786440 | tf_op jit(solution)/shard_map/ppermute | solution.py:1218
  113.6 21.1 %collective-permute-start.20 = (bf16[128,1024]{1,0:T(8,128)(2,1)}, bf16[128,1024]{1,0:T(8,128)(2,1)S(1)}, u32[]{:S(2)}, u32[]{:S(2)}) collective-permute-start(bf16[128,1024]{1,0:T(8,128)(2,1)} %collective-permute-done.14.w2), channel_id=1, source_target_pairs={{8,0},{16,8},{24,16},{28,24},{20,28},{12,20},{4,12},{0,4},{9,1},{1... | collective-permute-start | bytes 786440 | tf_op jit(solution)/shard_map/ppermute | solution.py:1222
  137.0 20.5 %collective-permute-start.24 = (bf16[128,1024]{1,0:T(8,128)(2,1)S(1)}, bf16[128,1024]{1,0:T(8,128)(2,1)S(1)}, u32[]{:S(2)}, u32[]{:S(2)}) collective-permute-start(bf16[128,1024]{1,0:T(8,128)(2,1)S(1)} %collective-permute-done.19.w3), channel_id=1, source_target_pairs={{0,8},{8,16},{16,24},{24,28},{28,20},{20,12},{12,4},{4,0},{1,9},{9... | collective-permute-start | bytes 786440 | tf_op jit(solution)/shard_map/ppermute | solution.py:1218
  138.7 18.8 %collective-permute-start.25 = (bf16[128,1024]{1,0:T(8,128)(2,1)S(1)}, bf16[128,1024]{1,0:T(8,128)(2,1)S(1)}, u32[]{:S(2)}, u32[]{:S(2)}) collective-permute-start(bf16[128,1024]{1,0:T(8,128)(2,1)S(1)} %collective-permute-done.20.w4), channel_id=1, source_target_pairs={{8,0},{16,8},{24,16},{28,24},{20,28},{12,20},{4,12},{0,4},{9,1},{1... | collective-permute-start | bytes 786440 | tf_op jit(solution)/shard_map/ppermute | solution.py:1222
  143.3 14.2 %collective-permute-start.23 = (bf16[128,1024]{1,0:T(8,128)(2,1)S(1)}, bf16[128,1024]{1,0:T(8,128)(2,1)S(1)}, u32[]{:S(2)}, u32[]{:S(2)}) collective-permute-start(bf16[128,1024]{1,0:T(8,128)(2,1)S(1)} %collective-permute-done.21.p1), channel_id=1, source_target_pairs={{0,1},{1,0},{2,3},{3,2},{4,5},{5,4},{6,7},{7,6},{8,9},{9,8},{10,11... | collective-permute-start | bytes 786440 | tf_op jit(solution)/shard_map/ppermute | solution.py:1200
  143.3 41.0 %collective-permute-start.26 = (bf16[128,3072]{1,0:T(8,128)(2,1)}, bf16[128,3072]{1,0:T(8,128)(2,1)}, u32[]{:S(2)}, u32[]{:S(2)}) collective-permute-start(bf16[128,3072]{1,0:T(8,128)(2,1)} %collective-permute-done.17.w1), channel_id=1, source_target_pairs={{0,8},{8,16},{16,24},{24,28},{28,20},{20,12},{12,4},{4,0},{1,9},{9... | collective-permute-start | bytes 2359304 | tf_op jit(solution)/shard_map/ppermute | solution.py:1218
  144.8 39.6 %collective-permute-start.27 = (bf16[128,3072]{1,0:T(8,128)(2,1)}, bf16[128,3072]{1,0:T(8,128)(2,1)}, u32[]{:S(2)}, u32[]{:S(2)}) collective-permute-start(bf16[128,3072]{1,0:T(8,128)(2,1)} %collective-permute-done.18.w2), channel_id=1, source_target_pairs={{8,0},{16,8},{24,16},{28,24},{20,28},{12,20},{4,12},{0,4},{9,1},{1... | collective-permute-start | bytes 2359304 | tf_op jit(solution)/shard_map/ppermute | solution.py:1222
  161.0 23.0 %all-to-all-start.4 = ((bf16[32,16,256]{2,1,0:T(8,128)(2,1)}), bf16[32,16,256]{2,1,0:T(8,128)(2,1)S(1)}, u32[]{:S(2)}, u32[]{:S(2)}) async-start(bf16[32,16,256]{2,1,0:T(8,128)(2,1)} %bitcast.295), calls=%async_computation.4 | async-start | bytes 524288 | tf_op jit(solution)/shard_map/all_to_all | solution.py:1296
  165.0 19.4 %collective-permute-start.28 = (bf16[64,1024]{1,0:T(8,128)(2,1)S(1)}, bf16[64,1024]{1,0:T(8,128)(2,1)}, u32[]{:S(2)}, u32[]{:S(2)}) collective-permute-start(bf16[64,1024]{1,0:T(8,128)(2,1)S(1)} %slice.271), channel_id=1, source_target_pairs={{0,8},{8,16},{16,24},{24,28},{28,20},{20,12},{12,4},{4,0},{1,9},{9... | collective-permute-start | bytes 393224 | tf_op jit(solution)/shard_map/ppermute | solution.py:1218
  166.8 17.5 %collective-permute-start.29 = (bf16[64,1024]{1,0:T(8,128)(2,1)S(1)}, bf16[64,1024]{1,0:T(8,128)(2,1)}, u32[]{:S(2)}, u32[]{:S(2)}) collective-permute-start(bf16[64,1024]{1,0:T(8,128)(2,1)S(1)} %slice.272), channel_id=1, source_target_pairs={{8,0},{16,8},{24,16},{28,24},{20,28},{12,20},{4,12},{0,4},{9,1},{1... | collective-permute-start | bytes 393224 | tf_op jit(solution)/shard_map/ppermute | solution.py:1222
  192.9 20.2 %collective-permute-start.33 = (bf16[128,3072]{1,0:T(8,128)(2,1)}, bf16[128,3072]{1,0:T(8,128)(2,1)S(1)}, u32[]{:S(2)}, u32[]{:S(2)}) collective-permute-start(bf16[128,3072]{1,0:T(8,128)(2,1)} %collective-permute-done.26.w3), channel_id=1, source_target_pairs={{0,8},{8,16},{16,24},{24,28},{28,20},{20,12},{12,4},{4,0},{1,9},{9... | collective-permute-start | bytes 2359304 | tf_op jit(solution)/shard_map/ppermute | solution.py:1218
  194.8 19.9 %collective-permute-start.34 = (bf16[128,3072]{1,0:T(8,128)(2,1)}, bf16[128,3072]{1,0:T(8,128)(2,1)S(1)}, u32[]{:S(2)}, u32[]{:S(2)}) collective-permute-start(bf16[128,3072]{1,0:T(8,128)(2,1)} %collective-permute-done.27.w4), channel_id=1, source_target_pairs={{8,0},{16,8},{24,16},{28,24},{20,28},{12,20},{4,12},{0,4},{9,1},{1... | collective-permute-start | bytes 2359304 | tf_op jit(solution)/shard_map/ppermute | solution.py:1222
  230.0 10.4 %collective-permute-start.40 = (bf16[64,3072]{1,0:T(8,128)(2,1)}, bf16[64,3072]{1,0:T(8,128)(2,1)}, u32[]{:S(2)}, u32[]{:S(2)}) collective-permute-start(bf16[64,3072]{1,0:T(8,128)(2,1)} %slice.275), channel_id=1, source_target_pairs={{0,8},{8,16},{16,24},{24,28},{28,20},{20,12},{12,4},{4,0},{1,9},{9... | collective-permute-start | bytes 1179656 | tf_op jit(solution)/shard_map/ppermute | solution.py:1218
  231.2 10.1 %collective-permute-start.41 = (bf16[64,3072]{1,0:T(8,128)(2,1)}, bf16[64,3072]{1,0:T(8,128)(2,1)}, u32[]{:S(2)}, u32[]{:S(2)}) collective-permute-start(bf16[64,3072]{1,0:T(8,128)(2,1)} %slice.276), channel_id=1, source_target_pairs={{8,0},{16,8},{24,16},{28,24},{20,28},{12,20},{4,12},{0,4},{9,1},{1... | collective-permute-start | bytes 1179656 | tf_op jit(solution)/shard_map/ppermute | solution.py:1222
  273.4 66.8 %collective-permute-start.53 = (bf16[2,128,1024]{2,1,0:T(8,128)(2,1)}, bf16[2,128,1024]{2,1,0:T(8,128)(2,1)}, u32[]{:S(2)}, u32[]{:S(2)}) collective-permute-start(bf16[2,128,1024]{2,1,0:T(8,128)(2,1)} %get-tuple-element.225), channel_id=1, source_target_pairs={{0,1},{1,0},{2,3},{3,2},{4,5},{5,4},{6,7},{7,6},{8,9},{9,8},{10,11... | collective-permute-start | bytes 1572872 | tf_op jit(solution)/shard_map/ppermute | solution.py:1200
  273.4 16.0 %collective-permute-start.44 = (bf16[128,1024]{1,0:T(8,128)(2,1)S(1)}, bf16[128,1024]{1,0:T(8,128)(2,1)S(1)}, u32[]{:S(2)}, u32[]{:S(2)}) collective-permute-start(bf16[128,1024]{1,0:T(8,128)(2,1)S(1)} %get-tuple-element.208.g0), channel_id=1, source_target_pairs={{0,1},{1,0},{2,3},{3,2},{4,5},{5,4},{6,7},{7,6},{8,9},{9,8},{10,11... | collective-permute-start | bytes 786440 | tf_op jit(solution)/shard_map/ppermute | solution.py:1200
  279.9 9.5 %collective-permute-start.46 = (bf16[128,1024]{1,0:T(8,128)(2,1)S(1)}, bf16[128,1024]{1,0:T(8,128)(2,1)S(1)}, u32[]{:S(2)}, u32[]{:S(2)}) collective-permute-start(bf16[128,1024]{1,0:T(8,128)(2,1)S(1)} %collective-permute-done.45.g2), channel_id=1, source_target_pairs={{0,1},{1,0},{2,3},{3,2},{4,5},{5,4},{6,7},{7,6},{8,9},{9,8},{10,11... | collective-permute-start | bytes 786440 | tf_op jit(solution)/shard_map/ppermute | solution.py:1200
  291.0 15.5 %collective-permute-start.47 = (bf16[64,3072]{1,0:T(8,128)(2,1)S(1)}, bf16[64,3072]{1,0:T(8,128)(2,1)S(1)}, u32[]{:S(2)}, u32[]{:S(2)}) collective-permute-start(bf16[64,3072]{1,0:T(8,128)(2,1)S(1)} %get-tuple-element.444), channel_id=1, source_target_pairs={{0,8},{8,16},{16,24},{24,28},{28,20},{20,12},{12,4},{4,0},{1,9},{9... | collective-permute-start | bytes 1179656 | tf_op jit(solution)/shard_map/ppermute | solution.py:1218
  291.8 14.8 %collective-permute-start.48 = (bf16[64,3072]{1,0:T(8,128)(2,1)S(1)}, bf16[64,3072]{1,0:T(8,128)(2,1)S(1)}, u32[]{:S(2)}, u32[]{:S(2)}) collective-permute-start(bf16[64,3072]{1,0:T(8,128)(2,1)S(1)} %get-tuple-element.443), channel_id=1, source_target_pairs={{8,0},{16,8},{24,16},{28,24},{20,28},{12,20},{4,12},{0,4},{9,1},{1... | collective-permute-start | bytes 1179656 | tf_op jit(solution)/shard_map/ppermute | solution.py:1222
  308.1 20.0 %collective-permute-start.52 = (bf16[128,3072]{1,0:T(8,128)(2,1)S(1)}, bf16[128,3072]{1,0:T(8,128)(2,1)S(1)}, u32[]{:S(2)}, u32[]{:S(2)}) collective-permute-start(bf16[128,3072]{1,0:T(8,128)(2,1)S(1)} %pad_maximum_fusion.6), channel_id=1, source_target_pairs={{8,0},{16,8},{24,16},{28,24},{20,28},{12,20},{4,12},{0,4},{9,1},{1... | collective-permute-start | bytes 2359304 | tf_op jit(solution)/shard_map/ppermute | solution.py:1222
  309.9 20.1 %collective-permute-start.51 = (bf16[128,3072]{1,0:T(8,128)(2,1)S(1)}, bf16[128,3072]{1,0:T(8,128)(2,1)S(1)}, u32[]{:S(2)}, u32[]{:S(2)}) collective-permute-start(bf16[128,3072]{1,0:T(8,128)(2,1)S(1)} %pad_maximum_fusion.5), channel_id=1, source_target_pairs={{0,8},{8,16},{16,24},{24,28},{28,20},{20,12},{12,4},{4,0},{1,9},{9... | collective-permute-start | bytes 2359304 | tf_op jit(solution)/shard_map/ppermute | solution.py:1218
  333.1 24.9 %collective-permute-start.54 = (bf16[128,3072]{1,0:T(8,128)(2,1)}, bf16[128,3072]{1,0:T(8,128)(2,1)}, u32[]{:S(2)}, u32[]{:S(2)}) collective-permute-start(bf16[128,3072]{1,0:T(8,128)(2,1)} %get-tuple-element.440), channel_id=1, source_target_pairs={{0,8},{8,16},{16,24},{24,28},{28,20},{20,12},{12,4},{4,0},{1,9},{9... | collective-permute-start | bytes 2359304 | tf_op jit(solution)/shard_map/ppermute | solution.py:1218
  333.4 24.5 %collective-permute-start.55 = (bf16[128,3072]{1,0:T(8,128)(2,1)}, bf16[128,3072]{1,0:T(8,128)(2,1)}, u32[]{:S(2)}, u32[]{:S(2)}) collective-permute-start(bf16[128,3072]{1,0:T(8,128)(2,1)} %get-tuple-element.439), channel_id=1, source_target_pairs={{8,0},{16,8},{24,16},{28,24},{20,28},{12,20},{4,12},{0,4},{9,1},{1... | collective-permute-start | bytes 2359304 | tf_op jit(solution)/shard_map/ppermute | solution.py:1222
  337.4 20.6 %all-to-all-start.5 = ((bf16[32,16,256]{2,1,0:T(8,128)(2,1)}), bf16[32,16,256]{2,1,0:T(8,128)(2,1)S(1)}, u32[]{:S(2)}, u32[]{:S(2)}) async-start(bf16[32,16,256]{2,1,0:T(8,128)(2,1)} %bitcast.47), calls=%async_computation.5 | async-start | bytes 524288 | tf_op jit(solution)/shard_map/all_to_all | solution.py:1296
  362.8 8.8 %collective-permute-start.57 = (bf16[128,1024]{1,0:T(8,128)(2,1)S(1)}, bf16[128,1024]{1,0:T(8,128)(2,1)S(1)}, u32[]{:S(2)}, u32[]{:S(2)}) collective-permute-start(bf16[128,1024]{1,0:T(8,128)(2,1)S(1)} %fusion.45), channel_id=1, source_target_pairs={{0,2},{1,3},{2,0},{3,1},{4,6},{5,7},{6,4},{7,5},{8,10},{9,11},{10,... | collective-permute-start | bytes 786440 | tf_op jit(solution)/shard_map/ppermute | solution.py:1204
  367.6 28.6 %collective-permute-start.59 = (bf16[128,3072]{1,0:T(8,128)(2,1)}, bf16[128,3072]{1,0:T(8,128)(2,1)}, u32[]{:S(2)}, u32[]{:S(2)}) collective-permute-start(bf16[128,3072]{1,0:T(8,128)(2,1)} %get-tuple-element.438), channel_id=1, source_target_pairs={{0,8},{8,16},{16,24},{24,28},{28,20},{20,12},{12,4},{4,0},{1,9},{9... | collective-permute-start | bytes 2359304 | tf_op jit(solution)/shard_map/ppermute | solution.py:1218
  368.3 27.9 %collective-permute-start.60 = (bf16[128,3072]{1,0:T(8,128)(2,1)}, bf16[128,3072]{1,0:T(8,128)(2,1)}, u32[]{:S(2)}, u32[]{:S(2)}) collective-permute-start(bf16[128,3072]{1,0:T(8,128)(2,1)} %get-tuple-element.437), channel_id=1, source_target_pairs={{8,0},{16,8},{24,16},{28,24},{20,28},{12,20},{4,12},{0,4},{9,1},{1... | collective-permute-start | bytes 2359304 | tf_op jit(solution)/shard_map/ppermute | solution.py:1222
  372.3 22.7 %all-to-all-start.6 = ((bf16[8,16,1024]{2,1,0:T(8,128)(2,1)}), bf16[8,16,1024]{2,1,0:T(8,128)(2,1)S(1)}, u32[]{:S(2)}, u32[]{:S(2)}) async-start(bf16[8,16,1024]{2,1,0:T(8,128)(2,1)} %bitcast.59), calls=%async_computation.6 | async-start | bytes 524288 | tf_op jit(solution)/shard_map/all_to_all | solution.py:1292
  378.2 39.3 %collective-permute-start.63 = (bf16[64,1024]{1,0:T(8,128)(2,1)}, bf16[64,1024]{1,0:T(8,128)(2,1)}, u32[]{:S(2)}, u32[]{:S(2)}) collective-permute-start(bf16[64,1024]{1,0:T(8,128)(2,1)} %get-tuple-element.454), channel_id=1, source_target_pairs={{0,8},{8,16},{16,24},{24,28},{28,20},{20,12},{12,4},{4,0},{1,9},{9... | collective-permute-start | bytes 393224 | tf_op jit(solution)/shard_map/ppermute | solution.py:1218
  380.2 37.3 %collective-permute-start.64 = (bf16[64,1024]{1,0:T(8,128)(2,1)}, bf16[64,1024]{1,0:T(8,128)(2,1)}, u32[]{:S(2)}, u32[]{:S(2)}) collective-permute-start(bf16[64,1024]{1,0:T(8,128)(2,1)} %get-tuple-element.453), channel_id=1, source_target_pairs={{8,0},{16,8},{24,16},{28,24},{20,28},{12,20},{4,12},{0,4},{9,1},{1... | collective-permute-start | bytes 393224 | tf_op jit(solution)/shard_map/ppermute | solution.py:1222
  380.2 14.9 %collective-permute-start.58 = (bf16[128,1024]{1,0:T(8,128)(2,1)S(1)}, bf16[128,1024]{1,0:T(8,128)(2,1)S(1)}, u32[]{:S(2)}, u32[]{:S(2)}) collective-permute-start(bf16[128,1024]{1,0:T(8,128)(2,1)S(1)} %copy-done.32), channel_id=1, source_target_pairs={{0,2},{1,3},{2,0},{3,1},{4,6},{5,7},{6,4},{7,5},{8,10},{9,11},{10,... | collective-permute-start | bytes 786440 | tf_op jit(solution)/shard_map/ppermute | solution.py:1204
  395.2 22.3 %collective-permute-start.61 = (bf16[128,1024]{1,0:T(8,128)(2,1)S(1)}, bf16[128,1024]{1,0:T(8,128)(2,1)S(1)}, u32[]{:S(2)}, u32[]{:S(2)}) collective-permute-start(bf16[128,1024]{1,0:T(8,128)(2,1)S(1)} %fusion.25), channel_id=1, source_target_pairs={{0,2},{1,3},{2,0},{3,1},{4,6},{5,7},{6,4},{7,5},{8,10},{9,11},{10,... | collective-permute-start | bytes 786440 | tf_op jit(solution)/shard_map/ppermute | solution.py:1204
  396.2 21.2 %collective-permute-start.62 = (bf16[128,1024]{1,0:T(8,128)(2,1)S(1)}, bf16[128,1024]{1,0:T(8,128)(2,1)}, u32[]{:S(2)}, u32[]{:S(2)}) collective-permute-start(bf16[128,1024]{1,0:T(8,128)(2,1)S(1)} %fusion.25), channel_id=1, source_target_pairs={{0,1},{1,0},{2,3},{3,2},{4,5},{5,4},{6,7},{7,6},{8,9},{9,8},{10,11... | collective-permute-start | bytes 786440 | tf_op jit(solution)/shard_map/ppermute | solution.py:1200
  397.1 16.7 %all-to-all-start.7 = ((bf16[8,24,1024]{2,1,0:T(8,128)(2,1)}), bf16[8,24,1024]{2,1,0:T(8,128)(2,1)}, u32[]{:S(2)}, u32[]{:S(2)}) async-start(bf16[8,24,1024]{2,1,0:T(8,128)(2,1)} %broadcast_in_dim.81), calls=%async_computation.7 | async-start | bytes 786432 | tf_op jit(solution)/shard_map/all_to_all | solution.py:1292
  413.8 53.3 %all-to-all-start.8 = ((bf16[8,128,256]{2,1,0:T(8,128)(2,1)}), bf16[8,128,256]{2,1,0:T(8,128)(2,1)S(1)}, u32[]{:S(2)}, u32[]{:S(2)}) async-start(bf16[8,128,256]{2,1,0:T(8,128)(2,1)} %bitcast.292), calls=%async_computation.8 | async-start | bytes 1048576 | tf_op jit(solution)/shard_map/all_to_all | solution.py:1292
  420.1 9.2 %collective-permute-start.65 = (bf16[136,1152]{1,0:T(8,128)(2,1)S(1)}, bf16[136,1152]{1,0:T(8,128)(2,1)S(1)}, u32[]{:S(2)}, u32[]{:S(2)}) collective-permute-start(bf16[136,1152]{1,0:T(8,128)(2,1)S(1)} %fusion.39.g0), channel_id=1, source_target_pairs={{0,2},{1,3},{2,0},{3,1},{4,6},{5,7},{6,4},{7,5},{8,10},{9,11},{10,... | collective-permute-start | bytes 940040 | tf_op jit(solution)/shard_map/ppermute | solution.py:1204
  421.2 16.9 %collective-permute-start.66 = (bf16[136,1152]{1,0:T(8,128)(2,1)S(1)}, bf16[136,1152]{1,0:T(8,128)(2,1)S(1)}, u32[]{:S(2)}, u32[]{:S(2)}) collective-permute-start(bf16[136,1152]{1,0:T(8,128)(2,1)S(1)} %fusion.39.g0), channel_id=1, source_target_pairs={{0,1},{1,0},{2,3},{3,2},{4,5},{5,4},{6,7},{7,6},{8,9},{9,8},{10,11... | collective-permute-start | bytes 940040 | tf_op jit(solution)/shard_map/ppermute | solution.py:1200
  422.4 12.2 %collective-permute-start.69 = (bf16[128,1024]{1,0:T(8,128)(2,1)S(1)}, bf16[128,1024]{1,0:T(8,128)(2,1)S(1)}, u32[]{:S(2)}, u32[]{:S(2)}) collective-permute-start(bf16[128,1024]{1,0:T(8,128)(2,1)S(1)} %pad_maximum_fusion.9), channel_id=1, source_target_pairs={{8,0},{16,8},{24,16},{28,24},{20,28},{12,20},{4,12},{0,4},{9,1},{1... | collective-permute-start | bytes 786440 | tf_op jit(solution)/shard_map/ppermute | solution.py:1222
  429.2 8.8 %collective-permute-start.67 = (bf16[136,1152]{1,0:T(8,128)(2,1)S(1)}, bf16[136,1152]{1,0:T(8,128)(2,1)S(1)}, u32[]{:S(2)}, u32[]{:S(2)}) collective-permute-start(bf16[136,1152]{1,0:T(8,128)(2,1)S(1)} %collective-permute-done.65.g1), channel_id=1, source_target_pairs={{0,1},{1,0},{2,3},{3,2},{4,5},{5,4},{6,7},{7,6},{8,9},{9,8},{10,11... | collective-permute-start | bytes 940040 | tf_op jit(solution)/shard_map/ppermute | solution.py:1200
  432.2 34.9 %collective-permute-start.70 = (bf16[128,1024]{1,0:T(8,128)(2,1)S(1)}, bf16[128,1024]{1,0:T(8,128)(2,1)S(1)}, u32[]{:S(2)}, u32[]{:S(2)}) collective-permute-start(bf16[128,1024]{1,0:T(8,128)(2,1)S(1)} %copy-done.38), channel_id=1, source_target_pairs={{0,1},{1,0},{2,3},{3,2},{4,5},{5,4},{6,7},{7,6},{8,9},{9,8},{10,11... | collective-permute-start | bytes 786440 | tf_op jit(solution)/shard_map/ppermute | solution.py:1200
  439.5 27.7 %collective-permute-start.71 = (bf16[128,1024]{1,0:T(8,128)(2,1)S(1)}, bf16[128,1024]{1,0:T(8,128)(2,1)S(1)}, u32[]{:S(2)}, u32[]{:S(2)}) collective-permute-start(bf16[128,1024]{1,0:T(8,128)(2,1)S(1)} %get-tuple-element.450), channel_id=1, source_target_pairs={{0,8},{8,16},{16,24},{24,28},{28,20},{20,12},{12,4},{4,0},{1,9},{9... | collective-permute-start | bytes 786440 | tf_op jit(solution)/shard_map/ppermute | solution.py:1218
  441.3 25.9 %collective-permute-start.72 = (bf16[128,1024]{1,0:T(8,128)(2,1)S(1)}, bf16[128,1024]{1,0:T(8,128)(2,1)S(1)}, u32[]{:S(2)}, u32[]{:S(2)}) collective-permute-start(bf16[128,1024]{1,0:T(8,128)(2,1)S(1)} %get-tuple-element.449), channel_id=1, source_target_pairs={{8,0},{16,8},{24,16},{28,24},{20,28},{12,20},{4,12},{0,4},{9,1},{1... | collective-permute-start | bytes 786440 | tf_op jit(solution)/shard_map/ppermute | solution.py:1222
  470.8 10.2 %collective-permute-start.74 = (bf16[128,1280]{1,0:T(8,128)(2,1)S(1)}, bf16[128,1280]{1,0:T(8,128)(2,1)S(1)}, u32[]{:S(2)}, u32[]{:S(2)}) collective-permute-start(bf16[128,1280]{1,0:T(8,128)(2,1)S(1)} %fusion.38), channel_id=1, source_target_pairs={{0,2},{1,3},{2,0},{3,1},{4,6},{5,7},{6,4},{7,5},{8,10},{9,11},{10,... | collective-permute-start | bytes 983048 | tf_op jit(solution)/shard_map/ppermute | solution.py:1204
  484.4 9.2 %collective-permute-start.77 = (bf16[136,1280]{1,0:T(8,128)(2,1)S(1)}, bf16[136,1280]{1,0:T(8,128)(2,1)S(1)}, u32[]{:S(2)}, u32[]{:S(2)}) collective-permute-start(bf16[136,1280]{1,0:T(8,128)(2,1)S(1)} %fusion.37.p0), channel_id=1, source_target_pairs={{0,2},{1,3},{2,0},{3,1},{4,6},{5,7},{6,4},{7,5},{8,10},{9,11},{10,... | collective-permute-start | bytes 1044488 | tf_op jit(solution)/shard_map/ppermute | solution.py:1204
  500.1 14.8 %all-to-all-start.9 = ((bf16[32,16,256]{2,1,0:T(8,128)(2,1)}), bf16[32,16,256]{2,1,0:T(8,128)(2,1)S(1)}, u32[]{:S(2)}, u32[]{:S(2)}) async-start(bf16[32,16,256]{2,1,0:T(8,128)(2,1)} %bitcast.296), calls=%async_computation.9 | async-start | bytes 524288 | tf_op jit(solution)/shard_map/all_to_all | solution.py:1296
  (121 other events, 1245.5 us)
